TPU v7x, 32 devices: a whole 2x2x4 slice. The times are simulated.
32 devices in a mesh: groups: 2 (over y), pool: 4 (over z), tp: 2 (over x), sub: 2 (over core).
Axes of the slice: x: 2, y: 2, z: 4, core: 2. Of those that a mesh axis runs over, the one named last changes fastest.
Arguments:
- hidden: bfloat16 [128, 3, 8192], P('groups', None, 'pool'), parts along dimension 0, may hold values from -6 to 6
- query_weight: bfloat16 [8192, 8192], P('pool', ('tp', 'sub')), may hold values from -0.0625 to 0.0625
- key_weight: bfloat16 [8192, 1024], P('pool', ('tp', 'sub')), may hold values from -0.0625 to 0.0625
- value_weight: bfloat16 [8192, 1024], P('pool', ('tp', 'sub')), may hold values from -0.0625 to 0.0625
- key_cache_rows: bfloat16 [128, 8, 256, 128], P(('groups', 'pool'), ('tp', 'sub')), parts along dimension 0, may hold values from -6 to 6
- value_cache_rows: bfloat16 [128, 8, 256, 128], P(('groups', 'pool'), ('tp', 'sub')), parts along dimension 0, may hold values from -6 to 6
- adapter_down_weight: bfloat16 [16, 128, 8192], P(('groups', 'pool'), None, ('tp', 'sub')), parts along dimension 0, may hold values from -0.0625 to 0.0625
- adapter_up_query: bfloat16 [16, 64, 8192], P(('groups', 'pool'), None, ('tp', 'sub')), parts along dimension 0, may hold values from -0.75 to 0.75
- adapter_up_value: bfloat16 [16, 64, 1024], P(('groups', 'pool'), None, ('tp', 'sub')), parts along dimension 0, may hold values from -0.75 to 0.75
- request_adapter: int32 [128], P('groups'), parts along dimension 0, may hold values from 0 to 7, as said below
- row_request: int32 [128], P('groups'), parts along dimension 0, may hold values from 0 to 63, as said below
- lengths: int32 [128], P('groups'), parts along dimension 0, may hold values from 1 to 256, as said below
Outputs:
- attended: bfloat16 [128, 3, 8192], P(('groups', 'pool'), None, ('tp', 'sub')), parts along dimension 0
There are 2 independent parts, one for each index of `groups`. A program takes and returns all parts, laid end to end along the dimension named above; an argument that names none is the same for every part. Nothing has to cross between parts.
Inputs may be any that keep to these rules, and one draw needn't show every extreme that they name: `request_adapter`: with owner = adapter // 2: among the rows of one device (batch rows b with equal b // 16, row b holding request row_request[b]) at most 8 use adapters of one owner, and in every draw some owner is used by exactly 8 rows of every device. `row_request`: A permutation: each request sits in exactly one batch row. `lengths`: some request holds all 256 positions.
All inputs are finite; a program needn't handle non-finite values.
Results may differ from a plain program's by a relative error of at most 0.03.
Values may be sent and summed in bfloat16 or wider, within the bound.
No kernel may reach another device: no remote copies, remote signals or barrier semaphores. Data moves between devices by JAX's collectives and lax.ppermute only.
A program may use at most 128 MiB of HBM per device.

v0:
```python
import math

import jax
import jax.numpy as jnp
from jax import lax
from jax.sharding import PartitionSpec as P

ROPE_BASE = 500000.0


def rotate(values, positions):
    head_dim = values.shape[-1]
    half_dim = head_dim // 2
    inverse_freq = ROPE_BASE ** (-2.0 * jnp.arange(half_dim, dtype=jnp.float32) / head_dim)
    angles = positions.astype(jnp.float32)[:, :, None, None] * inverse_freq
    cosine = jnp.cos(angles)
    sine_part = jnp.sin(angles)
    first = values[..., :half_dim]
    second = values[..., half_dim:]
    return jnp.concatenate(
        [first * cosine - second * sine_part, second * cosine + first * sine_part], -1
    )


def attend(queries, keys_new, values_new, key_cache_rows, value_cache_rows, row_length):
    rows, steps, heads, head_dim = queries.shape
    kv_heads = key_cache_rows.shape[1]
    group_size = heads // kv_heads
    grouped = queries.reshape(rows, steps, kv_heads, group_size, head_dim).transpose(0, 2, 1, 3, 4)
    grouped = grouped.reshape(rows, kv_heads, steps * group_size, head_dim)
    scale_factor = 1.0 / math.sqrt(head_dim)
    scores_cache = (
        jnp.einsum("rkqh,rkth->rkqt", grouped, key_cache_rows, preferred_element_type=jnp.float32)
        * scale_factor
    )
    new_keys = keys_new.transpose(0, 2, 1, 3)
    new_values = values_new.transpose(0, 2, 1, 3)
    scores_new = (
        jnp.einsum("rkqh,rksh->rkqs", grouped, new_keys, preferred_element_type=jnp.float32)
        * scale_factor
    )
    live_cache = jnp.arange(key_cache_rows.shape[2], dtype=jnp.int32)[None, :] < row_length[:, None]
    query_step = jnp.arange(steps * group_size, dtype=jnp.int32) // group_size
    live_new = jnp.arange(steps, dtype=jnp.int32)[None, :] <= query_step[:, None]
    weights_cache = jnp.where(live_cache[:, None, None, :], jnp.exp(scores_cache), 0.0)
    weights_new = jnp.where(live_new[None, None], jnp.exp(scores_new), 0.0)
    denominator = jnp.sum(weights_cache, -1) + jnp.sum(weights_new, -1)
    probs_cache = (weights_cache / denominator[..., None]).astype(jnp.bfloat16)
    probs_new = (weights_new / denominator[..., None]).astype(jnp.bfloat16)
    mixed = jnp.einsum(
        "rkqt,rkth->rkqh", probs_cache, value_cache_rows, preferred_element_type=jnp.float32
    )
    mixed = mixed + jnp.einsum(
        "rkqs,rksh->rkqh", probs_new, new_values, preferred_element_type=jnp.float32
    )
    mixed = mixed.reshape(rows, kv_heads, steps, group_size, head_dim).transpose(0, 2, 1, 3, 4)
    return mixed.reshape(rows, steps, heads * head_dim).astype(jnp.bfloat16)


def on_device(
    hidden,
    query_weight,
    key_weight,
    value_weight,
    key_cache_rows,
    value_cache_rows,
    adapter_down_weight,
    adapter_up_query,
    adapter_up_value,
    request_adapter,
    row_request,
    lengths,
):
    pool_size = lax.axis_size("pool")
    rows_here = key_cache_rows.shape[0]
    head_dim = key_cache_rows.shape[3]
    q_cols = query_weight.shape[1]
    kv_cols = key_weight.shape[1]
    portion_width = adapter_down_weight.shape[2]
    rank_length = adapter_up_query.shape[1]
    resident_adapters = adapter_down_weight.shape[0]
    capacity = max(2, 2 * rows_here // pool_size)
    pool_here = lax.axis_index("pool")
    feature_part = lax.axis_index(("tp", "sub"))
    requests_here = lax.dynamic_slice_in_dim(row_request, pool_here * rows_here, rows_here)
    matches = requests_here[:, None] == jnp.arange(row_request.shape[0], dtype=jnp.int32)[None, :]
    row_adapter = jnp.sum(jnp.where(matches, request_adapter[None, :], 0), 1)
    row_length = jnp.sum(jnp.where(matches, lengths[None, :], 0), 1)
    owner_of = row_adapter // resident_adapters
    local_index = row_adapter % resident_adapters
    same_owner = owner_of[:, None] == owner_of[None, :]
    row_ids = jnp.arange(rows_here, dtype=jnp.int32)
    slot_of = jnp.sum(
        jnp.logical_and(same_owner, row_ids[None, :] < row_ids[:, None]).astype(jnp.int32), 1
    )
    picked = jnp.logical_and(
        owner_of[:, None, None] == jnp.arange(pool_size, dtype=jnp.int32)[None, :, None],
        slot_of[:, None, None] == jnp.arange(capacity, dtype=jnp.int32)[None, None, :],
    )
    picked_rows = picked.astype(jnp.bfloat16)
    send_index = jnp.sum(jnp.where(picked, local_index[:, None, None] + 1, 0), 0) - 1
    w_all = jnp.concatenate([query_weight, key_weight, value_weight], 1)

    def owner_work(received):
        gathered_rows, got_index = received
        onehot = (
            got_index[:, :, None] == jnp.arange(resident_adapters, dtype=jnp.int32)[None, None, :]
        )
        all_terms = jnp.einsum(
            "wxql,ahl->wxqah",
            gathered_rows,
            adapter_down_weight,
            preferred_element_type=jnp.float32,
        )
        shrunk = jnp.sum(jnp.where(onehot[:, :, None, :, None], all_terms, 0.0), 3)
        shrunk = lax.psum(shrunk.astype(jnp.bfloat16), ("tp", "sub")).astype(jnp.float32)
        low_rank = shrunk.astype(jnp.bfloat16)
        spread_query = jnp.where(
            onehot[:, :, None, :, None],
            low_rank[:, :, :, None, :rank_length],
            jnp.zeros((), jnp.bfloat16),
        )
        spread_value = jnp.where(
            onehot[:, :, None, :, None],
            low_rank[:, :, :, None, rank_length:],
            jnp.zeros((), jnp.bfloat16),
        )
        delta_q = jnp.einsum(
            "bhejy,jyt->bhet", spread_query, adapter_up_query, preferred_element_type=jnp.float32
        )
        delta_v = jnp.einsum(
            "bhejy,jyt->bhet", spread_value, adapter_up_value, preferred_element_type=jnp.float32
        )
        return (
            lax.all_to_all(
                delta_q.astype(jnp.bfloat16), "pool", split_axis=0, concat_axis=0, tiled=True
            ),
            lax.all_to_all(
                delta_v.astype(jnp.bfloat16), "pool", split_axis=0, concat_axis=0, tiled=True
            ),
        )

    def project(hidden_part):
        projected = lax.psum_scatter(
            jnp.einsum(
                "rsd,dc->rsc", hidden_part, w_all, preferred_element_type=jnp.float32
            ).astype(jnp.bfloat16),
            "pool",
            scatter_dimension=0,
            tiled=True,
        ).astype(jnp.float32)
        full_rows = lax.all_to_all(hidden_part, "pool", split_axis=0, concat_axis=2, tiled=True)
        own_slice = lax.dynamic_slice_in_dim(
            full_rows, feature_part * portion_width, portion_width, 2
        )
        send_rows = jnp.einsum(
            "rpc,rsd->pcsd", picked_rows, own_slice, preferred_element_type=jnp.float32
        ).astype(jnp.bfloat16)
        back_q, back_v = owner_work(
            (
                lax.all_to_all(send_rows, "pool", split_axis=0, concat_axis=0, tiled=True),
                lax.all_to_all(send_index, "pool", split_axis=0, concat_axis=0, tiled=True),
            )
        )
        delta_q = jnp.einsum(
            "rpc,pcsn->rsn", picked_rows, back_q, preferred_element_type=jnp.float32
        )
        delta_v = jnp.einsum(
            "rpc,pcsn->rsn", picked_rows, back_v, preferred_element_type=jnp.float32
        )
        raw_q = projected[:, :, :q_cols] + delta_q
        raw_k = projected[:, :, q_cols : q_cols + kv_cols]
        raw_v = projected[:, :, q_cols + kv_cols :] + delta_v
        return (raw_q, raw_k, raw_v)

    results = [project(hidden[:, step : step + 1]) for step in range(hidden.shape[1])]
    raw_q = jnp.concatenate([item[0] for item in results], 1)
    raw_k = jnp.concatenate([item[1] for item in results], 1)
    raw_v = jnp.concatenate([item[2] for item in results], 1)
    steps_total = hidden.shape[1]
    positions = row_length[:, None] + jnp.arange(steps_total, dtype=jnp.int32)[None, :]
    queries = rotate(
        raw_q.reshape(rows_here, steps_total, q_cols // head_dim, head_dim), positions
    ).astype(jnp.bfloat16)
    keys_new = rotate(
        raw_k.reshape(rows_here, steps_total, kv_cols // head_dim, head_dim), positions
    ).astype(jnp.bfloat16)
    values_new = raw_v.reshape(rows_here, steps_total, kv_cols // head_dim, head_dim).astype(
        jnp.bfloat16
    )
    return attend(queries, keys_new, values_new, key_cache_rows, value_cache_rows, row_length)


def solution(mesh):
    return jax.shard_map(
        on_device,
        mesh=mesh,
        in_specs=(
            P("groups", None, "pool"),
            P("pool", ("tp", "sub")),
            P("pool", ("tp", "sub")),
            P("pool", ("tp", "sub")),
            P(("groups", "pool"), ("tp", "sub"), None, None),
            P(("groups", "pool"), ("tp", "sub"), None, None),
            P(("groups", "pool"), None, ("tp", "sub")),
            P(("groups", "pool"), None, ("tp", "sub")),
            P(("groups", "pool"), None, ("tp", "sub")),
            P("groups"),
            P("groups"),
            P("groups"),
        ),
        out_specs=P(("groups", "pool"), None, ("tp", "sub")),
        check_vma=False,
    )
```

profile of v0, /device:TPU:0, one launch (start us, length us, event | category | flops | bytes accessed | tf_op | source)
XLA Modules:
  0.0 198.2 jit_solution(17988438751372826867)
XLA Ops:
  6.6 8.5 %constant_dynamic-update-slice_fusion.2 = bf16[2048,2560]{1,0:T(8,128)(2,1)} fusion(bf16[2048,2048]{1,0:T(8,128)(2,1)} %param.13), kind=kLoop, calls=%fused_computation.151 | loop fusion | bytes 16777216
  17.3 6.6 %fusion.2 = bf16[64,1,2560]{2,0,1:T(8,128)(2,1)} fusion(bf16[2048,2560]{1,0:T(8,128)(2,1)} %constant_dynamic-update-slice_fusion, bf16[64,3,2048]{2,0,1:T(8,128)(2,1)S(1)} %copy-done.1), kind=kOutput, calls=%fused_computation.5 | convolution fusion | flops 671252480 | bytes 11075584 | tf_op jit(solution)/shard_map/rsd,dc->rsc/dot_general | solution.py:145
  25.2 6.3 %all-to-all-start = ((s32[4,1,8]{2,1,0:T(1,128)}), s32[4,1,8]{2,1,0:T(1,128)S(1)}, u32[]{:S(2)}, u32[]{:S(2)}) async-start(s32[4,1,8]{2,1,0:T(1,128)} %bitcast.4), calls=%async_computation.1 | async-start | bytes 4096 | tf_op jit(solution)/shard_map/all_to_all | solution.py:162
  31.5 6.7 %fusion.1 = bf16[64,1,2560]{2,0,1:T(8,128)(2,1)} fusion(bf16[2048,2560]{1,0:T(8,128)(2,1)} %constant_dynamic-update-slice_fusion, bf16[64,3,2048]{2,0,1:T(8,128)(2,1)S(1)} %copy-done.1), kind=kOutput, calls=%fused_computation.4 | convolution fusion | flops 671252480 | bytes 11075584 | tf_op jit(solution)/shard_map/rsd,dc->rsc/dot_general | solution.py:145
  41.4 5.2 %all-to-all-start.7 = ((bf16[4,2,16384]{2,1,0:T(2,128)(2,1)}), bf16[4,2,16384]{2,1,0:T(2,128)(2,1)S(1)}, u32[]{:S(2)}, u32[]{:S(2)}) async-start(bf16[4,2,16384]{2,1,0:T(2,128)(2,1)} %reshape.423), calls=%async_computation.10 | async-start | bytes 524288 | tf_op jit(solution)/shard_map/all_to_all | solution.py:152
  46.6 6.6 %fusion = bf16[64,1,2560]{2,0,1:T(8,128)(2,1)} fusion(bf16[2048,2560]{1,0:T(8,128)(2,1)} %constant_dynamic-update-slice_fusion, bf16[64,3,2048]{2,0,1:T(8,128)(2,1)S(1)} %copy-done.1), kind=kOutput, calls=%fused_computation.3 | convolution fusion | flops 671252480 | bytes 11075584 | tf_op jit(solution)/shard_map/rsd,dc->rsc/dot_general | solution.py:145
  53.3 1.8 reduce.7
  57.7 5.1 %all-to-all-start.4 = ((bf16[4,2,16384]{2,1,0:T(2,128)(2,1)}), bf16[4,2,16384]{2,1,0:T(2,128)(2,1)S(1)}, u32[]{:S(2)}, u32[]{:S(2)}) async-start(bf16[4,2,16384]{2,1,0:T(2,128)(2,1)} %reshape.425), calls=%async_computation.6 | async-start | bytes 524288 | tf_op jit(solution)/shard_map/all_to_all | solution.py:152
  62.8 8.2 %all-to-all-done.4 = bf16[4,2,16384]{2,1,0:T(2,128)(2,1)S(1)} async-done(((bf16[4,2,16384]{2,1,0:T(2,128)(2,1)}), bf16[4,2,16384]{2,1,0:T(2,128)(2,1)S(1)}, u32[]{:S(2)}, u32[]{:S(2)}) %all-to-all-start.4) | async-done | bytes 262176 | tf_op jit(solution)/shard_map/all_to_all | solution.py:152
  71.1 4.0 %all-to-all-start.1 = ((bf16[4,2,16384]{2,1,0:T(2,128)(2,1)}), bf16[4,2,16384]{2,1,0:T(2,128)(2,1)}, u32[]{:S(2)}, u32[]{:S(2)}) async-start(bf16[4,2,16384]{2,1,0:T(2,128)(2,1)} %reshape.427), calls=%async_computation.2 | async-start | bytes 524288 | tf_op jit(solution)/shard_map/all_to_all | solution.py:152
  76.6 10.1 %all-to-all-done.1 = bf16[4,2,16384]{2,1,0:T(2,128)(2,1)} async-done(((bf16[4,2,16384]{2,1,0:T(2,128)(2,1)}), bf16[4,2,16384]{2,1,0:T(2,128)(2,1)}, u32[]{:S(2)}, u32[]{:S(2)}) %all-to-all-start.1) | async-done | bytes 262176 | tf_op jit(solution)/shard_map/all_to_all | solution.py:152
  86.7 3.3 %all-to-all-start.8 = ((bf16[4,8,1,2048]{3,1,2,0:T(8,128)(2,1)}), bf16[4,8,1,2048]{3,1,2,0:T(8,128)(2,1)S(1)}, u32[]{:S(2)}, u32[]{:S(2)}) async-start(bf16[4,8,1,2048]{3,1,2,0:T(8,128)(2,1)} %fusion.8), calls=%async_computation.11 | async-start | bytes 262144 | tf_op jit(solution)/shard_map/all_to_all | solution.py:161
  92.3 3.6 %all-to-all-done.8 = bf16[4,8,1,2048]{3,1,2,0:T(8,128)(2,1)S(1)} async-done(((bf16[4,8,1,2048]{3,1,2,0:T(8,128)(2,1)}), bf16[4,8,1,2048]{3,1,2,0:T(8,128)(2,1)S(1)}, u32[]{:S(2)}, u32[]{:S(2)}) %all-to-all-start.8) | async-done | bytes 131104 | tf_op jit(solution)/shard_map/all_to_all | solution.py:161
  95.9 3.9 %all-to-all-start.5 = ((bf16[4,8,1,2048]{3,1,2,0:T(8,128)(2,1)}), bf16[4,8,1,2048]{3,1,2,0:T(8,128)(2,1)}, u32[]{:S(2)}, u32[]{:S(2)}) async-start(bf16[4,8,1,2048]{3,1,2,0:T(8,128)(2,1)} %fusion.7), calls=%async_computation.7 | async-start | bytes 262144 | tf_op jit(solution)/shard_map/all_to_all | solution.py:161
  102.1 3.8 %all-to-all-done.5 = bf16[4,8,1,2048]{3,1,2,0:T(8,128)(2,1)} async-done(((bf16[4,8,1,2048]{3,1,2,0:T(8,128)(2,1)}), bf16[4,8,1,2048]{3,1,2,0:T(8,128)(2,1)}, u32[]{:S(2)}, u32[]{:S(2)}) %all-to-all-start.5) | async-done | bytes 131104 | tf_op jit(solution)/shard_map/all_to_all | solution.py:161
  105.8 3.3 %all-to-all-start.2 = ((bf16[4,8,1,2048]{3,1,2,0:T(8,128)(2,1)}), bf16[4,8,1,2048]{3,1,2,0:T(8,128)(2,1)S(1)}, u32[]{:S(2)}, u32[]{:S(2)}) async-start(bf16[4,8,1,2048]{3,1,2,0:T(8,128)(2,1)} %fusion.6), calls=%async_computation.3 | async-start | bytes 262144 | tf_op jit(solution)/shard_map/all_to_all | solution.py:161
  109.2 1.6 fusion.23
  110.8 1.7 fusion.22
  112.6 2.5 %all-to-all-done.2 = bf16[4,8,1,2048]{3,1,2,0:T(8,128)(2,1)S(1)} async-done(((bf16[4,8,1,2048]{3,1,2,0:T(8,128)(2,1)}), bf16[4,8,1,2048]{3,1,2,0:T(8,128)(2,1)S(1)}, u32[]{:S(2)}, u32[]{:S(2)}) %all-to-all-start.2) | async-done | bytes 131104 | tf_op jit(solution)/shard_map/all_to_all | solution.py:161
  116.7 10.3 %all-reduce = (bf16[4,8,1,128]{3,1,0,2:T(8,128)(2,1)S(1)}, bf16[4,8,1,128]{3,1,0,2:T(8,128)(2,1)S(1)}, bf16[4,8,1,128]{3,1,0,2:T(8,128)(2,1)S(1)}) all-reduce(bf16[4,8,1,128]{3,1,0,2:T(8,128)(2,1)S(1)} %bitcast.298, bf16[4,8,1,128]{3,1,0,2:T(8,128)(2,1)S(1)} %bitcast.299, ...), channel_id=1, replica_groups=mesh['groups'=2,'pool'=4,'tp'=2,'sub'=2] {'tp','sub'}, use_global_device_ids=true, to_apply=%region_12.13 | all-reduce | flops 12288 | bytes 49152 | tf_op jit(solution)/shard_map/psum | solution.py:116
  128.0 3.2 %all-to-all-start.12 = ((bf16[4,8,1,256]{3,1,2,0:T(8,128)(2,1)}), bf16[4,8,1,256]{3,1,2,0:T(8,128)(2,1)S(1)}, u32[]{:S(2)}, u32[]{:S(2)}) async-start(bf16[4,8,1,256]{3,1,2,0:T(8,128)(2,1)} %fusion.27), calls=%async_computation.15 | async-start | bytes 32768 | tf_op jit(solution)/shard_map/all_to_all | solution.py:138
  139.1 5.1 %all-to-all-start.11 = ((bf16[4,8,1,256]{3,1,2,0:T(8,128)(2,1)}), bf16[4,8,1,256]{3,1,2,0:T(8,128)(2,1)S(1)}, u32[]{:S(2)}, u32[]{:S(2)}) async-start(bf16[4,8,1,256]{3,1,2,0:T(8,128)(2,1)} %fusion.28), calls=%async_computation.14 | async-start | bytes 32768 | tf_op jit(solution)/shard_map/all_to_all | solution.py:138
  145.3 4.5 %all-to-all-done.11 = bf16[4,8,1,256]{3,1,2,0:T(8,128)(2,1)S(1)} async-done(((bf16[4,8,1,256]{3,1,2,0:T(8,128)(2,1)}), bf16[4,8,1,256]{3,1,2,0:T(8,128)(2,1)S(1)}, u32[]{:S(2)}, u32[]{:S(2)}) %all-to-all-start.11) | async-done | bytes 16416 | tf_op jit(solution)/shard_map/all_to_all | solution.py:138
  149.8 3.2 %all-to-all-start.10 = ((bf16[4,8,1,256]{3,1,2,0:T(8,128)(2,1)}), bf16[4,8,1,256]{3,1,2,0:T(8,128)(2,1)S(1)}, u32[]{:S(2)}, u32[]{:S(2)}) async-start(bf16[4,8,1,256]{3,1,2,0:T(8,128)(2,1)} %fusion.29), calls=%async_computation.13 | async-start | bytes 32768 | tf_op jit(solution)/shard_map/all_to_all | solution.py:138
  154.2 4.5 %all-to-all-done.10 = bf16[4,8,1,256]{3,1,2,0:T(8,128)(2,1)S(1)} async-done(((bf16[4,8,1,256]{3,1,2,0:T(8,128)(2,1)}), bf16[4,8,1,256]{3,1,2,0:T(8,128)(2,1)S(1)}, u32[]{:S(2)}, u32[]{:S(2)}) %all-to-all-start.10) | async-done | bytes 16416 | tf_op jit(solution)/shard_map/all_to_all | solution.py:138
  158.6 3.3 %all-to-all-start.9 = ((bf16[4,8,1,2048]{3,1,2,0:T(8,128)(2,1)}), bf16[4,8,1,2048]{3,1,2,0:T(8,128)(2,1)S(1)}, u32[]{:S(2)}, u32[]{:S(2)}) async-start(bf16[4,8,1,2048]{3,1,2,0:T(8,128)(2,1)} %fusion.9), calls=%async_computation.12 | async-start | bytes 262144 | tf_op jit(solution)/shard_map/all_to_all | solution.py:135
  162.3 5.6 %all-to-all-done.9 = bf16[4,8,1,2048]{3,1,2,0:T(8,128)(2,1)S(1)} async-done(((bf16[4,8,1,2048]{3,1,2,0:T(8,128)(2,1)}), bf16[4,8,1,2048]{3,1,2,0:T(8,128)(2,1)S(1)}, u32[]{:S(2)}, u32[]{:S(2)}) %all-to-all-start.9) | async-done | bytes 131104 | tf_op jit(solution)/shard_map/all_to_all | solution.py:135
  167.9 3.3 %all-to-all-start.6 = ((bf16[4,8,1,2048]{3,1,2,0:T(8,128)(2,1)}), bf16[4,8,1,2048]{3,1,2,0:T(8,128)(2,1)S(1)}, u32[]{:S(2)}, u32[]{:S(2)}) async-start(bf16[4,8,1,2048]{3,1,2,0:T(8,128)(2,1)} %fusion.10), calls=%async_computation.8 | async-start | bytes 262144 | tf_op jit(solution)/shard_map/all_to_all | solution.py:135
  171.4 5.7 %all-to-all-done.6 = bf16[4,8,1,2048]{3,1,2,0:T(8,128)(2,1)S(1)} async-done(((bf16[4,8,1,2048]{3,1,2,0:T(8,128)(2,1)}), bf16[4,8,1,2048]{3,1,2,0:T(8,128)(2,1)S(1)}, u32[]{:S(2)}, u32[]{:S(2)}) %all-to-all-start.6) | async-done | bytes 131104 | tf_op jit(solution)/shard_map/all_to_all | solution.py:135
  177.1 3.3 %all-to-all-start.3 = ((bf16[4,8,1,2048]{3,1,2,0:T(8,128)(2,1)}), bf16[4,8,1,2048]{3,1,2,0:T(8,128)(2,1)S(1)}, u32[]{:S(2)}, u32[]{:S(2)}) async-start(bf16[4,8,1,2048]{3,1,2,0:T(8,128)(2,1)} %fusion.11), calls=%async_computation.4 | async-start | bytes 262144 | tf_op jit(solution)/shard_map/all_to_all | solution.py:135
  180.6 5.7 %all-to-all-done.3 = bf16[4,8,1,2048]{3,1,2,0:T(8,128)(2,1)S(1)} async-done(((bf16[4,8,1,2048]{3,1,2,0:T(8,128)(2,1)}), bf16[4,8,1,2048]{3,1,2,0:T(8,128)(2,1)S(1)}, u32[]{:S(2)}, u32[]{:S(2)}) %all-to-all-start.3) | async-done | bytes 131104 | tf_op jit(solution)/shard_map/all_to_all | solution.py:135
  188.5 2.1 %fusion.42 = f32[16,2,24,128]{3,2,1,0:T(8,128)S(1)} fusion(bf16[16,2,256,128]{3,2,1,0:T(8,128)(2,1)} %param.17, f32[16,2,24,256]{3,2,1,0:T(8,128)S(1)} %get-tuple-element.30, f32[16,2,24]{2,1,0:T(2,128)S(1)} %add.132), kind=kOutput, calls=%fused_computation.67 | convolution fusion | flops 50724864 | bytes 3279872 | tf_op jit(solution)/shard_map/rkqt,rkth->rkqh/dot_general | solution.py:50
  (108 shorter events, 31.9 us)
Async XLA Ops:
  6.5 180.3 %copy-start = (bf16[16,2,256,128]{3,2,1,0:T(8,128)(2,1)S(1)}, bf16[16,2,256,128]{3,2,1,0:T(8,128)(2,1)}, u32[]{:S(2)}) copy-start(bf16[16,2,256,128]{3,2,1,0:T(8,128)(2,1)} %param.16) | copy-start | bytes 6291460
  6.5 10.8 %copy-start.1 = (bf16[64,3,2048]{2,0,1:T(8,128)(2,1)S(1)}, bf16[64,3,2048]{2,0,1:T(8,128)(2,1)}, u32[]{:S(2)}) copy-start(bf16[64,3,2048]{2,0,1:T(8,128)(2,1)} %param.12) | copy-start | bytes 2359300
  6.5 129.4 %reduce-scatter.8.cloned.1.call-start = ((), (), s32[]{:S(2)}) async-start(), calls=%async_computation.18 | async-start | bytes 409600 | tf_op jit(solution)/shard_map/reduce_scatter | solution.py:144
  6.5 8.5 %copy-start.4 = (bf16[2048,256]{1,0:T(8,128)(2,1)S(1)}, bf16[2048,256]{1,0:T(8,128)(2,1)}, u32[]{:S(2)}) copy-start(bf16[2048,256]{1,0:T(8,128)(2,1)} %param.14) | copy-start | bytes 3145732
  6.5 9.6 %copy-start.5 = (bf16[2048,256]{1,0:T(8,128)(2,1)S(1)}, bf16[2048,256]{1,0:T(8,128)(2,1)}, u32[]{:S(2)}) copy-start(bf16[2048,256]{1,0:T(8,128)(2,1)} %param.15) | copy-start | bytes 3145732
  16.2 7.8 %copy-start.10 = (s32[64]{0:T(128)S(1)}, s32[64]{0:T(128)}, u32[]{:S(2)}) copy-start(s32[64]{0:T(128)} %param.22) | copy-start | bytes 772
  16.2 7.9 %copy-start.7 = (s32[64]{0:T(128)S(1)}, s32[64]{0:T(128)}, u32[]{:S(2)}) copy-start(s32[64]{0:T(128)} %param.21) | copy-start | bytes 772
  16.2 7.9 %copy-start.8 = (s32[64]{0:T(128)S(1)}, s32[64]{0:T(128)}, u32[]{:S(2)}) copy-start(s32[64]{0:T(128)} %param.23) | copy-start | bytes 772
  25.2 16.2 %all-to-all-start = ((s32[4,1,8]{2,1,0:T(1,128)}), s32[4,1,8]{2,1,0:T(1,128)S(1)}, u32[]{:S(2)}, u32[]{:S(2)}) async-start(s32[4,1,8]{2,1,0:T(1,128)} %bitcast.4), calls=%async_computation.1 | async-start | bytes 4096 | tf_op jit(solution)/shard_map/all_to_all | solution.py:162
  31.5 105.1 %reduce-scatter.6.cloned.1.call-start = ((), (), s32[]{:S(2)}) async-start(), calls=%async_computation.17 | async-start | bytes 409600 | tf_op jit(solution)/shard_map/reduce_scatter | solution.py:144
  41.4 14.6 %copy-start.6 = (bf16[64,1,2048]{2,0,1:T(8,128)(2,1)S(1)}, bf16[64,1,2048]{2,0,1:T(8,128)(2,1)}, u32[]{:S(2)}) copy-start(bf16[64,1,2048]{2,0,1:T(8,128)(2,1)} %get-tuple-element.10) | copy-start | bytes 786436
  41.4 16.3 %all-to-all-start.7 = ((bf16[4,2,16384]{2,1,0:T(2,128)(2,1)}), bf16[4,2,16384]{2,1,0:T(2,128)(2,1)S(1)}, u32[]{:S(2)}, u32[]{:S(2)}) async-start(bf16[4,2,16384]{2,1,0:T(2,128)(2,1)} %reshape.423), calls=%async_computation.10 | async-start | bytes 524288 | tf_op jit(solution)/shard_map/all_to_all | solution.py:152
  46.6 90.7 %reduce-scatter.4.cloned.1.call-start = ((), (), s32[]{:S(2)}) async-start(), calls=%async_computation.16 | async-start | bytes 409600 | tf_op jit(solution)/shard_map/reduce_scatter | solution.py:144
  53.2 73.9 %copy-start.9 = (bf16[2,64,256]{2,1,0:T(8,128)(2,1)S(1)}, bf16[2,64,256]{2,1,0:T(8,128)(2,1)}, u32[]{:S(2)}) copy-start(bf16[2,64,256]{2,1,0:T(8,128)(2,1)} %param.20) | copy-start | bytes 196612
  53.2 79.8 %copy-start.2 = (bf16[2,64,2048]{2,1,0:T(8,128)(2,1)S(1)}, bf16[2,64,2048]{2,1,0:T(8,128)(2,1)}, u32[]{:S(2)}) copy-start(bf16[2,64,2048]{2,1,0:T(8,128)(2,1)} %param.19) | copy-start | bytes 1572868
  57.7 13.4 %all-to-all-start.4 = ((bf16[4,2,16384]{2,1,0:T(2,128)(2,1)}), bf16[4,2,16384]{2,1,0:T(2,128)(2,1)S(1)}, u32[]{:S(2)}, u32[]{:S(2)}) async-start(bf16[4,2,16384]{2,1,0:T(2,128)(2,1)} %reshape.425), calls=%async_computation.6 | async-start | bytes 524288 | tf_op jit(solution)/shard_map/all_to_all | solution.py:152
  71.1 4.1 %copy-start.3 = (bf16[4,2,16384]{2,1,0:T(2,128)(2,1)}, bf16[4,2,16384]{2,1,0:T(2,128)(2,1)S(1)}, u32[]{:S(2)}) copy-start(bf16[4,2,16384]{2,1,0:T(2,128)(2,1)S(1)} %all-to-all-done.4) | copy-start | bytes 786436
  71.1 15.6 %all-to-all-start.1 = ((bf16[4,2,16384]{2,1,0:T(2,128)(2,1)}), bf16[4,2,16384]{2,1,0:T(2,128)(2,1)}, u32[]{:S(2)}, u32[]{:S(2)}) async-start(bf16[4,2,16384]{2,1,0:T(2,128)(2,1)} %reshape.427), calls=%async_computation.2 | async-start | bytes 524288 | tf_op jit(solution)/shard_map/all_to_all | solution.py:152
  86.7 9.2 %all-to-all-start.8 = ((bf16[4,8,1,2048]{3,1,2,0:T(8,128)(2,1)}), bf16[4,8,1,2048]{3,1,2,0:T(8,128)(2,1)S(1)}, u32[]{:S(2)}, u32[]{:S(2)}) async-start(bf16[4,8,1,2048]{3,1,2,0:T(8,128)(2,1)} %fusion.8), calls=%async_computation.11 | async-start | bytes 262144 | tf_op jit(solution)/shard_map/all_to_all | solution.py:161
  95.9 9.9 %all-to-all-start.5 = ((bf16[4,8,1,2048]{3,1,2,0:T(8,128)(2,1)}), bf16[4,8,1,2048]{3,1,2,0:T(8,128)(2,1)}, u32[]{:S(2)}, u32[]{:S(2)}) async-start(bf16[4,8,1,2048]{3,1,2,0:T(8,128)(2,1)} %fusion.7), calls=%async_computation.7 | async-start | bytes 262144 | tf_op jit(solution)/shard_map/all_to_all | solution.py:161
  105.8 9.2 %all-to-all-start.2 = ((bf16[4,8,1,2048]{3,1,2,0:T(8,128)(2,1)}), bf16[4,8,1,2048]{3,1,2,0:T(8,128)(2,1)S(1)}, u32[]{:S(2)}, u32[]{:S(2)}) async-start(bf16[4,8,1,2048]{3,1,2,0:T(8,128)(2,1)} %fusion.6), calls=%async_computation.3 | async-start | bytes 262144 | tf_op jit(solution)/shard_map/all_to_all | solution.py:161
  128.0 11.1 %all-to-all-start.12 = ((bf16[4,8,1,256]{3,1,2,0:T(8,128)(2,1)}), bf16[4,8,1,256]{3,1,2,0:T(8,128)(2,1)S(1)}, u32[]{:S(2)}, u32[]{:S(2)}) async-start(bf16[4,8,1,256]{3,1,2,0:T(8,128)(2,1)} %fusion.27), calls=%async_computation.15 | async-start | bytes 32768 | tf_op jit(solution)/shard_map/all_to_all | solution.py:138
  139.1 10.7 %all-to-all-start.11 = ((bf16[4,8,1,256]{3,1,2,0:T(8,128)(2,1)}), bf16[4,8,1,256]{3,1,2,0:T(8,128)(2,1)S(1)}, u32[]{:S(2)}, u32[]{:S(2)}) async-start(bf16[4,8,1,256]{3,1,2,0:T(8,128)(2,1)} %fusion.28), calls=%async_computation.14 | async-start | bytes 32768 | tf_op jit(solution)/shard_map/all_to_all | solution.py:138
  149.8 8.8 %all-to-all-start.10 = ((bf16[4,8,1,256]{3,1,2,0:T(8,128)(2,1)}), bf16[4,8,1,256]{3,1,2,0:T(8,128)(2,1)S(1)}, u32[]{:S(2)}, u32[]{:S(2)}) async-start(bf16[4,8,1,256]{3,1,2,0:T(8,128)(2,1)} %fusion.29), calls=%async_computation.13 | async-start | bytes 32768 | tf_op jit(solution)/shard_map/all_to_all | solution.py:138
  158.6 9.2 %all-to-all-start.9 = ((bf16[4,8,1,2048]{3,1,2,0:T(8,128)(2,1)}), bf16[4,8,1,2048]{3,1,2,0:T(8,128)(2,1)S(1)}, u32[]{:S(2)}, u32[]{:S(2)}) async-start(bf16[4,8,1,2048]{3,1,2,0:T(8,128)(2,1)} %fusion.9), calls=%async_computation.12 | async-start | bytes 262144 | tf_op jit(solution)/shard_map/all_to_all | solution.py:135
  167.9 9.2 %all-to-all-start.6 = ((bf16[4,8,1,2048]{3,1,2,0:T(8,128)(2,1)}), bf16[4,8,1,2048]{3,1,2,0:T(8,128)(2,1)S(1)}, u32[]{:S(2)}, u32[]{:S(2)}) async-start(bf16[4,8,1,2048]{3,1,2,0:T(8,128)(2,1)} %fusion.10), calls=%async_computation.8 | async-start | bytes 262144 | tf_op jit(solution)/shard_map/all_to_all | solution.py:135
  177.1 9.2 %all-to-all-start.3 = ((bf16[4,8,1,2048]{3,1,2,0:T(8,128)(2,1)}), bf16[4,8,1,2048]{3,1,2,0:T(8,128)(2,1)S(1)}, u32[]{:S(2)}, u32[]{:S(2)}) async-start(bf16[4,8,1,2048]{3,1,2,0:T(8,128)(2,1)} %fusion.11), calls=%async_computation.4 | async-start | bytes 262144 | tf_op jit(solution)/shard_map/all_to_all | solution.py:135
Sparse Core Ops, SparseCore 0:
  24.1 22.7 reduce-scatter.7
  49.1 18.5 reduce-scatter.5
  70.0 19.1 reduce-scatter.3
where the time goes:
time: 200 us; the launch traced here: 198 us
  waiting for transfers between devices  54.2 us (27%)
  starting transfers between devices  52.8 us (26%)
  matrix products  38.2 us (19%)
  local copies, waits for them, and re-layouts  21.4 us (11%)
  between operations  13.5 us (7%)
  blocking collectives  10.3 us (5%)
  other arithmetic  7.84 us (4%)
    dot_general x3, matrix products, project(): jnp.einsum('rsd,dc->rsc', hidden_part, w_all, preferred_element_type=jnp....  19.9 us
    all_to_all x3, waiting for transfers between devices, project(): lax.all_to_all(hidden_part, 'pool', split_axis=0, concat_axis=2, tiled=True)  18.3 us
    all_to_all x3, waiting for transfers between devices, owner_work(): lax.all_to_all(delta_q.astype(jnp.bfloat16), 'pool', split_axis=0, concat...  16.9 us
    unnamed x34, local copies, waits for them, and re-layouts  15.5 us
    all_to_all x3, starting transfers between devices, project(): lax.all_to_all(hidden_part, 'pool', split_axis=0, concat_axis=2, tiled=True)  14.4 us
    all_to_all x3, starting transfers between devices, owner_work(): lax.all_to_all(delta_v.astype(jnp.bfloat16), 'pool', split_axis=0, concat...  11.6 us
    all_to_all x3, starting transfers between devices, project(): lax.all_to_all(send_rows, 'pool', split_axis=0, concat_axis=0, tiled=True)  10.6 us
    psum x1, blocking collectives, owner_work(): lax.psum(shrunk.astype(jnp.bfloat16), ('tp', 'sub')).astype(jnp.float32)  10.3 us
  transfers between devices with their start and end apart: 16, of which 10 were waited for; matrix products, arithmetic and copies ran while one was open for 23% of the time, Pallas kernels for 0%

commit v1 on v0

v1 whole, which is shorter than its diff:
```python
import functools
import math

import jax
import jax.numpy as jnp
from jax import lax
from jax.experimental import pallas as pl
from jax.experimental.pallas import tpu as pltpu
from jax.sharding import PartitionSpec as P

ROPE_BASE = 500000.0
BF16 = jnp.bfloat16
F32 = jnp.float32
FEATURE_AXES = ("tp", "sub")
CARRIER = ((0, 3, 2, 1), (2, 1, 0, 3), (3, 1, 2, 0), (1, 2, 0, 3))
VMEM_LIMIT = 48 * 1024 * 1024


def call(body, out_shape, args, in_specs=None, out_specs=None, grid=None, scratch=(), flops=0, bytes_=0, **more):
    whole = pl.BlockSpec(memory_space=pltpu.VMEM)
    kwargs = {} if grid is None else {"grid": grid}
    if in_specs is None:
        in_specs = [whole] * len(args)
    if out_specs is None:
        out_specs = jax.tree.map(lambda _: whole, out_shape)
    return pl.pallas_call(
        body,
        out_shape=out_shape,
        in_specs=in_specs,
        out_specs=out_specs,
        scratch_shapes=list(scratch),
        compiler_params=pltpu.CompilerParams(vmem_limit_bytes=VMEM_LIMIT),
        cost_estimate=pl.CostEstimate(flops=flops, bytes_accessed=bytes_, transcendentals=0),
        **kwargs,
        **more,
    )(*args)


VMEM = pl.BlockSpec(memory_space=pltpu.VMEM)
SMEM = pl.BlockSpec(memory_space=pltpu.SMEM)


def iota(shape, dim):
    return lax.broadcasted_iota(jnp.int32, shape, dim)


def nn(a, b):
    return lax.dot_general(a, b, (((1,), (0,)), ((), ())), preferred_element_type=F32)


def nt(a, b):
    return lax.dot_general(a, b, (((1,), (1,)), ((), ())), preferred_element_type=F32)


def tn(a, b):
    return lax.dot_general(a, b, (((0,), (0,)), ((), ())), preferred_element_type=F32)


def row_facts(row_request, request_values, home_rows, resident):
    rows = row_request.shape[1]
    across, down = iota((rows, rows), 1), iota((rows, rows), 0)
    eye = across == down
    request_col = jnp.sum(jnp.where(eye, row_request.astype(F32), 0.0), 1, keepdims=True)
    held = request_col == across.astype(F32)
    adapter_col = jnp.sum(jnp.where(held, request_values.astype(F32), 0.0), 1, keepdims=True)
    adapter_row = jnp.sum(jnp.where(eye, adapter_col, 0.0), 0, keepdims=True)
    owner_col = jnp.floor((adapter_col + 0.5) / resident)
    owner_row = jnp.floor((adapter_row + 0.5) / resident)
    before = (owner_col == owner_row) & (down < across) & (down // home_rows == across // home_rows)
    slot_row = jnp.sum(jnp.where(before, 1.0, 0.0), 0, keepdims=True)
    return adapter_row, owner_row, slot_row


def slot_table(owner_row, slot_row, owner, home_rows, cap):
    rows = owner_row.shape[1]
    places = rows // home_rows * cap
    place, row = iota((places, rows), 0), iota((places, rows), 1)
    return (
        (owner_row == owner.astype(F32))
        & (place // cap == row // home_rows)
        & (slot_row == (place % cap).astype(F32))
    )


def select_body(home_rows, cap, resident, owners_here, rr_ref, ra_ref, where_ref, hid_ref, *outs):
    _, owner_row, slot_row = row_facts(rr_ref[...], ra_ref[...], home_rows, resident)
    for i, out in enumerate(outs):
        table = slot_table(owner_row, slot_row, where_ref[1 + i], home_rows, cap).astype(BF16)
        places = table.shape[0]
        for s in range(hid_ref.shape[0]):
            out[s * places : (s + 1) * places] = nn(table, hid_ref[s]).astype(BF16)


def project_body(home_rows, homes, emit_chunks, where_ref, x_ref, q_ref, k_ref, v_ref, *rest):
    steps, rows = x_ref.shape[0] // (homes * home_rows), homes * home_rows
    tile = q_ref.shape[1]
    head_dim = k_ref.shape[1]
    if emit_chunks:
        outs, scr, scr_kv = rest[:homes], rest[homes], rest[homes + 1]
    else:
        (out,) = rest
    i = pl.program_id(0)
    columns = pl.ds(pl.multiple_of(i * tile, tile), tile)
    product = nn(x_ref[...], q_ref[...])
    q_cols = pl.num_programs(0) * tile

    def put(value, source, where):
        source[...] = value
        for d in range(homes):
            home = where_ref[0] ^ d
            for s in range(steps):
                begin = pl.multiple_of(s * rows + home * home_rows, home_rows)
                outs[d][s * home_rows : (s + 1) * home_rows, where] = source[
                    pl.ds(begin, home_rows), :
                ].astype(BF16)

    if emit_chunks:
        put(product, scr, columns)
    else:
        out[:, columns] = product

    @pl.when(i == 0)
    def _():
        kv = jnp.concatenate([nn(x_ref[...], k_ref[...]), nn(x_ref[...], v_ref[...])], 1)
        width = outs[0].shape[1] if emit_chunks else out.shape[1]
        if emit_chunks:
            put(kv, scr_kv, slice(width - 2 * head_dim, width))
        else:
            out[:, width - 2 * head_dim :] = kv


def shrink_body(home_rows, cap, resident, parts, rr_ref, ra_ref, where_ref, down_ref, *rest):
    sent, out = rest[:-1], rest[-1]
    adapter_row, owner_row, slot_row = row_facts(rr_ref[...], ra_ref[...], home_rows, resident)
    me = where_ref[0]
    table = slot_table(owner_row, slot_row, me, home_rows, cap)
    local = jnp.sum(jnp.where(table, adapter_row - (me * resident).astype(F32) + 1.0, 0.0), 1, keepdims=True) - 1.0
    places = table.shape[0]
    steps = sent[0].shape[0] // places
    local = jnp.concatenate([local] * steps, 0)
    width = sent[0].shape[1]
    total = None
    for a in range(resident):
        term = None
        for i in range(parts):
            if parts == 1:
                block = down_ref[a]
            else:
                part = lax.rem(me + parts * places - i, parts)
                block = down_ref[a, :, pl.ds(pl.multiple_of(part * width, width), width)]
            piece = nt(sent[i][...], block)
            term = piece if term is None else term + piece
        term = jnp.where(local == float(a), term, 0.0)
        total = term if total is None else total + term
    out[...] = total.astype(BF16)


def expand_body(home_rows, homes, cap, resident, early, late, rr_ref, ra_ref, where_ref, upq_ref, upv_ref, *rest):
    n_parts = len(rest) - len(late) - homes * (len(early) + len(late)) - (1 if late else 0)
    shares, rest = rest[:n_parts], rest[n_parts:]
    partials, rest = rest[: len(late)], rest[len(late) :]
    early_outs, rest = rest[: homes * len(early)], rest[homes * len(early) :]
    late_outs, rest = rest[: homes * len(late)], rest[homes * len(late) :]
    adapter_row, owner_row, slot_row = row_facts(rr_ref[...], ra_ref[...], home_rows, resident)
    me = where_ref[0]
    table = slot_table(owner_row, slot_row, me, home_rows, cap)
    places, rows = table.shape
    local = jnp.sum(jnp.where(table, adapter_row - (me * resident).astype(F32) + 1.0, 0.0), 1, keepdims=True) - 1.0
    spread = table.astype(BF16)
    shrunk = shares[0][...].astype(F32)
    for share in shares[1:]:
        shrunk = shrunk + share[...].astype(F32)
    steps = shrunk.shape[0] // places
    local = jnp.concatenate([local] * steps, 0)
    rank = upq_ref.shape[1]
    low_q, low_v = shrunk[:, :rank], shrunk[:, rank:]
    masked_q = [jnp.where(local == float(a), low_q, 0.0).astype(BF16) for a in range(resident)]
    masked_v = [jnp.where(local == float(a), low_v, 0.0).astype(BF16) for a in range(resident)]
    kv_heads = len(early) + len(late)
    width_q = upq_ref.shape[2] // kv_heads
    width_v = upv_ref.shape[2] // kv_heads

    def up(h):
        delta_q = delta_v = None
        for a in range(resident):
            term_q = nn(masked_q[a], upq_ref[a, :, h * width_q : (h + 1) * width_q])
            term_v = nn(masked_v[a], upv_ref[a, :, h * width_v : (h + 1) * width_v])
            delta_q = term_q if delta_q is None else delta_q + term_q
            delta_v = term_v if delta_v is None else delta_v + term_v
        return delta_q, delta_v

    for n, h in enumerate(early):
        both = jnp.concatenate(up(h), 1)
        scr = rest[-1]
        scr[: both.shape[0], : both.shape[1]] = both
        for d in range(homes):
            home = me ^ d
            pieces = []
            for s in range(steps):
                begin = pl.multiple_of(s * places + home * cap, cap)
                pieces.append(scr[pl.ds(begin, cap), : both.shape[1]])
            early_outs[n * homes + d][...] = jnp.concatenate(pieces, 0).astype(BF16)
    for n, h in enumerate(late):
        delta_q, delta_v = up(h)
        scr = rest[-1]
        for s in range(steps):
            here = slice(s * places, (s + 1) * places)
            there = slice(s * rows, (s + 1) * rows)
            scr[there, :width_q] = partials[n][there, :width_q] + tn(spread, delta_q[here].astype(BF16))
            scr[there, width_q : width_q + width_v] = partials[n][there, width_q : width_q + width_v]
            scr[there, width_q + width_v :] = partials[n][there, width_q + width_v :] + tn(
                spread, delta_v[here].astype(BF16)
            )
        for d in range(homes):
            home = me ^ d
            for s in range(steps):
                begin = pl.multiple_of(s * rows + home * home_rows, home_rows)
                late_outs[n * homes + d][s * home_rows : (s + 1) * home_rows, :] = scr[
                    pl.ds(begin, home_rows), :
                ].astype(BF16)


def facts_body(home_rows, homes, cap, resident, head_dim, steps, rr_ref, ra_ref, len_ref, where_ref, cos_ref, sin_ref, *places_out):
    _, owner_row, slot_row = row_facts(rr_ref[...], ra_ref[...], home_rows, resident)
    length_row, _, _ = row_facts(rr_ref[...], len_ref[...], home_rows, resident)
    me = where_ref[0]
    local_rows = steps * home_rows
    rows = rr_ref.shape[1]
    row, batch = iota((local_rows, rows), 0), iota((local_rows, rows), 1)
    mine = batch == me * home_rows + row % home_rows
    length = jnp.sum(jnp.where(mine, length_row, 0.0), 1, keepdims=True)
    owner = jnp.sum(jnp.where(mine, owner_row, 0.0), 1, keepdims=True)
    slot = jnp.sum(jnp.where(mine, slot_row, 0.0), 1, keepdims=True)
    lane = iota((local_rows, head_dim), 1)
    step = iota((local_rows, head_dim), 0) // home_rows
    half = head_dim // 2
    entry = (lane % half).astype(F32)
    inverse_freq = jnp.exp(entry * (-2.0 * math.log(ROPE_BASE) / head_dim))
    angle = (length + step.astype(F32)) * inverse_freq
    cos_ref[...] = jnp.cos(angle)
    sin_ref[...] = jnp.where(lane < half, -1.0, 1.0) * jnp.sin(angle)
    for d, out in enumerate(places_out):
        place = iota((local_rows, steps * cap), 1)
        local = iota((local_rows, steps * cap), 0)
        out[...] = (
            (owner == (me ^ d).astype(F32))
            & (place // cap == local // home_rows)
            & (slot == (place % cap).astype(F32))
        ).astype(BF16)


def attend_body(home_rows, homes, steps, cache_head, early, where_ref, rr_ref, len_ref, cos_ref, sin_ref, kc_ref, vc_ref, *rest):
    chunks, rest = rest[:homes], rest[homes:]
    if early:
        places, rest = rest[:homes], rest[homes:]
        deltas, rest = rest[:homes], rest[homes:]
    out, q_scr, o_scr, d_scr = rest[-4:]
    local_rows = steps * home_rows
    head_dim = kc_ref.shape[3]
    cached = kc_ref.shape[2]
    heads = (chunks[0].shape[1] - 2 * head_dim) // head_dim
    width_q = heads * head_dim
    scale = 1.0 / math.sqrt(head_dim)
    cos, sin = cos_ref[...], sin_ref[...]

    def rope(v):
        return v * cos + pltpu.roll(v, head_dim // 2, 1) * sin

    def projected(begin, delta_begin):
        total = None
        for chunk in chunks:
            piece = chunk[:, begin : begin + head_dim].astype(F32)
            total = piece if total is None else total + piece
        if early and delta_begin is not None:
            delta = None
            for place, piece in zip(places, deltas):
                term = nn(place[...], piece[:, delta_begin : delta_begin + head_dim])
                delta = term if delta is None else delta + term
            total = total + delta
        return total

    key_new = rope(projected(width_q, None)).astype(BF16)
    value_new = projected(width_q + head_dim, width_q).astype(BF16)
    row, col = iota((local_rows, local_rows), 0), iota((local_rows, local_rows), 1)
    live = (row % home_rows == col % home_rows) & (col // home_rows <= row // home_rows)
    new_weights = []
    for n in range(heads):
        query = rope(projected(n * head_dim, n * head_dim)).astype(BF16)
        here = slice(n * local_rows, (n + 1) * local_rows)
        q_scr[here, :] = query.astype(F32)
        weight = jnp.where(live, jnp.exp(nt(query, key_new) * scale), 0.0)
        new_weights.append(weight)
        d_scr[here, :] = jnp.broadcast_to(jnp.sum(weight, 1, keepdims=True), (local_rows, head_dim))
    queries_row = heads * steps
    spot = iota((queries_row, cached), 1)
    for b in range(home_rows):
        length = len_ref[0, rr_ref[0, where_ref[0] * home_rows + b]]
        strided = pl.ds(b, queries_row, stride=home_rows)
        query = q_scr[strided, :].astype(BF16)
        weight = jnp.where(spot < length, jnp.exp(nt(query, kc_ref[b, 0]) * scale), 0.0)
        total = jnp.sum(weight, 1, keepdims=True) + d_scr[strided, :][:, :1]
        d_scr[strided, :] = jnp.broadcast_to(total, (queries_row, head_dim))
        o_scr[strided, :] = nn((weight / total).astype(BF16), vc_ref[b, 0])
    for n in range(heads):
        here = slice(n * local_rows, (n + 1) * local_rows)
        probs = (new_weights[n] / d_scr[here, :local_rows]).astype(BF16)
        out[:, n * head_dim : (n + 1) * head_dim] = (o_scr[here, :] + nn(probs, value_new)).astype(BF16)


def on_device(
    hidden,
    query_weight,
    key_weight,
    value_weight,
    key_cache_rows,
    value_cache_rows,
    adapter_down_weight,
    adapter_up_query,
    adapter_up_value,
    request_adapter,
    row_request,
    lengths,
):
    homes = lax.axis_size("pool")
    features = lax.axis_size(FEATURE_AXES)
    home_rows, kv_here, cached, head_dim = key_cache_rows.shape
    rows, steps, slice_width = hidden.shape
    resident = adapter_down_weight.shape[0]
    rank = adapter_up_query.shape[1]
    q_cols = query_weight.shape[1] // kv_here
    cap = max(2, 2 * home_rows // homes)
    places = homes * cap
    fold = homes // features
    local_rows = steps * home_rows
    width = q_cols + 2 * head_dim
    shape = jax.ShapeDtypeStruct

    pool_here = lax.axis_index("pool")
    feature_here = lax.axis_index(FEATURE_AXES)
    tuned = homes == len(CARRIER) and features == len(CARRIER)
    if tuned:
        targets = [[CARRIER[q].index(g) for g in range(features)] for q in range(homes)]
        target = sum(
            jnp.where((pool_here == q) & (feature_here == g), targets[q][g], 0)
            for q in range(homes)
            for g in range(features)
        )
        owners = [target]
        perms = [[(q * features + g, targets[q][g] * features + q) for q in range(homes) for g in range(features)]]
    else:
        owners = [feature_here * fold + (i + pool_here) % fold for i in range(fold)]
        perms = [
            [
                (q * features + g, (g * fold + (i + q) % fold) * features + q // fold)
                for q in range(homes)
                for g in range(features)
            ]
            for i in range(fold)
        ]
    where = jnp.stack([pool_here, *owners]).astype(jnp.int32)
    rr, ra, ln = row_request.reshape(1, rows), request_adapter.reshape(1, rows), lengths.reshape(1, rows)
    by_step = hidden.transpose(1, 0, 2)
    x = by_step.reshape(steps * rows, slice_width)
    early = tuple(range(kv_here // 2))
    late = tuple(range(kv_here // 2, kv_here))

    selected = call(
        functools.partial(select_body, home_rows, cap, resident, len(owners)),
        [shape((steps * places, slice_width), BF16)] * fold,
        (rr, ra, where, by_step),
        in_specs=[VMEM, VMEM, SMEM, VMEM],
        flops=2 * steps * places * rows * slice_width,
        bytes_=2 * steps * (rows + places) * slice_width,
    )
    sent = [lax.ppermute(s, ("pool", *FEATURE_AXES), perm) for s, perm in zip(selected, perms)]

    tile = min(256, q_cols)
    tiles = q_cols // tile

    def project(h, emit_chunks):
        out_shape = (
            [shape((local_rows, width), BF16)] * homes if emit_chunks else [shape((steps * rows, width), F32)]
        )
        return call(
            functools.partial(project_body, home_rows, homes, emit_chunks),
            out_shape,
            (where, x, query_weight, key_weight, value_weight),
            in_specs=[
                SMEM,
                pl.BlockSpec((steps * rows, slice_width), lambda i: (0, 0)),
                pl.BlockSpec((slice_width, tile), lambda i: (0, h * tiles + i)),
                pl.BlockSpec((slice_width, head_dim), lambda i: (0, h)),
                pl.BlockSpec((slice_width, head_dim), lambda i: (0, h)),
            ],
            out_specs=[pl.BlockSpec(s.shape, lambda i: (0, 0)) for s in out_shape],
            grid=(tiles,),
            scratch=[pltpu.VMEM((steps * rows, tile), F32), pltpu.VMEM((steps * rows, 2 * head_dim), F32)]
            if emit_chunks
            else [],
            flops=2 * steps * rows * slice_width * width,
            bytes_=2 * slice_width * width,
        )

    def to_home(pieces):
        return [pieces[0]] + [
            lax.ppermute(pieces[d], "pool", [(i, i ^ d) for i in range(homes)]) for d in range(1, homes)
        ]

    chunks = {}
    for h in early:
        chunks[h] = to_home(project(h, True))
    partials = [project(h, False)[0] for h in late]
    facts = call(
        functools.partial(facts_body, home_rows, homes, cap, resident, head_dim, steps),
        [shape((local_rows, head_dim), F32)] * 2 + [shape((local_rows, steps * cap), BF16)] * homes,
        (rr, ra, ln, where),
        in_specs=[VMEM, VMEM, VMEM, SMEM],
        flops=10**7,
        bytes_=10**5,
    )
    cos, sin, spots = facts[0], facts[1], facts[2:]

    share = call(
        functools.partial(shrink_body, home_rows, cap, resident, fold),
        shape((steps * places, 2 * rank), BF16),
        (rr, ra, where, adapter_down_weight, *sent),
        in_specs=[VMEM, VMEM, SMEM] + [VMEM] * (1 + fold),
        flops=4 * steps * places * rank * slice_width * fold * resident,
        bytes_=4 * resident * rank * slice_width * fold,
    )
    shares = [share] + [
        lax.ppermute(share, FEATURE_AXES, [(i, i ^ d) for i in range(features)]) for d in range(1, features)
    ]
    grown = call(
        functools.partial(expand_body, home_rows, homes, cap, resident, early, late),
        [shape((steps * cap, q_cols + head_dim), BF16)] * (homes * len(early))
        + [shape((local_rows, width), BF16)] * (homes * len(late)),
        (rr, ra, where, adapter_up_query, adapter_up_value, *shares, *partials),
        in_specs=[VMEM, VMEM, SMEM] + [VMEM] * (2 + len(shares) + len(partials)),
        scratch=[pltpu.VMEM((max(rows, places) * steps, width), F32)],
        flops=2 * steps * places * rank * resident * q_cols * kv_here,
        bytes_=2 * resident * rank * q_cols * kv_here,
    )
    deltas = {}
    for n, h in enumerate(early):
        deltas[h] = to_home(grown[n * homes : (n + 1) * homes])
    grown = grown[homes * len(early) :]
    for n, h in enumerate(late):
        chunks[h] = to_home(grown[n * homes : (n + 1) * homes])

    out = None
    for h in range(kv_here):
        is_early = h in early
        extra = (*spots, *deltas[h]) if is_early else ()
        args = (where, rr, ln, cos, sin, key_cache_rows, value_cache_rows, *chunks[h], *extra)
        cache_spec = pl.BlockSpec((home_rows, 1, cached, head_dim), lambda i: (0, h, 0, 0))
        in_specs = [SMEM, SMEM, SMEM, VMEM, VMEM, cache_spec, cache_spec] + [VMEM] * (len(chunks[h]) + len(extra))
        more = {}
        if out is not None:
            more["input_output_aliases"] = {len(args): 0}
            args = (*args, out)
            in_specs = in_specs + [pl.BlockSpec(memory_space=pl.ANY)]
        heads = q_cols // head_dim
        out = call(
            functools.partial(attend_body, home_rows, homes, steps, h, is_early),
            shape((local_rows, q_cols * kv_here), BF16),
            args,
            in_specs=in_specs,
            out_specs=pl.BlockSpec((local_rows, q_cols), lambda i, h=h: (0, h)),
            grid=(1,),
            scratch=[pltpu.VMEM((heads * local_rows, head_dim), F32)] * 3,
            flops=4 * local_rows * heads * cached * head_dim,
            bytes_=4 * home_rows * cached * head_dim,
            **more,
        )
    return out.reshape(steps, home_rows, q_cols * kv_here).transpose(1, 0, 2)


def solution(mesh):
    return jax.shard_map(
        on_device,
        mesh=mesh,
        in_specs=(
            P("groups", None, "pool"),
            P("pool", ("tp", "sub")),
            P("pool", ("tp", "sub")),
            P("pool", ("tp", "sub")),
            P(("groups", "pool"), ("tp", "sub"), None, None),
            P(("groups", "pool"), ("tp", "sub"), None, None),
            P(("groups", "pool"), None, ("tp", "sub")),
            P(("groups", "pool"), None, ("tp", "sub")),
            P(("groups", "pool"), None, ("tp", "sub")),
            P("groups"),
            P("groups"),
            P("groups"),
        ),
        out_specs=P(("groups", "pool"), None, ("tp", "sub")),
        check_vma=False,
    )
```

time: 200 us -> 74.6 us (0.37)
  waiting for transfers between devices: 54.2 us -> 7.12 us
  matrix products: 38.2 us -> 0 us
  Pallas kernels: 0 us -> 28 us
  starting transfers between devices: 52.8 us -> 34 us
  local copies, waits for them, and re-layouts: 21.4 us -> 4.92 us
  between operations: 13.5 us -> 0.15 us
  blocking collectives: 10.3 us -> 0 us
  other arithmetic: 7.84 us -> 0.07 us
    all_to_all x13 -> x0, waiting for transfers between devices: 54.1 us -> none  [the longest x3 18.3 us: project(): lax.all_to_all(hidden_part, 'pool', split_axis=0, concat_axis=2, tiled=True)]
    all_to_all x13 -> x0, starting transfers between devices: 52.8 us -> none  [the longest x3 14.4 us: project(): lax.all_to_all(hidden_part, 'pool', split_axis=0, concat_axis=2, tiled=True)]
    dot_general x25 -> x0, matrix products: 38.2 us -> none  [the longest x3 19.9 us: project(): jnp.einsum('rsd,dc->rsc', hidden_part, w_all, preferred_element_type=jnp....]
    ppermute x0 -> x13, starting transfers between devices: none -> 34 us  [the longest x9 19.2 us: to_home(): lax.ppermute(pieces[d], 'pool', [(i, i ^ d) for i in range(homes)])]
    pallas_call x0 -> x8, Pallas kernels: none -> 28 us  [call(): pl.pallas_call(body, out_shape=out_shape, in_specs=in_specs, out_specs=ou...]
    unnamed x34 -> x26, local copies, waits for them, and re-layouts: 15.5 us -> 4.92 us
    psum x1 -> x0, blocking collectives: 10.3 us -> none  [owner_work(): lax.psum(shrunk.astype(jnp.bfloat16), ('tp', 'sub')).astype(jnp.float32)]
    ppermute x0 -> x13, waiting for transfers between devices: none -> 7.12 us  [the longest x9 7.11 us: to_home(): lax.ppermute(pieces[d], 'pool', [(i, i ^ d) for i in range(homes)])]
  transfers between devices with their start and end apart: 16 -> 13, of which waited for: 10 -> 2; matrix products, arithmetic and copies ran while one was open for 23% -> 0% of each run, Pallas kernels for 0% -> 26%
where the time goes in v1:
time: 74.6 us; the launch traced here: 74.2 us
  starting transfers between devices  34 us (46%)
  Pallas kernels  28 us (38%)
  waiting for transfers between devices  7.12 us (10%)
  local copies, waits for them, and re-layouts  4.92 us (7%)
    pallas_call x8, Pallas kernels, call(): pl.pallas_call(body, out_shape=out_shape, in_specs=in_specs, out_specs=ou...  28 us
    ppermute x9, starting transfers between devices, to_home(): lax.ppermute(pieces[d], 'pool', [(i, i ^ d) for i in range(homes)])  19.2 us
    ppermute x3, starting transfers between devices, on_device(): lax.ppermute(share, FEATURE_AXES, [(i, i ^ d) for i in range(features)])  14.1 us
    ppermute x9, waiting for transfers between devices, to_home(): lax.ppermute(pieces[d], 'pool', [(i, i ^ d) for i in range(homes)])  7.11 us
    unnamed x26, local copies, waits for them, and re-layouts  4.92 us
  transfers between devices with their start and end apart: 13, of which 2 were waited for; matrix products, arithmetic and copies ran while one was open for 0% of the time, Pallas kernels for 26%

profile of v1, /device:TPU:0, one launch (start us, length us, event | category | flops | bytes accessed | tf_op | source)
XLA Modules:
  0.0 74.2 jit_solution(8660296087673134047)
XLA Ops:
  0.0 0.1 pad_add_fusion.where_ref
  0.1 1.1 %copy-done.2 = bf16[64,3,2048]{2,0,1:T(8,128)(2,1)S(1)} copy-done((bf16[64,3,2048]{2,0,1:T(8,128)(2,1)S(1)}, bf16[64,3,2048]{2,0,1:T(8,128)(2,1)}, u32[]{:S(2)}) %copy-start.2) | copy-done | bytes 786456
  1.2 0.7 copy-done.9
  1.9 0.7 copy-done.10
  2.5 1.0 %shard_map.119 = bf16[96,2048]{1,0:T(8,128)(2,1)S(1)} custom-call(s32[1,64]{1,0:T(1,128)S(1)} %bitcast.14, s32[1,64]{1,0:T(1,128)S(1)} %bitcast.20, s32[2]{0:T(128)S(1)} %pad_add_fusion.where_ref, bf16[3,64,2048]{2,1,0:T(8,128)(2,1)S(1)} %bitcast.11), custom_call_target="tpu_custom_call" | custom-call | flops 25165824 | bytes 1179648 | tf_op jit(solution)/shard_map/pallas_call | solution.py:26
  3.5 0.7 collective-permute-start
  4.2 0.0 collective-permute-done.rest_0_
  4.2 0.0 copy-start.6
  4.2 1.2 %copy-done.6 = bf16[2,128,2048]{2,1,0:T(8,128)(2,1)S(1)} copy-done((bf16[2,128,2048]{2,1,0:T(8,128)(2,1)S(1)}, bf16[2,128,2048]{2,1,0:T(8,128)(2,1)}, u32[]{:S(2)}) %copy-start.6) | copy-done | bytes 1048600
  5.4 1.0 %shard_map.120.rest_0_ = bf16[96,128]{1,0:T(8,128)(2,1)S(1)} custom-call(s32[1,64]{1,0:T(1,128)S(1)} %bitcast.15, s32[1,64]{1,0:T(1,128)S(1)} %bitcast.21, s32[2]{0:T(128)S(1)} %pad_add_fusion.where_ref, bf16[2,128,2048]{2,1,0:T(8,128)(2,1)S(1)} %copy-done.6, bf16[96,2048]{1,0:T(8,128)(2,1)S(1)} %collective-permute-done.rest_0_), custom_call_target="tpu_custom_call" | custom-call | flops 100663296 | bytes 1048576 | tf_op jit(solution)/shard_map/pallas_call | solution.py:26
  6.5 12.1 %collective-permute-start.1 = (bf16[96,128]{1,0:T(8,128)(2,1)S(1)}, bf16[96,128]{1,0:T(8,128)(2,1)S(1)}, u32[]{:S(2)}, u32[]{:S(2)}) collective-permute-start(bf16[96,128]{1,0:T(8,128)(2,1)S(1)} %shard_map.120.rest_0_), channel_id=1, source_target_pairs={{0,1},{1,0},{2,3},{3,2},{4,5},{5,4},{6,7},{7,6},{8,9},{9,8},{10,11... | collective-permute-start | bytes 73736 | tf_op jit(solution)/shard_map/ppermute | solution.py:432
  18.6 1.2 %copy-done.5 = bf16[2048,256]{1,0:T(8,128)(2,1)S(1)} copy-done((bf16[2048,256]{1,0:T(8,128)(2,1)S(1)}, bf16[2048,256]{1,0:T(8,128)(2,1)}, u32[]{:S(2)}) %copy-start.5) | copy-done | bytes 1048600
  19.8 4.4 %shard_map.123 = (bf16[48,1280]{1,0:T(8,128)(2,1)S(1)}, bf16[48,1280]{1,0:T(8,128)(2,1)S(1)}, bf16[48,1280]{1,0:T(8,128)(2,1)S(1)}, bf16[48,1280]{1,0:T(8,128)(2,1)S(1)}) custom-call(s32[2]{0:T(128)S(1)} %pad_add_fusion.where_ref, bf16[192,2048]{1,0:T(8,128)(2,1)S(1)} %bitcast.12, bf16[2048,2048]{1,0:T(8,128)(2,1)} %q_ref.3, ...), custom_call_target="tpu_custom_call" | custom-call | flops 1006632960 | bytes 5242880 | tf_op jit(solution)/shard_map/pallas_call | solution.py:26
  24.2 2.9 %collective-permute-start.7 = (bf16[48,1280]{1,0:T(8,128)(2,1)S(1)}, bf16[48,1280]{1,0:T(8,128)(2,1)S(1)}, u32[]{:S(2)}, u32[]{:S(2)}) collective-permute-start(bf16[48,1280]{1,0:T(8,128)(2,1)S(1)} %get-tuple-element.30), channel_id=1, source_target_pairs={{0,4},{4,0},{8,12},{12,8},{1,5},{5,1},{9,13},{13,9},{2,6},{6,2},{1... | collective-permute-start | bytes 368648 | tf_op jit(solution)/shard_map/ppermute | solution.py:406
  27.1 4.4 %collective-permute-start.8 = (bf16[48,1280]{1,0:T(8,128)(2,1)S(1)}, bf16[48,1280]{1,0:T(8,128)(2,1)S(1)}, u32[]{:S(2)}, u32[]{:S(2)}) collective-permute-start(bf16[48,1280]{1,0:T(8,128)(2,1)S(1)} %get-tuple-element.31), channel_id=1, source_target_pairs={{0,8},{4,12},{8,0},{12,4},{1,9},{5,13},{9,1},{13,5},{2,10},{6,14},... | collective-permute-start | bytes 368648 | tf_op jit(solution)/shard_map/ppermute | solution.py:406
  31.5 0.1 collective-permute-start.9
  31.6 2.0 %collective-permute-start.2 = (bf16[96,128]{1,0:T(8,128)(2,1)S(1)}, bf16[96,128]{1,0:T(8,128)(2,1)S(1)}, u32[]{:S(2)}, u32[]{:S(2)}) collective-permute-start(bf16[96,128]{1,0:T(8,128)(2,1)S(1)} %shard_map.120.rest_0_), channel_id=1, source_target_pairs={{0,2},{1,3},{2,0},{3,1},{4,6},{5,7},{6,4},{7,5},{8,10},{9,11},{10,... | collective-permute-start | bytes 73736 | tf_op jit(solution)/shard_map/ppermute | solution.py:432
  33.6 0.0 copy-start.1
  33.6 4.5 %shard_map.121.rest_4_ = f32[192,1280]{1,0:T(8,128)S(1)} custom-call(s32[2]{0:T(128)S(1)} %pad_add_fusion.where_ref, bf16[192,2048]{1,0:T(8,128)(2,1)S(1)} %bitcast.13, bf16[2048,2048]{1,0:T(8,128)(2,1)} %q_ref.3, bf16[2048,256]{1,0:T(8,128)(2,1)S(1)} %copy-done.4, bf16[2048,256]{1,0:T(8,128)(2,1)S(1)} %copy-done.5), custom_call_target="tpu_custom_call" | custom-call | flops 1006632960 | bytes 5242880 | tf_op jit(solution)/shard_map/pallas_call | solution.py:26
  38.2 0.0 collective-permute-done.3.rest_3_
  38.2 1.6 %shard_map.122 = (bf16[24,1152]{1,0:T(8,128)(2,1)S(1)}, bf16[24,1152]{1,0:T(8,128)(2,1)S(1)}, bf16[24,1152]{1,0:T(8,128)(2,1)S(1)}, bf16[24,1152]{1,0:T(8,128)(2...) custom-call(s32[1,64]{1,0:T(1,128)S(1)} %bitcast.16, ...), custom_call_target="tpu_custom_call" | custom-call | flops 50331648 | bytes 524288 | tf_op jit(solution)/shard_map/pallas_call | solution.py:26
  39.8 0.6 collective-permute-start.4
  40.3 3.8 %collective-permute-start.5 = (bf16[48,1280]{1,0:T(8,128)(2,1)S(1)}, bf16[48,1280]{1,0:T(8,128)(2,1)S(1)}, u32[]{:S(2)}, u32[]{:S(2)}) collective-permute-start(bf16[48,1280]{1,0:T(8,128)(2,1)S(1)} %get-tuple-element.27), channel_id=1, source_target_pairs={{0,8},{4,12},{8,0},{12,4},{1,9},{5,13},{9,1},{13,5},{2,10},{6,14},... | collective-permute-start | bytes 368648 | tf_op jit(solution)/shard_map/ppermute | solution.py:406
  44.2 0.1 collective-permute-start.6
  44.2 0.5 collective-permute-start.10
  44.7 3.8 %collective-permute-start.11 = (bf16[24,1152]{1,0:T(8,128)(2,1)S(1)}, bf16[24,1152]{1,0:T(8,128)(2,1)S(1)}, u32[]{:S(2)}, u32[]{:S(2)}) collective-permute-start(bf16[24,1152]{1,0:T(8,128)(2,1)S(1)} %get-tuple-element.39), channel_id=1, source_target_pairs={{0,8},{4,12},{8,0},{12,4},{1,9},{5,13},{9,1},{13,5},{2,10},{6,14},... | collective-permute-start | bytes 165896 | tf_op jit(solution)/shard_map/ppermute | solution.py:406
  48.6 2.7 %collective-permute-done.10.rest_9_ = bf16[24,1152]{1,0:T(8,128)(2,1)S(1)} collective-permute-done((bf16[24,1152]{1,0:T(8,128)(2,1)S(1)}, bf16[24,1152]{1,0:T(8,128)(2,1)S(1)}, u32[]{:S(2)}, u32[]{:S(2)}) %collective-permute-start.10) | collective-permute-done | bytes 55328 | tf_op jit(solution)/shard_map/ppermute | solution.py:406
  51.2 3.1 %collective-permute-start.12 = (bf16[24,1152]{1,0:T(8,128)(2,1)S(1)}, bf16[24,1152]{1,0:T(8,128)(2,1)S(1)}, u32[]{:S(2)}, u32[]{:S(2)}) collective-permute-start(bf16[24,1152]{1,0:T(8,128)(2,1)S(1)} %get-tuple-element.40), channel_id=1, source_target_pairs={{0,12},{4,8},{8,4},{12,0},{1,13},{5,9},{9,5},{13,1},{2,14},{6,10},... | collective-permute-start | bytes 165896 | tf_op jit(solution)/shard_map/ppermute | solution.py:406
  54.3 0.9 %shard_map.118 = (f32[48,128]{1,0:T(8,128)S(1)}, f32[48,128]{1,0:T(8,128)S(1)}, bf16[48,24]{1,0:T(8,128)(2,1)S(1)}, bf16[48,24]{1,0:T(8,128)(2,1)S(1)}, bf16[48,...) custom-call(s32[1,64]{1,0:T(1,128)S(1)} %bitcast.17, s32[1,64]{1,0:T(1,128)S(1)} %bitcast.23, s32[1,64]{1,0:T(1,128)S(1)} %bitcast.24, ...), custom_call_target="tpu_custom_call" | custom-call | flops 10000000 | bytes 100000 | tf_op jit(solution)/shard_map/pallas_call | solution.py:26
  55.2 4.4 %collective-permute-done.11.rest_10_ = bf16[24,1152]{1,0:T(8,128)(2,1)S(1)} collective-permute-done((bf16[24,1152]{1,0:T(8,128)(2,1)S(1)}, bf16[24,1152]{1,0:T(8,128)(2,1)S(1)}, u32[]{:S(2)}, u32[]{:S(2)}) %collective-permute-start.11) | collective-permute-done | bytes 55328 | tf_op jit(solution)/shard_map/ppermute | solution.py:406
  59.6 8.1 %shard_map.124.rest_4_ = bf16[48,2048]{1,0:T(8,128)(2,1)} custom-call(s32[2]{0:T(128)S(1)} %pad_add_fusion.where_ref, s32[1,64]{1,0:T(1,128)S(1)} %bitcast.18, s32[1,64]{1,0:T(1,128)S(1)} %bitcast.25, f32[48,128]{1,0:T(8,128)S(1)} %get-tuple-element.23.cos_ref, f32[48,128]{1,0:T(8,128)S(1)} %get-tuple-element.24.sin_ref, ...), custom_call_target="tpu_custom_call" | custom-call | flops 50331648 | bytes 2097152 | tf_op jit(solution)/shard_map/pallas_call | solution.py:26
  67.7 6.5 %shard_map.125 = bf16[48,2048]{1,0:T(8,128)(2,1)} custom-call(s32[2]{0:T(128)S(1)} %pad_add_fusion.where_ref, s32[1,64]{1,0:T(1,128)S(1)} %bitcast.19, s32[1,64]{1,0:T(1,128)S(1)} %bitcast.26, f32[48,128]{1,0:T(8,128)S(1)} %get-tuple-element.23.cos_ref, f32[48,128]{1,0:T(8,128)S(1)} %get-tuple-element.24.sin_ref, ...), custom_call_target="tpu_custom_call", output_to_operand_aliasing={{}: (11, {})} | custom-call | flops 50331648 | bytes 2097152 | tf_op jit(solution)/shard_map/pallas_call | solution.py:26
  (29 shorter events, 0.1 us)
Async XLA Ops:
  0.1 1.1 %copy-start.2 = (bf16[64,3,2048]{2,0,1:T(8,128)(2,1)S(1)}, bf16[64,3,2048]{2,0,1:T(8,128)(2,1)}, u32[]{:S(2)}) copy-start(bf16[64,3,2048]{2,0,1:T(8,128)(2,1)} %param.12) | copy-start | bytes 2359300
  1.2 0.7 copy-start.9
  1.9 0.7 copy-start.10
  2.5 16.1 %copy-start.3 = (bf16[64,3,2048]{2,0,1:T(8,128)(2,1)S(1)}, bf16[64,3,2048]{2,0,1:T(8,128)(2,1)}, u32[]{:S(2)}) copy-start(bf16[64,3,2048]{2,0,1:T(8,128)(2,1)} %param.12) | copy-start | bytes 2359300
  2.5 16.1 %copy-start.4 = (bf16[2048,256]{1,0:T(8,128)(2,1)S(1)}, bf16[2048,256]{1,0:T(8,128)(2,1)}, u32[]{:S(2)}) copy-start(bf16[2048,256]{1,0:T(8,128)(2,1)} %k_ref.3) | copy-start | bytes 3145732
  3.5 0.7 collective-permute-start
  4.2 1.2 %copy-start.6 = (bf16[2,128,2048]{2,1,0:T(8,128)(2,1)S(1)}, bf16[2,128,2048]{2,1,0:T(8,128)(2,1)}, u32[]{:S(2)}) copy-start(bf16[2,128,2048]{2,1,0:T(8,128)(2,1)} %down_ref.1) | copy-start | bytes 3145732
  6.5 27.2 %collective-permute-start.1 = (bf16[96,128]{1,0:T(8,128)(2,1)S(1)}, bf16[96,128]{1,0:T(8,128)(2,1)S(1)}, u32[]{:S(2)}, u32[]{:S(2)}) collective-permute-start(bf16[96,128]{1,0:T(8,128)(2,1)S(1)} %shard_map.120.rest_0_), channel_id=1, source_target_pairs={{0,1},{1,0},{2,3},{3,2},{4,5},{5,4},{6,7},{7,6},{8,9},{9,8},{10,11... | collective-permute-start | bytes 73736 | tf_op jit(solution)/shard_map/ppermute | solution.py:432
  18.6 1.2 %copy-start.5 = (bf16[2048,256]{1,0:T(8,128)(2,1)S(1)}, bf16[2048,256]{1,0:T(8,128)(2,1)}, u32[]{:S(2)}) copy-start(bf16[2048,256]{1,0:T(8,128)(2,1)} %v_ref.3) | copy-start | bytes 3145732
  24.2 19.9 %collective-permute-start.7 = (bf16[48,1280]{1,0:T(8,128)(2,1)S(1)}, bf16[48,1280]{1,0:T(8,128)(2,1)S(1)}, u32[]{:S(2)}, u32[]{:S(2)}) collective-permute-start(bf16[48,1280]{1,0:T(8,128)(2,1)S(1)} %get-tuple-element.30), channel_id=1, source_target_pairs={{0,4},{4,0},{8,12},{12,8},{1,5},{5,1},{9,13},{13,9},{2,6},{6,2},{1... | collective-permute-start | bytes 368648 | tf_op jit(solution)/shard_map/ppermute | solution.py:406
  27.1 17.1 %collective-permute-start.8 = (bf16[48,1280]{1,0:T(8,128)(2,1)S(1)}, bf16[48,1280]{1,0:T(8,128)(2,1)S(1)}, u32[]{:S(2)}, u32[]{:S(2)}) collective-permute-start(bf16[48,1280]{1,0:T(8,128)(2,1)S(1)} %get-tuple-element.31), channel_id=1, source_target_pairs={{0,8},{4,12},{8,0},{12,4},{1,9},{5,13},{9,1},{13,5},{2,10},{6,14},... | collective-permute-start | bytes 368648 | tf_op jit(solution)/shard_map/ppermute | solution.py:406
  31.5 6.7 %copy-start.7 = (bf16[2,64,2048]{2,1,0:T(8,128)(2,1)S(1)}, bf16[2,64,2048]{2,1,0:T(8,128)(2,1)}, u32[]{:S(2)}) copy-start(bf16[2,64,2048]{2,1,0:T(8,128)(2,1)} %upq_ref.1) | copy-start | bytes 1572868
  31.5 6.7 %copy-start.8 = (bf16[2,64,256]{2,1,0:T(8,128)(2,1)S(1)}, bf16[2,64,256]{2,1,0:T(8,128)(2,1)}, u32[]{:S(2)}) copy-start(bf16[2,64,256]{2,1,0:T(8,128)(2,1)} %upv_ref.1) | copy-start | bytes 196612
  31.5 6.7 %copy-start.11 = (s32[64]{0:T(128)S(1)}, s32[64]{0:T(128)}, u32[]{:S(2)}) copy-start(s32[64]{0:T(128)} %param.21) | copy-start | bytes 772
  31.5 22.8 %copy-start.12 = (s32[64]{0:T(128)S(1)}, s32[64]{0:T(128)}, u32[]{:S(2)}) copy-start(s32[64]{0:T(128)} %param.23) | copy-start | bytes 772
  31.5 13.2 %collective-permute-start.9 = (bf16[48,1280]{1,0:T(8,128)(2,1)S(1)}, bf16[48,1280]{1,0:T(8,128)(2,1)S(1)}, u32[]{:S(2)}, u32[]{:S(2)}) collective-permute-start(bf16[48,1280]{1,0:T(8,128)(2,1)S(1)} %get-tuple-element.32), channel_id=1, source_target_pairs={{0,12},{4,8},{8,4},{12,0},{1,13},{5,9},{9,5},{13,1},{2,14},{6,10},... | collective-permute-start | bytes 368648 | tf_op jit(solution)/shard_map/ppermute | solution.py:406
  31.6 6.5 %collective-permute-start.2 = (bf16[96,128]{1,0:T(8,128)(2,1)S(1)}, bf16[96,128]{1,0:T(8,128)(2,1)S(1)}, u32[]{:S(2)}, u32[]{:S(2)}) collective-permute-start(bf16[96,128]{1,0:T(8,128)(2,1)S(1)} %shard_map.120.rest_0_), channel_id=1, source_target_pairs={{0,2},{1,3},{2,0},{3,1},{4,6},{5,7},{6,4},{7,5},{8,10},{9,11},{10,... | collective-permute-start | bytes 73736 | tf_op jit(solution)/shard_map/ppermute | solution.py:432
  33.6 4.6 %collective-permute-start.3 = (bf16[96,128]{1,0:T(8,128)(2,1)S(1)}, bf16[96,128]{1,0:T(8,128)(2,1)S(1)}, u32[]{:S(2)}, u32[]{:S(2)}) collective-permute-start(bf16[96,128]{1,0:T(8,128)(2,1)S(1)} %shard_map.120.rest_0_), channel_id=1, source_target_pairs={{0,3},{1,2},{2,1},{3,0},{4,7},{5,6},{6,5},{7,4},{8,11},{9,10},{10,... | collective-permute-start | bytes 73736 | tf_op jit(solution)/shard_map/ppermute | solution.py:432
  33.6 26.0 %copy-start = (bf16[16,2,256,128]{3,2,1,0:T(8,128)(2,1)S(1)}, bf16[16,2,256,128]{3,2,1,0:T(8,128)(2,1)}, u32[]{:S(2)}) copy-start(bf16[16,2,256,128]{3,2,1,0:T(8,128)(2,1)} %kc_ref.3) | copy-start | bytes 6291460
  33.6 26.0 %copy-start.1 = (bf16[16,2,256,128]{3,2,1,0:T(8,128)(2,1)S(1)}, bf16[16,2,256,128]{3,2,1,0:T(8,128)(2,1)}, u32[]{:S(2)}) copy-start(bf16[16,2,256,128]{3,2,1,0:T(8,128)(2,1)} %vc_ref.3) | copy-start | bytes 6291460
  39.8 27.9 %collective-permute-start.4 = (bf16[48,1280]{1,0:T(8,128)(2,1)S(1)}, bf16[48,1280]{1,0:T(8,128)(2,1)S(1)}, u32[]{:S(2)}, u32[]{:S(2)}) collective-permute-start(bf16[48,1280]{1,0:T(8,128)(2,1)S(1)} %get-tuple-element.26), channel_id=1, source_target_pairs={{0,4},{4,0},{8,12},{12,8},{1,5},{5,1},{9,13},{13,9},{2,6},{6,2},{1... | collective-permute-start | bytes 368648 | tf_op jit(solution)/shard_map/ppermute | solution.py:406
  40.3 27.4 %collective-permute-start.5 = (bf16[48,1280]{1,0:T(8,128)(2,1)S(1)}, bf16[48,1280]{1,0:T(8,128)(2,1)S(1)}, u32[]{:S(2)}, u32[]{:S(2)}) collective-permute-start(bf16[48,1280]{1,0:T(8,128)(2,1)S(1)} %get-tuple-element.27), channel_id=1, source_target_pairs={{0,8},{4,12},{8,0},{12,4},{1,9},{5,13},{9,1},{13,5},{2,10},{6,14},... | collective-permute-start | bytes 368648 | tf_op jit(solution)/shard_map/ppermute | solution.py:406
  44.2 23.6 %collective-permute-start.6 = (bf16[48,1280]{1,0:T(8,128)(2,1)S(1)}, bf16[48,1280]{1,0:T(8,128)(2,1)S(1)}, u32[]{:S(2)}, u32[]{:S(2)}) collective-permute-start(bf16[48,1280]{1,0:T(8,128)(2,1)S(1)} %get-tuple-element.28), channel_id=1, source_target_pairs={{0,12},{4,8},{8,4},{12,0},{1,13},{5,9},{9,5},{13,1},{2,14},{6,10},... | collective-permute-start | bytes 368648 | tf_op jit(solution)/shard_map/ppermute | solution.py:406
  44.2 7.0 %collective-permute-start.10 = (bf16[24,1152]{1,0:T(8,128)(2,1)S(1)}, bf16[24,1152]{1,0:T(8,128)(2,1)S(1)}, u32[]{:S(2)}, u32[]{:S(2)}) collective-permute-start(bf16[24,1152]{1,0:T(8,128)(2,1)S(1)} %get-tuple-element.38), channel_id=1, source_target_pairs={{0,4},{4,0},{8,12},{12,8},{1,5},{5,1},{9,13},{13,9},{2,6},{6,2},{1... | collective-permute-start | bytes 165896 | tf_op jit(solution)/shard_map/ppermute | solution.py:406
  44.7 14.9 %collective-permute-start.11 = (bf16[24,1152]{1,0:T(8,128)(2,1)S(1)}, bf16[24,1152]{1,0:T(8,128)(2,1)S(1)}, u32[]{:S(2)}, u32[]{:S(2)}) collective-permute-start(bf16[24,1152]{1,0:T(8,128)(2,1)S(1)} %get-tuple-element.39), channel_id=1, source_target_pairs={{0,8},{4,12},{8,0},{12,4},{1,9},{5,13},{9,1},{13,5},{2,10},{6,14},... | collective-permute-start | bytes 165896 | tf_op jit(solution)/shard_map/ppermute | solution.py:406
  51.2 8.4 %collective-permute-start.12 = (bf16[24,1152]{1,0:T(8,128)(2,1)S(1)}, bf16[24,1152]{1,0:T(8,128)(2,1)S(1)}, u32[]{:S(2)}, u32[]{:S(2)}) collective-permute-start(bf16[24,1152]{1,0:T(8,128)(2,1)S(1)} %get-tuple-element.40), channel_id=1, source_target_pairs={{0,12},{4,8},{8,4},{12,0},{1,13},{5,9},{9,5},{13,1},{2,14},{6,10},... | collective-permute-start | bytes 165896 | tf_op jit(solution)/shard_map/ppermute | solution.py:406

commit v2 on v1

--- a/solution.py
+++ b/solution.py
@@ -38,6 +38,8 @@
 
 VMEM = pl.BlockSpec(memory_space=pltpu.VMEM)
 SMEM = pl.BlockSpec(memory_space=pltpu.SMEM)
+HBM = pl.BlockSpec(memory_space=pltpu.HBM)
+ANY = pl.BlockSpec(memory_space=pl.ANY)
 
 
 def iota(shape, dim):
@@ -56,19 +58,21 @@
     return lax.dot_general(a, b, (((0,), (0,)), ((), ())), preferred_element_type=F32)
 
 
-def row_facts(row_request, request_values, home_rows, resident):
+def row_facts(row_request, request_adapter, lengths, home_rows, resident):
     rows = row_request.shape[1]
     across, down = iota((rows, rows), 1), iota((rows, rows), 0)
     eye = across == down
     request_col = jnp.sum(jnp.where(eye, row_request.astype(F32), 0.0), 1, keepdims=True)
     held = request_col == across.astype(F32)
-    adapter_col = jnp.sum(jnp.where(held, request_values.astype(F32), 0.0), 1, keepdims=True)
+    adapter_col = jnp.sum(jnp.where(held, request_adapter.astype(F32), 0.0), 1, keepdims=True)
+    length_col = jnp.sum(jnp.where(held, lengths.astype(F32), 0.0), 1, keepdims=True)
     adapter_row = jnp.sum(jnp.where(eye, adapter_col, 0.0), 0, keepdims=True)
+    length_row = jnp.sum(jnp.where(eye, length_col, 0.0), 0, keepdims=True)
     owner_col = jnp.floor((adapter_col + 0.5) / resident)
     owner_row = jnp.floor((adapter_row + 0.5) / resident)
     before = (owner_col == owner_row) & (down < across) & (down // home_rows == across // home_rows)
     slot_row = jnp.sum(jnp.where(before, 1.0, 0.0), 0, keepdims=True)
-    return adapter_row, owner_row, slot_row
+    return adapter_row, owner_row, slot_row, length_row
 
 
 def slot_table(owner_row, slot_row, owner, home_rows, cap):
@@ -82,29 +86,46 @@
     )
 
 
-def select_body(home_rows, cap, resident, owners_here, rr_ref, ra_ref, where_ref, hid_ref, *outs):
-    _, owner_row, slot_row = row_facts(rr_ref[...], ra_ref[...], home_rows, resident)
-    for i, out in enumerate(outs):
-        table = slot_table(owner_row, slot_row, where_ref[1 + i], home_rows, cap).astype(BF16)
+def select_body(home_rows, cap, resident, where_ref, rr_hbm, ra_hbm, ln_hbm, hid_hbm, *rest):
+    outs, rest = rest[:-6], rest[-6:]
+    facts_ref, rr_ref, ra_ref, ln_ref, hid_ref, sems = rest
+    copies = [
+        pltpu.make_async_copy(source, target, sems.at[n])
+        for n, (source, target) in enumerate(
+            ((rr_hbm, rr_ref), (ra_hbm, ra_ref), (ln_hbm, ln_ref), (hid_hbm, hid_ref))
+        )
+    ]
+    for copy in copies:
+        copy.start()
+    for copy in copies[:3]:
+        copy.wait()
+    adapter_row, owner_row, slot_row, length_row = row_facts(
+        rr_ref[...], ra_ref[...], ln_ref[...], home_rows, resident
+    )
+    facts_ref[...] = jnp.concatenate([adapter_row, owner_row, slot_row, length_row] * 2, 0)
+    tables = [
+        slot_table(owner_row, slot_row, where_ref[1 + i], home_rows, cap).astype(BF16) for i in range(len(outs))
+    ]
+    copies[3].wait()
+    for table, out in zip(tables, outs):
         places = table.shape[0]
         for s in range(hid_ref.shape[0]):
             out[s * places : (s + 1) * places] = nn(table, hid_ref[s]).astype(BF16)
 
 
-def project_body(home_rows, homes, emit_chunks, where_ref, x_ref, q_ref, k_ref, v_ref, *rest):
+def project_body(home_rows, homes, early, late, where_ref, x_ref, q_ref, k_ref, v_ref, *rest):
     steps, rows = x_ref.shape[0] // (homes * home_rows), homes * home_rows
     tile = q_ref.shape[1]
-    head_dim = k_ref.shape[1]
-    if emit_chunks:
-        outs, scr, scr_kv = rest[:homes], rest[homes], rest[homes + 1]
-    else:
-        (out,) = rest
+    kv_heads = len(early) + len(late)
+    head_dim = k_ref.shape[1] // kv_heads
+    chunks, rest = rest[: homes * len(early)], rest[homes * len(early) :]
+    whole, (scr, scr_kv) = rest[: len(late)], rest[len(late) :]
     i = pl.program_id(0)
-    columns = pl.ds(pl.multiple_of(i * tile, tile), tile)
-    product = nn(x_ref[...], q_ref[...])
-    q_cols = pl.num_programs(0) * tile
-
-    def put(value, source, where):
+    tiles = pl.num_programs(0) // kv_heads
+    q_cols = tiles * tile
+    columns = pl.ds(pl.multiple_of(lax.rem(i, tiles) * tile, tile), tile)
+
+    def put(value, source, outs, where):
         source[...] = value
         for d in range(homes):
             home = where_ref[0] ^ d
@@ -114,24 +135,34 @@
                     pl.ds(begin, home_rows), :
                 ].astype(BF16)
 
-    if emit_chunks:
-        put(product, scr, columns)
-    else:
-        out[:, columns] = product
+    for n, h in enumerate(early):
+
+        @pl.when(i // tiles == h)
+        def _(n=n):
+            put(nn(x_ref[...], q_ref[...]), scr, chunks[n * homes : (n + 1) * homes], columns)
+
+    for n, h in enumerate(late):
+
+        @pl.when(i // tiles == h)
+        def _(n=n):
+            whole[n][:, columns] = nn(x_ref[...], q_ref[...])
 
     @pl.when(i == 0)
     def _():
-        kv = jnp.concatenate([nn(x_ref[...], k_ref[...]), nn(x_ref[...], v_ref[...])], 1)
-        width = outs[0].shape[1] if emit_chunks else out.shape[1]
-        if emit_chunks:
-            put(kv, scr_kv, slice(width - 2 * head_dim, width))
-        else:
-            out[:, width - 2 * head_dim :] = kv
-
-
-def shrink_body(home_rows, cap, resident, parts, rr_ref, ra_ref, where_ref, down_ref, *rest):
-    sent, out = rest[:-1], rest[-1]
-    adapter_row, owner_row, slot_row = row_facts(rr_ref[...], ra_ref[...], home_rows, resident)
+        keys, values = nn(x_ref[...], k_ref[...]), nn(x_ref[...], v_ref[...])
+        for h in range(kv_heads):
+            here = slice(h * head_dim, (h + 1) * head_dim)
+            both = jnp.concatenate([keys[:, here], values[:, here]], 1)
+            if h in early:
+                n = early.index(h)
+                put(both, scr_kv, chunks[n * homes : (n + 1) * homes], slice(q_cols, q_cols + 2 * head_dim))
+            else:
+                whole[late.index(h)][:, q_cols:] = both
+
+
+def shrink_body(home_rows, cap, resident, parts, where_ref, facts_ref, down_ref, *rest):
+    sent, out = rest[:parts], rest[-1]
+    adapter_row, owner_row, slot_row = facts_ref[0:1], facts_ref[1:2], facts_ref[2:3]
     me = where_ref[0]
     table = slot_table(owner_row, slot_row, me, home_rows, cap)
     local = jnp.sum(jnp.where(table, adapter_row - (me * resident).astype(F32) + 1.0, 0.0), 1, keepdims=True) - 1.0
@@ -155,13 +186,13 @@
     out[...] = total.astype(BF16)
 
 
-def expand_body(home_rows, homes, cap, resident, early, late, rr_ref, ra_ref, where_ref, upq_ref, upv_ref, *rest):
+def expand_body(home_rows, homes, cap, resident, early, late, where_ref, facts_ref, upq_ref, upv_ref, *rest):
     n_parts = len(rest) - len(late) - homes * (len(early) + len(late)) - (1 if late else 0)
     shares, rest = rest[:n_parts], rest[n_parts:]
     partials, rest = rest[: len(late)], rest[len(late) :]
     early_outs, rest = rest[: homes * len(early)], rest[homes * len(early) :]
     late_outs, rest = rest[: homes * len(late)], rest[homes * len(late) :]
-    adapter_row, owner_row, slot_row = row_facts(rr_ref[...], ra_ref[...], home_rows, resident)
+    adapter_row, owner_row, slot_row = facts_ref[0:1], facts_ref[1:2], facts_ref[2:3]
     me = where_ref[0]
     table = slot_table(owner_row, slot_row, me, home_rows, cap)
     places, rows = table.shape
@@ -220,28 +251,26 @@
                 ].astype(BF16)
 
 
-def facts_body(home_rows, homes, cap, resident, head_dim, steps, rr_ref, ra_ref, len_ref, where_ref, cos_ref, sin_ref, *places_out):
-    _, owner_row, slot_row = row_facts(rr_ref[...], ra_ref[...], home_rows, resident)
-    length_row, _, _ = row_facts(rr_ref[...], len_ref[...], home_rows, resident)
+def home_body(home_rows, homes, cap, steps, where_ref, facts_ref, _, cos_ref, sin_ref, len_ref, *places_out):
+    owner_row, slot_row, length_row = facts_ref[1:2], facts_ref[2:3], facts_ref[3:4]
     me = where_ref[0]
-    local_rows = steps * home_rows
-    rows = rr_ref.shape[1]
+    local_rows, head_dim = cos_ref.shape
+    rows = facts_ref.shape[1]
     row, batch = iota((local_rows, rows), 0), iota((local_rows, rows), 1)
     mine = batch == me * home_rows + row % home_rows
     length = jnp.sum(jnp.where(mine, length_row, 0.0), 1, keepdims=True)
     owner = jnp.sum(jnp.where(mine, owner_row, 0.0), 1, keepdims=True)
     slot = jnp.sum(jnp.where(mine, slot_row, 0.0), 1, keepdims=True)
+    len_ref[...] = jnp.broadcast_to(length[:home_rows], len_ref.shape)
     lane = iota((local_rows, head_dim), 1)
     step = iota((local_rows, head_dim), 0) // home_rows
     half = head_dim // 2
-    entry = (lane % half).astype(F32)
-    inverse_freq = jnp.exp(entry * (-2.0 * math.log(ROPE_BASE) / head_dim))
+    inverse_freq = jnp.exp((lane % half).astype(F32) * (-2.0 * math.log(ROPE_BASE) / head_dim))
     angle = (length + step.astype(F32)) * inverse_freq
     cos_ref[...] = jnp.cos(angle)
     sin_ref[...] = jnp.where(lane < half, -1.0, 1.0) * jnp.sin(angle)
+    place, local = iota((local_rows, steps * cap), 1), iota((local_rows, steps * cap), 0)
     for d, out in enumerate(places_out):
-        place = iota((local_rows, steps * cap), 1)
-        local = iota((local_rows, steps * cap), 0)
         out[...] = (
             (owner == (me ^ d).astype(F32))
             & (place // cap == local // home_rows)
@@ -249,14 +278,13 @@
         ).astype(BF16)
 
 
-def attend_body(home_rows, homes, steps, cache_head, early, where_ref, rr_ref, len_ref, cos_ref, sin_ref, kc_ref, vc_ref, *rest):
+def attend_body(home_rows, homes, steps, h, early, cos_ref, sin_ref, len_ref, kc_ref, vc_ref, *rest):
     chunks, rest = rest[:homes], rest[homes:]
+    places = deltas = ()
     if early:
-        places, rest = rest[:homes], rest[homes:]
-        deltas, rest = rest[:homes], rest[homes:]
-    out, q_scr, o_scr, d_scr = rest[-4:]
-    local_rows = steps * home_rows
-    head_dim = kc_ref.shape[3]
+        places, deltas, rest = rest[:homes], rest[homes : 2 * homes], rest[2 * homes :]
+    done, (out, q_scr, new_scr, o_scr, total_scr) = rest[:-5], rest[-5:]
+    local_rows, head_dim = cos_ref.shape
     cached = kc_ref.shape[2]
     heads = (chunks[0].shape[1] - 2 * head_dim) // head_dim
     width_q = heads * head_dim
@@ -271,7 +299,7 @@
         for chunk in chunks:
             piece = chunk[:, begin : begin + head_dim].astype(F32)
             total = piece if total is None else total + piece
-        if early and delta_begin is not None:
+        if deltas and delta_begin is not None:
             delta = None
             for place, piece in zip(places, deltas):
                 term = nn(place[...], piece[:, delta_begin : delta_begin + head_dim])
@@ -290,21 +318,28 @@
         q_scr[here, :] = query.astype(F32)
         weight = jnp.where(live, jnp.exp(nt(query, key_new) * scale), 0.0)
         new_weights.append(weight)
-        d_scr[here, :] = jnp.broadcast_to(jnp.sum(weight, 1, keepdims=True), (local_rows, head_dim))
-    queries_row = heads * steps
-    spot = iota((queries_row, cached), 1)
+        new_scr[here, :] = jnp.broadcast_to(jnp.sum(weight, 1, keepdims=True), (local_rows, head_dim))
+    per_row = heads * steps
+    spot = iota((per_row, cached), 1).astype(F32)
+    mine = [pl.ds(b, per_row, stride=home_rows) for b in range(home_rows)]
+    scores = [nt(q_scr[mine[b], :].astype(BF16), kc_ref[b, h]) for b in range(home_rows)]
+    probs = []
     for b in range(home_rows):
-        length = len_ref[0, rr_ref[0, where_ref[0] * home_rows + b]]
-        strided = pl.ds(b, queries_row, stride=home_rows)
-        query = q_scr[strided, :].astype(BF16)
-        weight = jnp.where(spot < length, jnp.exp(nt(query, kc_ref[b, 0]) * scale), 0.0)
-        total = jnp.sum(weight, 1, keepdims=True) + d_scr[strided, :][:, :1]
-        d_scr[strided, :] = jnp.broadcast_to(total, (queries_row, head_dim))
-        o_scr[strided, :] = nn((weight / total).astype(BF16), vc_ref[b, 0])
+        weight = jnp.where(spot < len_ref[b : b + 1, :], jnp.exp(scores[b] * scale), 0.0)
+        total = jnp.sum(weight, 1, keepdims=True) + new_scr[mine[b], :][:, :1]
+        total_scr[mine[b], :] = jnp.broadcast_to(total, (per_row, head_dim))
+        probs.append((weight / total).astype(BF16))
+    for b in range(home_rows):
+        o_scr[mine[b], :] = nn(probs[b], vc_ref[b, h])
+    begin = out.shape[1] - width_q
     for n in range(heads):
         here = slice(n * local_rows, (n + 1) * local_rows)
-        probs = (new_weights[n] / d_scr[here, :local_rows]).astype(BF16)
-        out[:, n * head_dim : (n + 1) * head_dim] = (o_scr[here, :] + nn(probs, value_new)).astype(BF16)
+        prob = (new_weights[n] / total_scr[here, :local_rows]).astype(BF16)
+        out[:, begin + n * head_dim : begin + (n + 1) * head_dim] = (
+            o_scr[here, :] + nn(prob, value_new)
+        ).astype(BF16)
+    for n, piece in enumerate(done):
+        out[:, n * width_q : (n + 1) * width_q] = piece[...]
 
 
 def on_device(
@@ -364,11 +399,13 @@
     early = tuple(range(kv_here // 2))
     late = tuple(range(kv_here // 2, kv_here))
 
-    selected = call(
-        functools.partial(select_body, home_rows, cap, resident, len(owners)),
-        [shape((steps * places, slice_width), BF16)] * fold,
-        (rr, ra, where, by_step),
-        in_specs=[VMEM, VMEM, SMEM, VMEM],
+    *selected, facts = call(
+        functools.partial(select_body, home_rows, cap, resident),
+        [shape((steps * places, slice_width), BF16)] * fold + [shape((8, rows), F32)],
+        (where, rr, ra, ln, by_step),
+        in_specs=[SMEM] + [HBM] * 4,
+        scratch=[pltpu.VMEM((1, rows), jnp.int32)] * 3
+        + [pltpu.VMEM(by_step.shape, BF16), pltpu.SemaphoreType.DMA((4,))],
         flops=2 * steps * places * rows * slice_width,
         bytes_=2 * steps * (rows + places) * slice_width,
     )
@@ -376,55 +413,51 @@
 
     tile = min(256, q_cols)
     tiles = q_cols // tile
-
-    def project(h, emit_chunks):
-        out_shape = (
-            [shape((local_rows, width), BF16)] * homes if emit_chunks else [shape((steps * rows, width), F32)]
-        )
-        return call(
-            functools.partial(project_body, home_rows, homes, emit_chunks),
-            out_shape,
-            (where, x, query_weight, key_weight, value_weight),
-            in_specs=[
-                SMEM,
-                pl.BlockSpec((steps * rows, slice_width), lambda i: (0, 0)),
-                pl.BlockSpec((slice_width, tile), lambda i: (0, h * tiles + i)),
-                pl.BlockSpec((slice_width, head_dim), lambda i: (0, h)),
-                pl.BlockSpec((slice_width, head_dim), lambda i: (0, h)),
-            ],
-            out_specs=[pl.BlockSpec(s.shape, lambda i: (0, 0)) for s in out_shape],
-            grid=(tiles,),
-            scratch=[pltpu.VMEM((steps * rows, tile), F32), pltpu.VMEM((steps * rows, 2 * head_dim), F32)]
-            if emit_chunks
-            else [],
-            flops=2 * steps * rows * slice_width * width,
-            bytes_=2 * slice_width * width,
-        )
+    project_shape = [shape((local_rows, width), BF16)] * (homes * len(early)) + [
+        shape((steps * rows, width), F32)
+    ] * len(late)
+    projected = call(
+        functools.partial(project_body, home_rows, homes, early, late),
+        project_shape,
+        (where, x, query_weight, key_weight, value_weight),
+        in_specs=[
+            SMEM,
+            pl.BlockSpec(x.shape, lambda i: (0, 0)),
+            pl.BlockSpec((slice_width, tile), lambda i: (0, i)),
+            pl.BlockSpec(key_weight.shape, lambda i: (0, 0)),
+            pl.BlockSpec(value_weight.shape, lambda i: (0, 0)),
+        ],
+        out_specs=[pl.BlockSpec(s.shape, lambda i: (0, 0)) for s in project_shape],
+        grid=(tiles * kv_here,),
+        scratch=[pltpu.VMEM((steps * rows, tile), F32), pltpu.VMEM((steps * rows, 2 * head_dim), F32)],
+        flops=2 * steps * rows * slice_width * width * kv_here,
+        bytes_=2 * slice_width * width * kv_here,
+    )
+    partials = projected[homes * len(early) :]
 
     def to_home(pieces):
         return [pieces[0]] + [
             lax.ppermute(pieces[d], "pool", [(i, i ^ d) for i in range(homes)]) for d in range(1, homes)
         ]
 
-    chunks = {}
-    for h in early:
-        chunks[h] = to_home(project(h, True))
-    partials = [project(h, False)[0] for h in late]
-    facts = call(
-        functools.partial(facts_body, home_rows, homes, cap, resident, head_dim, steps),
-        [shape((local_rows, head_dim), F32)] * 2 + [shape((local_rows, steps * cap), BF16)] * homes,
-        (rr, ra, ln, where),
-        in_specs=[VMEM, VMEM, VMEM, SMEM],
+    chunks = {h: to_home(projected[n * homes : (n + 1) * homes]) for n, h in enumerate(early)}
+    tables = call(
+        functools.partial(home_body, home_rows, homes, cap, steps),
+        [shape((local_rows, head_dim), F32)] * 2
+        + [shape((home_rows, cached), F32)]
+        + [shape((local_rows, steps * cap), BF16)] * homes,
+        (where, facts, partials[0]),
+        in_specs=[SMEM, VMEM, ANY],
         flops=10**7,
         bytes_=10**5,
     )
-    cos, sin, spots = facts[0], facts[1], facts[2:]
+    cos, sin, length, spots = tables[0], tables[1], tables[2], tables[3:]
 
     share = call(
         functools.partial(shrink_body, home_rows, cap, resident, fold),
         shape((steps * places, 2 * rank), BF16),
-        (rr, ra, where, adapter_down_weight, *sent),
-        in_specs=[VMEM, VMEM, SMEM] + [VMEM] * (1 + fold),
+        (where, facts, adapter_down_weight, *sent, partials[0]),
+        in_specs=[SMEM] + [VMEM] * (2 + fold) + [ANY],
         flops=4 * steps * places * rank * slice_width * fold * resident,
         bytes_=4 * resident * rank * slice_width * fold,
     )
@@ -435,45 +468,34 @@
         functools.partial(expand_body, home_rows, homes, cap, resident, early, late),
         [shape((steps * cap, q_cols + head_dim), BF16)] * (homes * len(early))
         + [shape((local_rows, width), BF16)] * (homes * len(late)),
-        (rr, ra, where, adapter_up_query, adapter_up_value, *shares, *partials),
-        in_specs=[VMEM, VMEM, SMEM] + [VMEM] * (2 + len(shares) + len(partials)),
+        (where, facts, adapter_up_query, adapter_up_value, *shares, *partials),
+        in_specs=[SMEM] + [VMEM] * (3 + len(shares) + len(partials)),
         scratch=[pltpu.VMEM((max(rows, places) * steps, width), F32)],
         flops=2 * steps * places * rank * resident * q_cols * kv_here,
         bytes_=2 * resident * rank * q_cols * kv_here,
     )
-    deltas = {}
-    for n, h in enumerate(early):
-        deltas[h] = to_home(grown[n * homes : (n + 1) * homes])
+    deltas = {h: to_home(grown[n * homes : (n + 1) * homes]) for n, h in enumerate(early)}
     grown = grown[homes * len(early) :]
     for n, h in enumerate(late):
         chunks[h] = to_home(grown[n * homes : (n + 1) * homes])
 
-    out = None
+    heads = q_cols // head_dim
+    done = []
     for h in range(kv_here):
-        is_early = h in early
-        extra = (*spots, *deltas[h]) if is_early else ()
-        args = (where, rr, ln, cos, sin, key_cache_rows, value_cache_rows, *chunks[h], *extra)
-        cache_spec = pl.BlockSpec((home_rows, 1, cached, head_dim), lambda i: (0, h, 0, 0))
-        in_specs = [SMEM, SMEM, SMEM, VMEM, VMEM, cache_spec, cache_spec] + [VMEM] * (len(chunks[h]) + len(extra))
-        more = {}
-        if out is not None:
-            more["input_output_aliases"] = {len(args): 0}
-            args = (*args, out)
-            in_specs = in_specs + [pl.BlockSpec(memory_space=pl.ANY)]
-        heads = q_cols // head_dim
-        out = call(
-            functools.partial(attend_body, home_rows, homes, steps, h, is_early),
-            shape((local_rows, q_cols * kv_here), BF16),
-            args,
-            in_specs=in_specs,
-            out_specs=pl.BlockSpec((local_rows, q_cols), lambda i, h=h: (0, h)),
-            grid=(1,),
-            scratch=[pltpu.VMEM((heads * local_rows, head_dim), F32)] * 3,
-            flops=4 * local_rows * heads * cached * head_dim,
-            bytes_=4 * home_rows * cached * head_dim,
-            **more,
+        extra = (*spots, *deltas[h]) if h in early else ()
+        before = done if h == kv_here - 1 else []
+        args = (cos, sin, length, key_cache_rows, value_cache_rows, *chunks[h], *extra, *before)
+        done.append(
+            call(
+                functools.partial(attend_body, home_rows, homes, steps, h, h in early),
+                shape((local_rows, q_cols * (1 + len(before))), BF16),
+                args,
+                scratch=[pltpu.VMEM((heads * local_rows, head_dim), F32)] * 4,
+                flops=4 * local_rows * heads * cached * head_dim,
+                bytes_=4 * home_rows * cached * head_dim,
+            )
         )
-    return out.reshape(steps, home_rows, q_cols * kv_here).transpose(1, 0, 2)
+    return done[-1].reshape(steps, home_rows, q_cols * kv_here).transpose(1, 0, 2)
 
 
 def solution(mesh):

time: 74.6 us -> 57.1 us (0.77)
  starting transfers between devices: 34 us -> 20.8 us
  Pallas kernels: 28 us -> 16.6 us
  waiting for transfers between devices: 7.12 us -> 12.4 us
  local copies, waits for them, and re-layouts: 4.92 us -> 6.7 us
    pallas_call x8 -> x7, Pallas kernels: 28 us -> 16.6 us  [call(): pl.pallas_call(body, out_shape=out_shape, in_specs=in_specs, out_specs=ou...]
    ppermute x3, starting transfers between devices: 14.1 us -> 2.91 us  [on_device(): lax.ppermute(share, FEATURE_AXES, [(i, i ^ d) for i in range(features)])]
    ppermute x9, waiting for transfers between devices: 7.11 us -> 10.1 us  [to_home(): lax.ppermute(pieces[d], 'pool', [(i, i ^ d) for i in range(homes)])]
    ppermute x3, waiting for transfers between devices: 0.01 us -> 2.37 us  [on_device(): lax.ppermute(share, FEATURE_AXES, [(i, i ^ d) for i in range(features)])]
    ppermute x9, starting transfers between devices: 19.2 us -> 17.2 us  [to_home(): lax.ppermute(pieces[d], 'pool', [(i, i ^ d) for i in range(homes)])]
    unnamed x26 -> x24, local copies, waits for them, and re-layouts: 4.92 us -> 6.7 us
  transfers between devices with their start and end apart: 13 -> 13, of which waited for: 2 -> 4; matrix products, arithmetic and copies ran while one was open for 0% -> 0% of each run, Pallas kernels for 26% -> 24%
where the time goes in v2:
time: 57.1 us; the launch traced here: 56.7 us
  starting transfers between devices  20.8 us (36%)
  Pallas kernels  16.6 us (29%)
  waiting for transfers between devices  12.4 us (22%)
  local copies, waits for them, and re-layouts  6.7 us (12%)
    ppermute x9, starting transfers between devices, to_home(): lax.ppermute(pieces[d], 'pool', [(i, i ^ d) for i in range(homes)])  17.2 us
    pallas_call x7, Pallas kernels, call(): pl.pallas_call(body, out_shape=out_shape, in_specs=in_specs, out_specs=ou...  16.6 us
    ppermute x9, waiting for transfers between devices, to_home(): lax.ppermute(pieces[d], 'pool', [(i, i ^ d) for i in range(homes)])  10.1 us
    unnamed x24, local copies, waits for them, and re-layouts  6.7 us
    ppermute x3, starting transfers between devices, on_device(): lax.ppermute(share, FEATURE_AXES, [(i, i ^ d) for i in range(features)])  2.91 us
    ppermute x3, waiting for transfers between devices, on_device(): lax.ppermute(share, FEATURE_AXES, [(i, i ^ d) for i in range(features)])  2.37 us
  transfers between devices with their start and end apart: 13, of which 4 were waited for; matrix products, arithmetic and copies ran while one was open for 0% of the time, Pallas kernels for 24%

profile of v2, /device:TPU:0, one launch (start us, length us, event | category | flops | bytes accessed | tf_op | source)
XLA Modules:
  0.0 56.7 jit_solution(18183124287622862641)
XLA Ops:
  0.0 0.1 pad_add_fusion.where_ref
  0.1 1.1 %copy-done.2 = bf16[64,3,2048]{2,0,1:T(8,128)(2,1)S(1)} copy-done((bf16[64,3,2048]{2,0,1:T(8,128)(2,1)S(1)}, bf16[64,3,2048]{2,0,1:T(8,128)(2,1)}, u32[]{:S(2)}) %copy-start.2) | copy-done | bytes 786456
  1.2 0.7 %copy-done.9 = s32[64]{0:T(128)S(1)} copy-done((s32[64]{0:T(128)S(1)}, s32[64]{0:T(128)}, u32[]{:S(2)}) %copy-start.9) | copy-done | bytes 280
  1.9 0.7 %copy-done.10 = s32[64]{0:T(128)S(1)} copy-done((s32[64]{0:T(128)S(1)}, s32[64]{0:T(128)}, u32[]{:S(2)}) %copy-start.10) | copy-done | bytes 280
  2.5 0.7 %copy-done.11 = s32[64]{0:T(128)S(1)} copy-done((s32[64]{0:T(128)S(1)}, s32[64]{0:T(128)}, u32[]{:S(2)}) %copy-start.11) | copy-done | bytes 280
  3.2 1.1 %shard_map.118 = (bf16[96,2048]{1,0:T(8,128)(2,1)S(1)}, f32[8,64]{1,0:T(8,128)S(1)}) custom-call(s32[2]{0:T(128)S(1)} %pad_add_fusion.where_ref, s32[1,64]{1,0:T(1,128)S(1)} %bitcast.13, s32[1,64]{1,0:T(1,128)S(1)} %bitcast.14, s32[1,64]{1,0:T(1,128)S(1)} %bitcast.15, bf16[3,64,2048]{2,1,0:T(8,128)(2,1)S(1)} %bitcast.11), custom_call_target="tpu_custom_call" | custom-call | flops 25165824 | bytes 1179648 | tf_op jit(solution)/shard_map/pallas_call | solution.py:26
  4.3 0.7 %collective-permute-start = (bf16[96,2048]{1,0:T(8,128)(2,1)S(1)}, bf16[96,2048]{1,0:T(8,128)(2,1)S(1)}, u32[]{:S(2)}, u32[]{:S(2)}) collective-permute-start(bf16[96,2048]{1,0:T(8,128)(2,1)S(1)} %get-tuple-element.32), channel_id=1, source_target_pairs={{0,0},{1,12},{2,8},{3,4},{4,9},{5,5},{6,1},{7,13},{8,14},{9,6},{10... | collective-permute-start | bytes 1179656 | tf_op jit(solution)/shard_map/ppermute | solution.py:412
  5.0 0.0 copy-start.3
  5.0 1.1 %copy-done.3 = bf16[64,3,2048]{2,0,1:T(8,128)(2,1)S(1)} copy-done((bf16[64,3,2048]{2,0,1:T(8,128)(2,1)S(1)}, bf16[64,3,2048]{2,0,1:T(8,128)(2,1)}, u32[]{:S(2)}) %copy-start.3) | copy-done | bytes 786456
  6.1 1.2 %copy-done.5 = bf16[2048,256]{1,0:T(8,128)(2,1)S(1)} copy-done((bf16[2048,256]{1,0:T(8,128)(2,1)S(1)}, bf16[2048,256]{1,0:T(8,128)(2,1)}, u32[]{:S(2)}) %copy-start.5) | copy-done | bytes 1048600
  7.3 1.2 %copy-done.6 = bf16[2048,256]{1,0:T(8,128)(2,1)S(1)} copy-done((bf16[2048,256]{1,0:T(8,128)(2,1)S(1)}, bf16[2048,256]{1,0:T(8,128)(2,1)}, u32[]{:S(2)}) %copy-start.6) | copy-done | bytes 1048600
  8.6 8.0 %shard_map.119 = (bf16[48,1280]{1,0:T(8,128)(2,1)S(1)}, bf16[48,1280]{1,0:T(8,128)(2,1)S(1)}, bf16[48,1280]{1,0:T(8,128)(2,1)S(1)}, bf16[48,1280]{1,0:T(8,128)(2,1)S(1)}, f32[192,1280]{1,0:T(8,128)S(1)}) custom-call(s32[2]{0:T(128)S(1)} %pad_add_fusion.where_ref, bf16[192,2048]{1,0:T(8,128)(2,1)S(1)} %bitcast.12, bf16[2048,2048]{1,0:T(8,128)(2,1)} %q_ref.1, ...), custom_call_target="tpu_custom_call" | custom-call | flops 2013265920 | bytes 10485760 | tf_op jit(solution)/shard_map/pallas_call | solution.py:26
  16.6 5.3 %collective-permute-start.7 = (bf16[48,1280]{1,0:T(8,128)(2,1)S(1)}, bf16[48,1280]{1,0:T(8,128)(2,1)S(1)}, u32[]{:S(2)}, u32[]{:S(2)}) collective-permute-start(bf16[48,1280]{1,0:T(8,128)(2,1)S(1)} %get-tuple-element.38), channel_id=1, source_target_pairs={{0,4},{4,0},{8,12},{12,8},{1,5},{5,1},{9,13},{13,9},{2,6},{6,2},{1... | collective-permute-start | bytes 368648 | tf_op jit(solution)/shard_map/ppermute | solution.py:440
  21.9 2.6 %collective-permute-start.8 = (bf16[48,1280]{1,0:T(8,128)(2,1)S(1)}, bf16[48,1280]{1,0:T(8,128)(2,1)S(1)}, u32[]{:S(2)}, u32[]{:S(2)}) collective-permute-start(bf16[48,1280]{1,0:T(8,128)(2,1)S(1)} %get-tuple-element.39), channel_id=1, source_target_pairs={{0,8},{4,12},{8,0},{12,4},{1,9},{5,13},{9,1},{13,5},{2,10},{6,14},... | collective-permute-start | bytes 368648 | tf_op jit(solution)/shard_map/ppermute | solution.py:440
  24.5 1.4 %collective-permute-start.9 = (bf16[48,1280]{1,0:T(8,128)(2,1)S(1)}, bf16[48,1280]{1,0:T(8,128)(2,1)S(1)}, u32[]{:S(2)}, u32[]{:S(2)}) collective-permute-start(bf16[48,1280]{1,0:T(8,128)(2,1)S(1)} %get-tuple-element.40), channel_id=1, source_target_pairs={{0,12},{4,8},{8,4},{12,0},{1,13},{5,9},{9,5},{13,1},{2,14},{6,10},... | collective-permute-start | bytes 368648 | tf_op jit(solution)/shard_map/ppermute | solution.py:440
  25.9 1.0 %shard_map.121.rest_0_ = bf16[96,128]{1,0:T(8,128)(2,1)S(1)} custom-call(s32[2]{0:T(128)S(1)} %pad_add_fusion.where_ref, f32[8,64]{1,0:T(8,128)S(1)} %get-tuple-element.27.facts_ref, bf16[2,128,2048]{2,1,0:T(8,128)(2,1)S(1)} %copy-done.4, bf16[96,2048]{1,0:T(8,128)(2,1)S(1)} %collective-permute-done.rest_0_, f32[192,1280]{1,0:T(8,128)S(1)} %get-tuple-element.28._.rest_1_.rest_4_), custom_call_target="tpu_custom_call" | custom-call | flops 100663296 | bytes 1048576 | tf_op jit(solution)/shard_map/pallas_call | solution.py:26
  26.9 0.8 %collective-permute-start.1 = (bf16[96,128]{1,0:T(8,128)(2,1)S(1)}, bf16[96,128]{1,0:T(8,128)(2,1)S(1)}, u32[]{:S(2)}, u32[]{:S(2)}) collective-permute-start(bf16[96,128]{1,0:T(8,128)(2,1)S(1)} %shard_map.121.rest_0_), channel_id=1, source_target_pairs={{0,1},{1,0},{2,3},{3,2},{4,5},{5,4},{6,7},{7,6},{8,9},{9,8},{10,11... | collective-permute-start | bytes 73736 | tf_op jit(solution)/shard_map/ppermute | solution.py:465
  27.7 1.3 %collective-permute-start.2 = (bf16[96,128]{1,0:T(8,128)(2,1)S(1)}, bf16[96,128]{1,0:T(8,128)(2,1)S(1)}, u32[]{:S(2)}, u32[]{:S(2)}) collective-permute-start(bf16[96,128]{1,0:T(8,128)(2,1)S(1)} %shard_map.121.rest_0_), channel_id=1, source_target_pairs={{0,2},{1,3},{2,0},{3,1},{4,6},{5,7},{6,4},{7,5},{8,10},{9,11},{10,... | collective-permute-start | bytes 73736 | tf_op jit(solution)/shard_map/ppermute | solution.py:465
  28.9 0.9 %collective-permute-start.3 = (bf16[96,128]{1,0:T(8,128)(2,1)S(1)}, bf16[96,128]{1,0:T(8,128)(2,1)S(1)}, u32[]{:S(2)}, u32[]{:S(2)}) collective-permute-start(bf16[96,128]{1,0:T(8,128)(2,1)S(1)} %shard_map.121.rest_0_), channel_id=1, source_target_pairs={{0,3},{1,2},{2,1},{3,0},{4,7},{5,6},{6,5},{7,4},{8,11},{9,10},{10,... | collective-permute-start | bytes 73736 | tf_op jit(solution)/shard_map/ppermute | solution.py:465
  29.8 1.7 %collective-permute-done.2.rest_2_ = bf16[96,128]{1,0:T(8,128)(2,1)S(1)} collective-permute-done((bf16[96,128]{1,0:T(8,128)(2,1)S(1)}, bf16[96,128]{1,0:T(8,128)(2,1)S(1)}, u32[]{:S(2)}, u32[]{:S(2)}) %collective-permute-start.2) | collective-permute-done | bytes 24608 | tf_op jit(solution)/shard_map/ppermute | solution.py:465
  31.5 0.7 %collective-permute-done.3.rest_3_ = bf16[96,128]{1,0:T(8,128)(2,1)S(1)} collective-permute-done((bf16[96,128]{1,0:T(8,128)(2,1)S(1)}, bf16[96,128]{1,0:T(8,128)(2,1)S(1)}, u32[]{:S(2)}, u32[]{:S(2)}) %collective-permute-start.3) | collective-permute-done | bytes 24608 | tf_op jit(solution)/shard_map/ppermute | solution.py:465
  32.2 1.4 %shard_map.122 = (bf16[24,1152]{1,0:T(8,128)(2,1)S(1)}, bf16[24,1152]{1,0:T(8,128)(2,1)S(1)}, bf16[24,1152]{1,0:T(8,128)(2,1)S(1)}, bf16[24,1152]{1,0:T(8,128)(2...) custom-call(s32[2]{0:T(128)S(1)} %pad_add_fusion.where_ref, ...), custom_call_target="tpu_custom_call" | custom-call | flops 50331648 | bytes 524288 | tf_op jit(solution)/shard_map/pallas_call | solution.py:26
  33.6 0.1 collective-permute-start.4
  33.6 2.2 %collective-permute-start.5 = (bf16[48,1280]{1,0:T(8,128)(2,1)S(1)}, bf16[48,1280]{1,0:T(8,128)(2,1)S(1)}, u32[]{:S(2)}, u32[]{:S(2)}) collective-permute-start(bf16[48,1280]{1,0:T(8,128)(2,1)S(1)} %get-tuple-element.35), channel_id=1, source_target_pairs={{0,8},{4,12},{8,0},{12,4},{1,9},{5,13},{9,1},{13,5},{2,10},{6,14},... | collective-permute-start | bytes 368648 | tf_op jit(solution)/shard_map/ppermute | solution.py:440
  35.9 2.2 %collective-permute-start.6 = (bf16[48,1280]{1,0:T(8,128)(2,1)S(1)}, bf16[48,1280]{1,0:T(8,128)(2,1)S(1)}, u32[]{:S(2)}, u32[]{:S(2)}) collective-permute-start(bf16[48,1280]{1,0:T(8,128)(2,1)S(1)} %get-tuple-element.36), channel_id=1, source_target_pairs={{0,12},{4,8},{8,4},{12,0},{1,13},{5,9},{9,5},{13,1},{2,14},{6,10},... | collective-permute-start | bytes 368648 | tf_op jit(solution)/shard_map/ppermute | solution.py:440
  38.0 2.2 %collective-permute-start.11 = (bf16[24,1152]{1,0:T(8,128)(2,1)S(1)}, bf16[24,1152]{1,0:T(8,128)(2,1)S(1)}, u32[]{:S(2)}, u32[]{:S(2)}) collective-permute-start(bf16[24,1152]{1,0:T(8,128)(2,1)S(1)} %get-tuple-element.47), channel_id=1, source_target_pairs={{0,8},{4,12},{8,0},{12,4},{1,9},{5,13},{9,1},{13,5},{2,10},{6,14},... | collective-permute-start | bytes 165896 | tf_op jit(solution)/shard_map/ppermute | solution.py:440
  40.2 4.8 %collective-permute-done.10.rest_9_ = bf16[24,1152]{1,0:T(8,128)(2,1)S(1)} collective-permute-done((bf16[24,1152]{1,0:T(8,128)(2,1)S(1)}, bf16[24,1152]{1,0:T(8,128)(2,1)S(1)}, u32[]{:S(2)}, u32[]{:S(2)}) %collective-permute-start.10) | collective-permute-done | bytes 55328 | tf_op jit(solution)/shard_map/ppermute | solution.py:440
  45.1 1.2 %collective-permute-start.12 = (bf16[24,1152]{1,0:T(8,128)(2,1)S(1)}, bf16[24,1152]{1,0:T(8,128)(2,1)S(1)}, u32[]{:S(2)}, u32[]{:S(2)}) collective-permute-start(bf16[24,1152]{1,0:T(8,128)(2,1)S(1)} %get-tuple-element.48), channel_id=1, source_target_pairs={{0,12},{4,8},{8,4},{12,0},{1,13},{5,9},{9,5},{13,1},{2,14},{6,10},... | collective-permute-start | bytes 165896 | tf_op jit(solution)/shard_map/ppermute | solution.py:440
  46.3 0.7 %shard_map.120 = (f32[48,128]{1,0:T(8,128)S(1)}, f32[48,128]{1,0:T(8,128)S(1)}, f32[16,256]{1,0:T(8,128)S(1)}, bf16[48,24]{1,0:T(8,128)(2,1)S(1)}, bf16[48,24]{1...) custom-call(s32[2]{0:T(128)S(1)} %pad_add_fusion.where_ref, ...), custom_call_target="tpu_custom_call" | custom-call | flops 10000000 | bytes 100000 | tf_op jit(solution)/shard_map/pallas_call | solution.py:26
  47.1 5.2 %collective-permute-done.11.rest_10_ = bf16[24,1152]{1,0:T(8,128)(2,1)S(1)} collective-permute-done((bf16[24,1152]{1,0:T(8,128)(2,1)S(1)}, bf16[24,1152]{1,0:T(8,128)(2,1)S(1)}, u32[]{:S(2)}, u32[]{:S(2)}) %collective-permute-start.11) | collective-permute-done | bytes 55328 | tf_op jit(solution)/shard_map/ppermute | solution.py:440
  52.3 2.6 %shard_map.123.rest_4_ = bf16[48,1024]{1,0:T(8,128)(2,1)S(1)} custom-call(f32[48,128]{1,0:T(8,128)S(1)} %get-tuple-element.29.cos_ref, f32[48,128]{1,0:T(8,128)S(1)} %get-tuple-element.30.sin_ref, f32[16,256]{1,0:T(8,128)S(1)} %get-tuple-element.31.len_ref, bf16[16,2,256,128]{3,2,1,0:T(8,128)(2,1)S(1)} %copy-done, bf16[16,2,256,128]{3,2,1,0:T(8,128)(2,1)S(1)} %copy-done.1, ...), custom_call_target="tpu_custom_call" | custom-call | flops 50331648 | bytes 2097152 | tf_op jit(solution)/shard_map/pallas_call | solution.py:26
  54.9 1.8 %shard_map.124 = bf16[48,2048]{1,0:T(8,128)(2,1)} custom-call(f32[48,128]{1,0:T(8,128)S(1)} %get-tuple-element.29.cos_ref, f32[48,128]{1,0:T(8,128)S(1)} %get-tuple-element.30.sin_ref, f32[16,256]{1,0:T(8,128)S(1)} %get-tuple-element.31.len_ref, bf16[16,2,256,128]{3,2,1,0:T(8,128)(2,1)S(1)} %copy-done, bf16[16,2,256,128]{3,2,1,0:T(8,128)(2,1)S(1)} %copy-done.1, ...), custom_call_target="tpu_custom_call" | custom-call | flops 50331648 | bytes 2097152 | tf_op jit(solution)/shard_map/pallas_call | solution.py:26
  (26 shorter events, 0.1 us)
Async XLA Ops:
  0.1 1.1 %copy-start.2 = (bf16[64,3,2048]{2,0,1:T(8,128)(2,1)S(1)}, bf16[64,3,2048]{2,0,1:T(8,128)(2,1)}, u32[]{:S(2)}) copy-start(bf16[64,3,2048]{2,0,1:T(8,128)(2,1)} %param.12) | copy-start | bytes 2359300
  1.2 0.7 %copy-start.9 = (s32[64]{0:T(128)S(1)}, s32[64]{0:T(128)}, u32[]{:S(2)}) copy-start(s32[64]{0:T(128)} %param.22) | copy-start | bytes 772
  1.9 0.7 %copy-start.10 = (s32[64]{0:T(128)S(1)}, s32[64]{0:T(128)}, u32[]{:S(2)}) copy-start(s32[64]{0:T(128)} %param.21) | copy-start | bytes 772
  2.5 0.7 %copy-start.11 = (s32[64]{0:T(128)S(1)}, s32[64]{0:T(128)}, u32[]{:S(2)}) copy-start(s32[64]{0:T(128)} %param.23) | copy-start | bytes 772
  4.3 21.6 %collective-permute-start = (bf16[96,2048]{1,0:T(8,128)(2,1)S(1)}, bf16[96,2048]{1,0:T(8,128)(2,1)S(1)}, u32[]{:S(2)}, u32[]{:S(2)}) collective-permute-start(bf16[96,2048]{1,0:T(8,128)(2,1)S(1)} %get-tuple-element.32), channel_id=1, source_target_pairs={{0,0},{1,12},{2,8},{3,4},{4,9},{5,5},{6,1},{7,13},{8,14},{9,6},{10... | collective-permute-start | bytes 1179656 | tf_op jit(solution)/shard_map/ppermute | solution.py:412
  5.0 1.1 %copy-start.3 = (bf16[64,3,2048]{2,0,1:T(8,128)(2,1)S(1)}, bf16[64,3,2048]{2,0,1:T(8,128)(2,1)}, u32[]{:S(2)}) copy-start(bf16[64,3,2048]{2,0,1:T(8,128)(2,1)} %param.12) | copy-start | bytes 2359300
  6.1 1.2 %copy-start.5 = (bf16[2048,256]{1,0:T(8,128)(2,1)S(1)}, bf16[2048,256]{1,0:T(8,128)(2,1)}, u32[]{:S(2)}) copy-start(bf16[2048,256]{1,0:T(8,128)(2,1)} %k_ref.1) | copy-start | bytes 3145732
  7.3 1.2 %copy-start.6 = (bf16[2048,256]{1,0:T(8,128)(2,1)S(1)}, bf16[2048,256]{1,0:T(8,128)(2,1)}, u32[]{:S(2)}) copy-start(bf16[2048,256]{1,0:T(8,128)(2,1)} %v_ref.1) | copy-start | bytes 3145732
  8.6 17.3 %copy-start.4 = (bf16[2,128,2048]{2,1,0:T(8,128)(2,1)S(1)}, bf16[2,128,2048]{2,1,0:T(8,128)(2,1)}, u32[]{:S(2)}) copy-start(bf16[2,128,2048]{2,1,0:T(8,128)(2,1)} %down_ref.1) | copy-start | bytes 3145732
  16.5 15.6 %copy-start.7 = (bf16[2,64,2048]{2,1,0:T(8,128)(2,1)S(1)}, bf16[2,64,2048]{2,1,0:T(8,128)(2,1)}, u32[]{:S(2)}) copy-start(bf16[2,64,2048]{2,1,0:T(8,128)(2,1)} %upq_ref.1) | copy-start | bytes 1572868
  16.6 15.6 %copy-start.8 = (bf16[2,64,256]{2,1,0:T(8,128)(2,1)S(1)}, bf16[2,64,256]{2,1,0:T(8,128)(2,1)}, u32[]{:S(2)}) copy-start(bf16[2,64,256]{2,1,0:T(8,128)(2,1)} %upv_ref.1) | copy-start | bytes 196612
  16.6 19.3 %collective-permute-start.7 = (bf16[48,1280]{1,0:T(8,128)(2,1)S(1)}, bf16[48,1280]{1,0:T(8,128)(2,1)S(1)}, u32[]{:S(2)}, u32[]{:S(2)}) collective-permute-start(bf16[48,1280]{1,0:T(8,128)(2,1)S(1)} %get-tuple-element.38), channel_id=1, source_target_pairs={{0,4},{4,0},{8,12},{12,8},{1,5},{5,1},{9,13},{13,9},{2,6},{6,2},{1... | collective-permute-start | bytes 368648 | tf_op jit(solution)/shard_map/ppermute | solution.py:440
  21.9 16.1 %collective-permute-start.8 = (bf16[48,1280]{1,0:T(8,128)(2,1)S(1)}, bf16[48,1280]{1,0:T(8,128)(2,1)S(1)}, u32[]{:S(2)}, u32[]{:S(2)}) collective-permute-start(bf16[48,1280]{1,0:T(8,128)(2,1)S(1)} %get-tuple-element.39), channel_id=1, source_target_pairs={{0,8},{4,12},{8,0},{12,4},{1,9},{5,13},{9,1},{13,5},{2,10},{6,14},... | collective-permute-start | bytes 368648 | tf_op jit(solution)/shard_map/ppermute | solution.py:440
  24.5 13.5 %collective-permute-start.9 = (bf16[48,1280]{1,0:T(8,128)(2,1)S(1)}, bf16[48,1280]{1,0:T(8,128)(2,1)S(1)}, u32[]{:S(2)}, u32[]{:S(2)}) collective-permute-start(bf16[48,1280]{1,0:T(8,128)(2,1)S(1)} %get-tuple-element.40), channel_id=1, source_target_pairs={{0,12},{4,8},{8,4},{12,0},{1,13},{5,9},{9,5},{13,1},{2,14},{6,10},... | collective-permute-start | bytes 368648 | tf_op jit(solution)/shard_map/ppermute | solution.py:440
  25.9 26.4 %copy-start = (bf16[16,2,256,128]{3,2,1,0:T(8,128)(2,1)S(1)}, bf16[16,2,256,128]{3,2,1,0:T(8,128)(2,1)}, u32[]{:S(2)}) copy-start(bf16[16,2,256,128]{3,2,1,0:T(8,128)(2,1)} %kc_ref.3) | copy-start | bytes 6291460
  25.9 26.4 %copy-start.1 = (bf16[16,2,256,128]{3,2,1,0:T(8,128)(2,1)S(1)}, bf16[16,2,256,128]{3,2,1,0:T(8,128)(2,1)}, u32[]{:S(2)}) copy-start(bf16[16,2,256,128]{3,2,1,0:T(8,128)(2,1)} %vc_ref.3) | copy-start | bytes 6291460
  26.9 2.0 %collective-permute-start.1 = (bf16[96,128]{1,0:T(8,128)(2,1)S(1)}, bf16[96,128]{1,0:T(8,128)(2,1)S(1)}, u32[]{:S(2)}, u32[]{:S(2)}) collective-permute-start(bf16[96,128]{1,0:T(8,128)(2,1)S(1)} %shard_map.121.rest_0_), channel_id=1, source_target_pairs={{0,1},{1,0},{2,3},{3,2},{4,5},{5,4},{6,7},{7,6},{8,9},{9,8},{10,11... | collective-permute-start | bytes 73736 | tf_op jit(solution)/shard_map/ppermute | solution.py:465
  27.7 3.8 %collective-permute-start.2 = (bf16[96,128]{1,0:T(8,128)(2,1)S(1)}, bf16[96,128]{1,0:T(8,128)(2,1)S(1)}, u32[]{:S(2)}, u32[]{:S(2)}) collective-permute-start(bf16[96,128]{1,0:T(8,128)(2,1)S(1)} %shard_map.121.rest_0_), channel_id=1, source_target_pairs={{0,2},{1,3},{2,0},{3,1},{4,6},{5,7},{6,4},{7,5},{8,10},{9,11},{10,... | collective-permute-start | bytes 73736 | tf_op jit(solution)/shard_map/ppermute | solution.py:465
  28.9 3.3 %collective-permute-start.3 = (bf16[96,128]{1,0:T(8,128)(2,1)S(1)}, bf16[96,128]{1,0:T(8,128)(2,1)S(1)}, u32[]{:S(2)}, u32[]{:S(2)}) collective-permute-start(bf16[96,128]{1,0:T(8,128)(2,1)S(1)} %shard_map.121.rest_0_), channel_id=1, source_target_pairs={{0,3},{1,2},{2,1},{3,0},{4,7},{5,6},{6,5},{7,4},{8,11},{9,10},{10,... | collective-permute-start | bytes 73736 | tf_op jit(solution)/shard_map/ppermute | solution.py:465
  33.6 21.4 %collective-permute-start.4 = (bf16[48,1280]{1,0:T(8,128)(2,1)S(1)}, bf16[48,1280]{1,0:T(8,128)(2,1)S(1)}, u32[]{:S(2)}, u32[]{:S(2)}) collective-permute-start(bf16[48,1280]{1,0:T(8,128)(2,1)S(1)} %get-tuple-element.34), channel_id=1, source_target_pairs={{0,4},{4,0},{8,12},{12,8},{1,5},{5,1},{9,13},{13,9},{2,6},{6,2},{1... | collective-permute-start | bytes 368648 | tf_op jit(solution)/shard_map/ppermute | solution.py:440
  33.6 21.3 %collective-permute-start.5 = (bf16[48,1280]{1,0:T(8,128)(2,1)S(1)}, bf16[48,1280]{1,0:T(8,128)(2,1)S(1)}, u32[]{:S(2)}, u32[]{:S(2)}) collective-permute-start(bf16[48,1280]{1,0:T(8,128)(2,1)S(1)} %get-tuple-element.35), channel_id=1, source_target_pairs={{0,8},{4,12},{8,0},{12,4},{1,9},{5,13},{9,1},{13,5},{2,10},{6,14},... | collective-permute-start | bytes 368648 | tf_op jit(solution)/shard_map/ppermute | solution.py:440
  35.9 19.1 %collective-permute-start.6 = (bf16[48,1280]{1,0:T(8,128)(2,1)S(1)}, bf16[48,1280]{1,0:T(8,128)(2,1)S(1)}, u32[]{:S(2)}, u32[]{:S(2)}) collective-permute-start(bf16[48,1280]{1,0:T(8,128)(2,1)S(1)} %get-tuple-element.36), channel_id=1, source_target_pairs={{0,12},{4,8},{8,4},{12,0},{1,13},{5,9},{9,5},{13,1},{2,14},{6,10},... | collective-permute-start | bytes 368648 | tf_op jit(solution)/shard_map/ppermute | solution.py:440
  38.0 7.1 %collective-permute-start.10 = (bf16[24,1152]{1,0:T(8,128)(2,1)S(1)}, bf16[24,1152]{1,0:T(8,128)(2,1)S(1)}, u32[]{:S(2)}, u32[]{:S(2)}) collective-permute-start(bf16[24,1152]{1,0:T(8,128)(2,1)S(1)} %get-tuple-element.46), channel_id=1, source_target_pairs={{0,4},{4,0},{8,12},{12,8},{1,5},{5,1},{9,13},{13,9},{2,6},{6,2},{1... | collective-permute-start | bytes 165896 | tf_op jit(solution)/shard_map/ppermute | solution.py:440
  38.0 14.2 %collective-permute-start.11 = (bf16[24,1152]{1,0:T(8,128)(2,1)S(1)}, bf16[24,1152]{1,0:T(8,128)(2,1)S(1)}, u32[]{:S(2)}, u32[]{:S(2)}) collective-permute-start(bf16[24,1152]{1,0:T(8,128)(2,1)S(1)} %get-tuple-element.47), channel_id=1, source_target_pairs={{0,8},{4,12},{8,0},{12,4},{1,9},{5,13},{9,1},{13,5},{2,10},{6,14},... | collective-permute-start | bytes 165896 | tf_op jit(solution)/shard_map/ppermute | solution.py:440
  45.1 7.2 %collective-permute-start.12 = (bf16[24,1152]{1,0:T(8,128)(2,1)S(1)}, bf16[24,1152]{1,0:T(8,128)(2,1)S(1)}, u32[]{:S(2)}, u32[]{:S(2)}) collective-permute-start(bf16[24,1152]{1,0:T(8,128)(2,1)S(1)} %get-tuple-element.48), channel_id=1, source_target_pairs={{0,12},{4,8},{8,4},{12,0},{1,13},{5,9},{9,5},{13,1},{2,14},{6,10},... | collective-permute-start | bytes 165896 | tf_op jit(solution)/shard_map/ppermute | solution.py:440

commit v3 on v2

v3 whole, which is shorter than its diff:
```python
import functools
import math

import jax
import jax.numpy as jnp
from jax import lax
from jax.experimental import pallas as pl
from jax.experimental.pallas import tpu as pltpu
from jax.sharding import PartitionSpec as P

ROPE_BASE = 500000.0
BF16 = jnp.bfloat16
F32 = jnp.float32
FEATURE_AXES = ("tp", "sub")
CARRIER = ((0, 3, 2, 1), (2, 1, 0, 3), (3, 1, 2, 0), (1, 2, 0, 3))


def call(body, out_shape, args, in_specs=None, out_specs=None, grid=None, scratch=(), flops=0, bytes_=0, limit=40, **more):
    whole = pl.BlockSpec(memory_space=pltpu.VMEM)
    kwargs = {} if grid is None else {"grid": grid}
    if in_specs is None:
        in_specs = [whole] * len(args)
    if out_specs is None:
        out_specs = jax.tree.map(lambda _: whole, out_shape)
    inner = getattr(body, "func", body)
    return pl.pallas_call(
        body,
        name=inner.__name__,
        out_shape=out_shape,
        in_specs=in_specs,
        out_specs=out_specs,
        scratch_shapes=list(scratch),
        compiler_params=pltpu.CompilerParams(vmem_limit_bytes=limit * 1024 * 1024),
        cost_estimate=pl.CostEstimate(flops=flops, bytes_accessed=bytes_, transcendentals=0),
        **kwargs,
        **more,
    )(*args)


VMEM = pl.BlockSpec(memory_space=pltpu.VMEM)
SMEM = pl.BlockSpec(memory_space=pltpu.SMEM)
HBM = pl.BlockSpec(memory_space=pltpu.HBM)
ANY = pl.BlockSpec(memory_space=pl.ANY)


def iota(shape, dim):
    return lax.broadcasted_iota(jnp.int32, shape, dim)


def nn(a, b):
    return lax.dot_general(a, b, (((1,), (0,)), ((), ())), preferred_element_type=F32)


def nt(a, b):
    return lax.dot_general(a, b, (((1,), (1,)), ((), ())), preferred_element_type=F32)


def tn(a, b):
    return lax.dot_general(a, b, (((0,), (0,)), ((), ())), preferred_element_type=F32)


def row_facts(row_request, request_adapter, lengths, home_rows, resident):
    rows = row_request.shape[1]
    across, down = iota((rows, rows), 1), iota((rows, rows), 0)
    eye = across == down
    request_col = jnp.sum(jnp.where(eye, row_request.astype(F32), 0.0), 1, keepdims=True)
    held = request_col == across.astype(F32)
    adapter_col = jnp.sum(jnp.where(held, request_adapter.astype(F32), 0.0), 1, keepdims=True)
    length_col = jnp.sum(jnp.where(held, lengths.astype(F32), 0.0), 1, keepdims=True)
    adapter_row = jnp.sum(jnp.where(eye, adapter_col, 0.0), 0, keepdims=True)
    length_row = jnp.sum(jnp.where(eye, length_col, 0.0), 0, keepdims=True)
    owner_col = jnp.floor((adapter_col + 0.5) / resident)
    owner_row = jnp.floor((adapter_row + 0.5) / resident)
    before = (owner_col == owner_row) & (down < across) & (down // home_rows == across // home_rows)
    slot_row = jnp.sum(jnp.where(before, 1.0, 0.0), 0, keepdims=True)
    return adapter_row, owner_row, slot_row, length_row


def slot_table(owner_row, slot_row, owner, home_rows, cap):
    rows = owner_row.shape[1]
    places = rows // home_rows * cap
    place, row = iota((places, rows), 0), iota((places, rows), 1)
    return (
        (owner_row == owner.astype(F32))
        & (place // cap == row // home_rows)
        & (slot_row == (place % cap).astype(F32))
    )


def select_body(home_rows, cap, resident, owners, rr_hbm, ra_hbm, ln_hbm, hid_hbm, *rest):
    outs, rest = rest[:-6], rest[-6:]
    facts_ref, rr_ref, ra_ref, ln_ref, hid_ref, sems = rest
    copies = [
        pltpu.make_async_copy(source, target, sems.at[n])
        for n, (source, target) in enumerate(
            ((rr_hbm, rr_ref), (ra_hbm, ra_ref), (ln_hbm, ln_ref), (hid_hbm, hid_ref))
        )
    ]
    for copy in copies:
        copy.start()
    for copy in copies[:3]:
        copy.wait()
    adapter_row, owner_row, slot_row, length_row = row_facts(
        rr_ref[...], ra_ref[...], ln_ref[...], home_rows, resident
    )
    facts_ref[...] = jnp.concatenate([adapter_row, owner_row, slot_row, length_row] * 2, 0)
    tables = [
        slot_table(owner_row, slot_row, owner, home_rows, cap).astype(BF16) for owner in owners()
    ]
    copies[3].wait()
    for table, out in zip(tables, outs):
        places = table.shape[0]
        for s in range(hid_ref.shape[0]):
            out[s * places : (s + 1) * places] = nn(table, hid_ref[s]).astype(BF16)


def project_early_body(home_rows, homes, heads, x_ref, q_ref, k_ref, v_ref, near_ref, far_ref, scr):
    steps, rows = x_ref.shape[0] // (homes * home_rows), homes * home_rows
    q_cols = q_ref.shape[1]
    head_dim = k_ref.shape[1]
    me = lax.axis_index("pool")
    local_rows = steps * home_rows
    base = pl.program_id(0) * 2 * local_rows
    scr[:, :q_cols] = nn(x_ref[...], q_ref[...])
    scr[:, q_cols : q_cols + head_dim] = nn(x_ref[...], k_ref[...])
    scr[:, q_cols + head_dim :] = nn(x_ref[...], v_ref[...])
    for out, ds in ((far_ref, (1, 3)), (near_ref, (0, 2))):
        for n, d in enumerate(ds):
            for s in range(steps):
                begin = pl.multiple_of(s * rows + (me ^ d) * home_rows, home_rows)
                there = pl.multiple_of(base + n * local_rows + s * home_rows, home_rows)
                out[pl.ds(there, home_rows), :] = scr[pl.ds(begin, home_rows), :].astype(BF16)


def project_late_body(x_ref, q_ref, k_ref, v_ref, facts_ref, out, facts_out):
    q_cols = q_ref.shape[1]
    head_dim = k_ref.shape[1]
    facts_out[...] = facts_ref[...]
    out[0, :, :q_cols] = nn(x_ref[...], q_ref[...]).astype(BF16)
    out[0, :, q_cols : q_cols + head_dim] = nn(x_ref[...], k_ref[...]).astype(BF16)
    out[0, :, q_cols + head_dim :] = nn(x_ref[...], v_ref[...]).astype(BF16)


def pass_body(message_ref, _, out_ref):
    out_ref[...] = message_ref[...]


def add_body(heads, near_ref, got_ref, out_ref):
    rows = near_ref.shape[0] // (2 * heads)
    for n in range(heads):
        here = slice((2 * n + 1) * rows, (2 * n + 2) * rows)
        out_ref[n * rows : (n + 1) * rows, :] = (
            near_ref[here, :].astype(F32) + got_ref[here, :].astype(F32)
        ).astype(BF16)


def shrink_body(home_rows, cap, resident, parts, facts_ref, down_ref, *rest):
    sent, out = rest[:parts], rest[-1]
    adapter_row, owner_row, slot_row = facts_ref[0:1], facts_ref[1:2], facts_ref[2:3]
    me = lax.axis_index("pool")
    table = slot_table(owner_row, slot_row, me, home_rows, cap)
    local = jnp.sum(jnp.where(table, adapter_row - (me * resident).astype(F32) + 1.0, 0.0), 1, keepdims=True) - 1.0
    places = table.shape[0]
    steps = sent[0].shape[0] // places
    local = jnp.concatenate([local] * steps, 0)
    width = sent[0].shape[1]
    total = None
    for a in range(resident):
        term = None
        for i in range(parts):
            if parts == 1:
                block = down_ref[a]
            else:
                part = lax.rem(me + parts * places - i, parts)
                block = down_ref[a, :, pl.ds(pl.multiple_of(part * width, width), width)]
            piece = nt(sent[i][...], block)
            term = piece if term is None else term + piece
        term = jnp.where(local == float(a), term, 0.0)
        total = term if total is None else total + term
    out[...] = total.astype(BF16)


def expand_body(home_rows, homes, cap, resident, early, late, facts_ref, upq_ref, upv_ref, *rest):
    messages, rest, scr = rest[-1 - homes : -1], rest[: -1 - homes], rest[-1]
    shares, partials = rest[:-1], rest[-1]
    adapter_row, owner_row, slot_row = facts_ref[0:1], facts_ref[1:2], facts_ref[2:3]
    me = lax.axis_index("pool")
    table = slot_table(owner_row, slot_row, me, home_rows, cap)
    places, rows = table.shape
    local = jnp.sum(jnp.where(table, adapter_row - (me * resident).astype(F32) + 1.0, 0.0), 1, keepdims=True) - 1.0
    spread = table.astype(BF16)
    shrunk = shares[0][...].astype(F32)
    for share in shares[1:]:
        shrunk = shrunk + share[...].astype(F32)
    steps = shrunk.shape[0] // places
    local_rows = steps * home_rows
    local = jnp.concatenate([local] * steps, 0)
    rank = upq_ref.shape[1]
    low_q, low_v = shrunk[:, :rank], shrunk[:, rank:]
    masked_q = [jnp.where(local == float(a), low_q, 0.0).astype(BF16) for a in range(resident)]
    masked_v = [jnp.where(local == float(a), low_v, 0.0).astype(BF16) for a in range(resident)]
    kv_heads = len(early) + len(late)
    width_q = upq_ref.shape[2] // kv_heads
    width_v = upv_ref.shape[2] // kv_heads

    def up(h):
        delta_q = delta_v = None
        for a in range(resident):
            term_q = nn(masked_q[a], upq_ref[a, :, h * width_q : (h + 1) * width_q])
            term_v = nn(masked_v[a], upv_ref[a, :, h * width_v : (h + 1) * width_v])
            delta_q = term_q if delta_q is None else delta_q + term_q
            delta_v = term_v if delta_v is None else delta_v + term_v
        return delta_q, delta_v

    for n, h in enumerate(late):
        delta_q, delta_v = up(h)
        for s in range(steps):
            here = slice(s * places, (s + 1) * places)
            there = slice(s * rows, (s + 1) * rows)
            scr[there, :width_q] = partials[n, there, :width_q].astype(F32) + tn(spread, delta_q[here].astype(BF16))
            scr[there, width_q : width_q + width_v] = partials[n, there, width_q : width_q + width_v].astype(F32)
            scr[there, width_q + width_v :] = partials[n, there, width_q + width_v :].astype(F32) + tn(
                spread, delta_v[here].astype(BF16)
            )
        for d in range(homes):
            home = me ^ d
            for s in range(steps):
                begin = pl.multiple_of(s * rows + home * home_rows, home_rows)
                row = n * local_rows + s * home_rows
                messages[d][row : row + home_rows, :] = scr[pl.ds(begin, home_rows), :].astype(BF16)
    for n, h in enumerate(early):
        delta_q, delta_v = up(h)
        both = jnp.concatenate([delta_q, delta_v, jnp.zeros((steps * places, width_v), F32)], 1)
        scr[: steps * places, :] = both
        for d in range(homes):
            home = me ^ d
            pieces = []
            for s in range(steps):
                begin = pl.multiple_of(s * places + home * cap, cap)
                pieces.append(scr[pl.ds(begin, cap), :])
            row = len(late) * local_rows + n * steps * cap
            messages[d][row : row + steps * cap, :] = jnp.concatenate(pieces, 0).astype(BF16)


def home_body(home_rows, homes, cap, steps, facts_ref, cos_ref, sin_ref, len_ref, *places_out):
    owner_row, slot_row, length_row = facts_ref[1:2], facts_ref[2:3], facts_ref[3:4]
    me = lax.axis_index("pool")
    local_rows, head_dim = cos_ref.shape
    rows = facts_ref.shape[1]
    row, batch = iota((local_rows, rows), 0), iota((local_rows, rows), 1)
    mine = batch == me * home_rows + row % home_rows
    length = jnp.sum(jnp.where(mine, length_row, 0.0), 1, keepdims=True)
    owner = jnp.sum(jnp.where(mine, owner_row, 0.0), 1, keepdims=True)
    slot = jnp.sum(jnp.where(mine, slot_row, 0.0), 1, keepdims=True)
    len_ref[...] = jnp.broadcast_to(length[:home_rows], len_ref.shape)
    lane = iota((local_rows, head_dim), 1)
    step = iota((local_rows, head_dim), 0) // home_rows
    half = head_dim // 2
    inverse_freq = jnp.exp((lane % half).astype(F32) * (-2.0 * math.log(ROPE_BASE) / head_dim))
    angle = (length + step.astype(F32)) * inverse_freq
    cos_ref[...] = jnp.cos(angle)
    sin_ref[...] = jnp.where(lane < half, -1.0, 1.0) * jnp.sin(angle)
    place, local = iota((local_rows, steps * cap), 1), iota((local_rows, steps * cap), 0)
    for d, out in enumerate(places_out):
        out[...] = (
            (owner == (me ^ d).astype(F32))
            & (place // cap == local // home_rows)
            & (slot == (place % cap).astype(F32))
        ).astype(BF16)


def attend_body(home_rows, homes, steps, early, late, cos_ref, sin_ref, len_ref, kc_ref, vc_ref, *rest):
    spots, rest = rest[: homes if early else 0], rest[homes if early else 0 :]
    early_sums, rest = rest[: 3 if early else 0], rest[3 if early else 0 :]
    messages, (out, q_scr, new_scr, o_scr, total_scr) = rest[:homes], rest[homes:]
    local_rows, head_dim = cos_ref.shape
    cached = kc_ref.shape[2]
    heads = (messages[0].shape[1] - 2 * head_dim) // head_dim
    width_q = heads * head_dim
    places = (messages[0].shape[0] - local_rows * len(late)) // max(1, len(early))
    scale = 1.0 / math.sqrt(head_dim)
    cos, sin = cos_ref[...], sin_ref[...]
    kv_heads = len(early) + len(late)

    def rope(v):
        return v * cos + pltpu.roll(v, head_dim // 2, 1) * sin

    def projected(h, begin, delta_begin):
        columns = slice(begin, begin + head_dim)
        if h in late:
            row = late.index(h) * local_rows
            pieces = [m[row : row + local_rows, columns] for m in messages]
        else:
            n = early.index(h)
            near, got, far_sum = early_sums
            here = slice(2 * n * local_rows, (2 * n + 1) * local_rows)
            pieces = [near[here, columns], got[here, columns], far_sum[n * local_rows : (n + 1) * local_rows, columns]]
        total = sum(piece.astype(F32) for piece in pieces)
        if h in early and delta_begin is not None:
            row = len(late) * local_rows + early.index(h) * places
            columns = slice(delta_begin, delta_begin + head_dim)
            total = total + sum(nn(spot[...], m[row : row + places, columns]) for spot, m in zip(spots, messages))
        return total

    row, col = iota((local_rows, local_rows), 0), iota((local_rows, local_rows), 1)
    live = (row % home_rows == col % home_rows) & (col // home_rows <= row // home_rows)
    per_row = heads * steps
    spot_ids = iota((per_row, cached), 1).astype(F32)
    every = [(h, b) for h in range(kv_heads) for b in range(home_rows)]
    mine = {
        (h, b): pl.ds(h * heads * local_rows + b, per_row, stride=home_rows) for h, b in every
    }
    new_weights, values_new = {}, {}
    for h in range(kv_heads):
        key_new = rope(projected(h, width_q, None)).astype(BF16)
        values_new[h] = projected(h, width_q + head_dim, width_q).astype(BF16)
        for n in range(heads):
            query = rope(projected(h, n * head_dim, n * head_dim)).astype(BF16)
            here = slice((h * heads + n) * local_rows, (h * heads + n + 1) * local_rows)
            q_scr[here, :] = query.astype(F32)
            weight = jnp.where(live, jnp.exp(nt(query, key_new) * scale), 0.0)
            new_weights[h, n] = weight
            new_scr[here, :] = jnp.broadcast_to(jnp.sum(weight, 1, keepdims=True), (local_rows, head_dim))
    for h in range(kv_heads):
        scores = [nt(q_scr[mine[h, b], :].astype(BF16), kc_ref[b, h]) for b in range(home_rows)]
        probs = []
        for b in range(home_rows):
            weight = jnp.where(spot_ids < len_ref[b : b + 1, :], jnp.exp(scores[b] * scale), 0.0)
            total = jnp.sum(weight, 1, keepdims=True) + new_scr[mine[h, b], :][:, :1]
            total_scr[mine[h, b], :] = jnp.broadcast_to(total, (per_row, head_dim))
            probs.append((weight / total).astype(BF16))
        for b in range(home_rows):
            o_scr[mine[h, b], :] = nn(probs[b], vc_ref[b, h])
    for h in range(kv_heads):
        for n in range(heads):
            at = h * heads + n
            here = slice(at * local_rows, (at + 1) * local_rows)
            prob = (new_weights[h, n] / total_scr[here, :local_rows]).astype(BF16)
            out[:, at * head_dim : (at + 1) * head_dim] = (
                o_scr[here, :] + nn(prob, values_new[h])
            ).astype(BF16)


def on_device(
    hidden,
    query_weight,
    key_weight,
    value_weight,
    key_cache_rows,
    value_cache_rows,
    adapter_down_weight,
    adapter_up_query,
    adapter_up_value,
    request_adapter,
    row_request,
    lengths,
):
    homes = lax.axis_size("pool")
    features = lax.axis_size(FEATURE_AXES)
    home_rows, kv_here, cached, head_dim = key_cache_rows.shape
    rows, steps, slice_width = hidden.shape
    resident = adapter_down_weight.shape[0]
    rank = adapter_up_query.shape[1]
    q_cols = query_weight.shape[1] // kv_here
    cap = max(2, 2 * home_rows // homes)
    places = homes * cap
    fold = homes // features
    local_rows = steps * home_rows
    width = q_cols + 2 * head_dim
    shape = jax.ShapeDtypeStruct

    if homes == len(CARRIER) and features == len(CARRIER):
        targets = [[CARRIER[q].index(g) for g in range(features)] for q in range(homes)]
        perms = [[(q * features + g, targets[q][g] * features + q) for q in range(homes) for g in range(features)]]

        def owners():
            pool_here, feature_here = lax.axis_index("pool"), lax.axis_index(FEATURE_AXES)
            at = pool_here * features + feature_here
            owner = jnp.int32(0)
            for q in range(homes):
                for g in range(features):
                    owner = jnp.where(at == q * features + g, targets[q][g], owner)
            return [owner]

    else:
        perms = [
            [
                (q * features + g, (g * fold + (i + q) % fold) * features + q // fold)
                for q in range(homes)
                for g in range(features)
            ]
            for i in range(fold)
        ]

        def owners():
            pool_here, feature_here = lax.axis_index("pool"), lax.axis_index(FEATURE_AXES)
            return [feature_here * fold + lax.rem(pool_here + i, fold) for i in range(fold)]

    rr, ra, ln = row_request.reshape(1, rows), request_adapter.reshape(1, rows), lengths.reshape(1, rows)
    by_step = hidden.transpose(1, 0, 2)
    x = by_step.reshape(steps * rows, slice_width)
    early = ()
    late = tuple(range(kv_here))

    *selected, facts = call(
        functools.partial(select_body, home_rows, cap, resident, owners),
        [shape((steps * places, slice_width), BF16)] * fold + [shape((8, rows), F32)],
        (rr, ra, ln, by_step),
        in_specs=[HBM] * 4,
        limit=60,
        scratch=[pltpu.VMEM((1, rows), jnp.int32)] * 3
        + [pltpu.VMEM(by_step.shape, BF16), pltpu.SemaphoreType.DMA((4,))],
        flops=2 * steps * places * rows * slice_width,
        bytes_=2 * steps * (rows + places) * slice_width,
    )
    sent = [lax.ppermute(s, ("pool", *FEATURE_AXES), perm) for s, perm in zip(selected, perms)]

    def swap(value, d):
        return lax.ppermute(value, "pool", [(i, i ^ d) for i in range(homes)])

    weights = (x, query_weight, key_weight, value_weight)

    def weight_specs(first):
        return [
            pl.BlockSpec(x.shape, lambda i: (0, 0)),
            pl.BlockSpec((slice_width, q_cols), lambda i: (0, first + i)),
            pl.BlockSpec((slice_width, head_dim), lambda i: (0, first + i)),
            pl.BlockSpec((slice_width, head_dim), lambda i: (0, first + i)),
        ]

    early_sums = ()
    if early:
        pair = shape((2 * local_rows * len(early), width), BF16)
        near, far = call(
            functools.partial(project_early_body, home_rows, homes, len(early)),
            [pair] * 2,
            weights,
            limit=60,
            in_specs=weight_specs(0),
            out_specs=[pl.BlockSpec(pair.shape, lambda i: (0, 0))] * 2,
            grid=(len(early),),
            scratch=[pltpu.VMEM((steps * rows, width), F32)],
            flops=2 * steps * rows * slice_width * width * len(early),
            bytes_=2 * slice_width * width * len(early),
        )
        got = swap(far, 1)

    partials, facts = call(
        project_late_body,
        [shape((kv_here, steps * rows, width), BF16), shape(facts.shape, F32)],
        (*weights, facts),
        in_specs=weight_specs(0) + [pl.BlockSpec(facts.shape, lambda i: (0, 0))],
        out_specs=[
            pl.BlockSpec((1, steps * rows, width), lambda i: (i, 0, 0)),
            pl.BlockSpec(facts.shape, lambda i: (0, 0)),
        ],
        grid=(kv_here,),
        limit=50,
        flops=2 * steps * rows * slice_width * width * kv_here,
        bytes_=2 * slice_width * width * kv_here,
    )
    share = call(
        functools.partial(shrink_body, home_rows, cap, resident, fold),
        shape((steps * places, 2 * rank), BF16),
        (facts, adapter_down_weight, *sent),
        flops=4 * steps * places * rank * slice_width * fold * resident,
        bytes_=4 * resident * rank * slice_width * fold,
    )
    shares = [share] + [
        lax.ppermute(share, FEATURE_AXES, [(i, i ^ d) for i in range(features)]) for d in range(1, features)
    ]
    tables = call(
        functools.partial(home_body, home_rows, homes, cap, steps),
        [shape((local_rows, head_dim), F32)] * 2
        + [shape((home_rows, cached), F32)]
        + [shape((local_rows, steps * cap), BF16)] * homes,
        (facts,),
        flops=10**7,
        bytes_=10**5,
    )
    cos, sin, length, spots = tables[0], tables[1], tables[2], tables[3:]
    if early:
        far_sum = call(
            functools.partial(add_body, len(early)),
            shape((local_rows * len(early), width), BF16),
            (near, got),
            flops=local_rows * len(early) * width,
            bytes_=6 * local_rows * len(early) * width,
        )
        early_sums = (near, got, swap(far_sum, 2))
    message = shape((local_rows * len(late) + steps * cap * len(early), width), BF16)
    messages = call(
            functools.partial(expand_body, home_rows, homes, cap, resident, early, late),
            [message] * homes,
            (facts, adapter_up_query, adapter_up_value, *shares, partials),
                        scratch=[pltpu.VMEM((max(rows, places) * steps, width), F32)],
            flops=2 * steps * places * rank * resident * q_cols * kv_here,
            bytes_=2 * resident * rank * q_cols * kv_here,
        )
    messages = list(messages)
    if early:
        messages[1] = call(pass_body, message, (messages[1], early_sums[2]), in_specs=[VMEM, ANY])
    messages = [messages[0]] + [swap(messages[d], d) for d in range(1, homes)]
    out = call(
        functools.partial(attend_body, home_rows, homes, steps, early, late),
        shape((local_rows, q_cols * kv_here), BF16),
        (
            cos,
            sin,
            length,
            key_cache_rows,
            value_cache_rows,
            *(spots if early else ()),
            *early_sums,
            *messages,
        ),
        scratch=[pltpu.VMEM((kv_here * q_cols // head_dim * local_rows, head_dim), F32)] * 4,
        flops=4 * local_rows * q_cols * kv_here * cached,
        bytes_=4 * home_rows * cached * head_dim * kv_here,
    )
    return out.reshape(steps, home_rows, q_cols * kv_here).transpose(1, 0, 2)


def solution(mesh):
    return jax.shard_map(
        on_device,
        mesh=mesh,
        in_specs=(
            P("groups", None, "pool"),
            P("pool", ("tp", "sub")),
            P("pool", ("tp", "sub")),
            P("pool", ("tp", "sub")),
            P(("groups", "pool"), ("tp", "sub"), None, None),
            P(("groups", "pool"), ("tp", "sub"), None, None),
            P(("groups", "pool"), None, ("tp", "sub")),
            P(("groups", "pool"), None, ("tp", "sub")),
            P(("groups", "pool"), None, ("tp", "sub")),
            P("groups"),
            P("groups"),
            P("groups"),
        ),
        out_specs=P(("groups", "pool"), None, ("tp", "sub")),
        check_vma=False,
    )
```

time: 57.1 us -> 51.1 us (0.89)
  the two profiles are of different devices: /device:TPU:0 before, /device:TPU:8 now
where the time goes in v3:
time: 51.1 us; the launch traced here: 50.7 us
  waiting for transfers between devices  24.2 us (47%)
  Pallas kernels  12.4 us (24%)
  starting transfers between devices  9.81 us (19%)
  local copies, waits for them, and re-layouts  4.28 us (8%)
    ppermute x3, waiting for transfers between devices, swap(): return lax.ppermute(value, 'pool', [(i, i ^ d) for i in range(homes)])  21.4 us
    pallas_call x6, Pallas kernels, call(): pl.pallas_call(body, name=inner.__name__, out_shape=out_shape, in_specs=i...  12.4 us
    unnamed x18, local copies, waits for them, and re-layouts  4.28 us
    ppermute x3, starting transfers between devices, swap(): return lax.ppermute(value, 'pool', [(i, i ^ d) for i in range(homes)])  3.55 us
    ppermute x3, starting transfers between devices, on_device(): lax.ppermute(share, FEATURE_AXES, [(i, i ^ d) for i in range(features)])  3.33 us
    ppermute x1, starting transfers between devices, on_device(): lax.ppermute(s, ('pool', *FEATURE_AXES), perm)  2.92 us
    ppermute x3, waiting for transfers between devices, on_device(): lax.ppermute(share, FEATURE_AXES, [(i, i ^ d) for i in range(features)])  2.44 us
  transfers between devices with their start and end apart: 7, of which 6 were waited for; matrix products, arithmetic and copies ran while one was open for 0% of the time, Pallas kernels for 12%

profile of v3, /device:TPU:8, one launch (start us, length us, event | category | flops | bytes accessed | tf_op | source)
XLA Modules:
  0.0 50.7 jit_solution(1155602620317120108)
XLA Ops:
  0.0 2.2 %select_body.1 = (bf16[96,2048]{1,0:T(8,128)(2,1)}, f32[8,64]{1,0:T(8,128)}) custom-call(s32[1,64]{1,0:T(1,128)} %bitcast.11, s32[1,64]{1,0:T(1,128)} %bitcast.12, s32[1,64]{1,0:T(1,128)} %bitcast.13, bf16[3,64,2048]{2,1,0:T(8,128)(2,1)} %bitcast.9), custom_call_target="tpu_custom_call" | custom-call | flops 25165824 | bytes 1179648 | tf_op jit(solution)/shard_map/select_body/pallas_call | solution.py:26
  2.2 2.9 %collective-permute-start = (bf16[96,2048]{1,0:T(8,128)(2,1)}, bf16[96,2048]{1,0:T(8,128)(2,1)S(1)}, u32[]{:S(2)}, u32[]{:S(2)}) collective-permute-start(bf16[96,2048]{1,0:T(8,128)(2,1)} %get-tuple-element.21), channel_id=1, source_target_pairs={{0,0},{1,12},{2,8},{3,4},{4,9},{5,5},{6,1},{7,13},{8,14},{9,6},{10... | collective-permute-start | bytes 1179656 | tf_op jit(solution)/shard_map/ppermute | solution.py:416
  5.2 0.0 copy-start
  5.2 1.1 %copy-done = bf16[64,3,2048]{2,0,1:T(8,128)(2,1)S(1)} copy-done((bf16[64,3,2048]{2,0,1:T(8,128)(2,1)S(1)}, bf16[64,3,2048]{2,0,1:T(8,128)(2,1)}, u32[]{:S(2)}) %copy-start) | copy-done | bytes 786456
  6.3 0.0 copy-start.3
  6.3 1.2 %copy-done.3 = bf16[2048,256]{1,0:T(8,128)(2,1)S(1)} copy-done((bf16[2048,256]{1,0:T(8,128)(2,1)S(1)}, bf16[2048,256]{1,0:T(8,128)(2,1)}, u32[]{:S(2)}) %copy-start.3) | copy-done | bytes 1048600
  7.5 1.2 %copy-done.4 = bf16[2048,256]{1,0:T(8,128)(2,1)S(1)} copy-done((bf16[2048,256]{1,0:T(8,128)(2,1)S(1)}, bf16[2048,256]{1,0:T(8,128)(2,1)}, u32[]{:S(2)}) %copy-start.4) | copy-done | bytes 1048600
  8.7 0.7 %copy-done.8 = f32[8,64]{1,0:T(8,128)S(1)} copy-done((f32[8,64]{1,0:T(8,128)S(1)}, f32[8,64]{1,0:T(8,128)}, u32[]{:S(2)}) %copy-start.8) | copy-done | bytes 2072
  9.4 5.2 %project_late_body.1 = (bf16[2,192,1280]{2,1,0:T(8,128)(2,1)S(1)}, f32[8,64]{1,0:T(8,128)S(1)}) custom-call(bf16[192,2048]{1,0:T(8,128)(2,1)S(1)} %bitcast.10, bf16[2048,2048]{1,0:T(8,128)(2,1)} %q_ref.1, bf16[2048,256]{1,0:T(8,128)(2,1)S(1)} %copy-done.3, bf16[2048,256]{1,0:T(8,128)(2,1)S(1)} %copy-done.4, f32[8,64]{1,0:T(8,128)S(1)} %copy-done.8), custom_call_target="tpu_custom_call" | custom-call | flops 2013265920 | bytes 10485760 | tf_op jit(solution)/shard_map/project_late_body/pallas_call | solution.py:26
  14.6 0.0 copy-start.1
  14.6 0.3 collective-permute-done.rest_0_
  15.0 0.0 copy-done.5
  15.0 0.5 shrink_body.1.rest_0_
  15.5 1.9 %collective-permute-start.3 = (bf16[96,128]{1,0:T(8,128)(2,1)S(1)}, bf16[96,128]{1,0:T(8,128)(2,1)S(1)}, u32[]{:S(2)}, u32[]{:S(2)}) collective-permute-start(bf16[96,128]{1,0:T(8,128)(2,1)S(1)} %shrink_body.1.rest_0_), channel_id=1, source_target_pairs={{0,3},{1,2},{2,1},{3,0},{4,7},{5,6},{6,5},{7,4},{8,11},{9,10},{10,... | collective-permute-start | bytes 73736 | tf_op jit(solution)/shard_map/ppermute | solution.py:470
  17.4 1.4 %collective-permute-start.2 = (bf16[96,128]{1,0:T(8,128)(2,1)S(1)}, bf16[96,128]{1,0:T(8,128)(2,1)S(1)}, u32[]{:S(2)}, u32[]{:S(2)}) collective-permute-start(bf16[96,128]{1,0:T(8,128)(2,1)S(1)} %shrink_body.1.rest_0_), channel_id=1, source_target_pairs={{0,2},{1,3},{2,0},{3,1},{4,6},{5,7},{6,4},{7,5},{8,10},{9,11},{10,... | collective-permute-start | bytes 73736 | tf_op jit(solution)/shard_map/ppermute | solution.py:470
  18.8 0.0 collective-permute-start.1
  18.8 0.1 collective-permute-done.3.rest_3_
  18.9 2.3 %collective-permute-done.2.rest_2_ = bf16[96,128]{1,0:T(8,128)(2,1)S(1)} collective-permute-done((bf16[96,128]{1,0:T(8,128)(2,1)S(1)}, bf16[96,128]{1,0:T(8,128)(2,1)S(1)}, u32[]{:S(2)}, u32[]{:S(2)}) %collective-permute-start.2) | collective-permute-done | bytes 24608 | tf_op jit(solution)/shard_map/ppermute | solution.py:470
  21.2 0.0 collective-permute-done.1.rest_1_
  21.2 0.0 copy-done.6
  21.2 0.0 copy-done.7
  21.2 1.1 %expand_body.1 = (bf16[96,1280]{1,0:T(8,128)(2,1)S(1)}, bf16[96,1280]{1,0:T(8,128)(2,1)S(1)}, bf16[96,1280]{1,0:T(8,128)(2,1)S(1)}, bf16[96,1280]{1,0:T(8,128)(2,1)S(1)}) custom-call(f32[8,64]{1,0:T(8,128)S(1)} %get-tuple-element.17.facts_ref, bf16[2,64,2048]{2,1,0:T(8,128)(2,1)S(1)} %copy-done.6, bf16[2,64,256]{2,1,0:T(8,128)(2,1)S(1)} %copy-done.7, ...), custom_call_target="tpu_custom_call" | custom-call | flops 50331648 | bytes 524288 | tf_op jit(solution)/shard_map/expand_body/pallas_call | solution.py:26
  22.4 1.7 %collective-permute-start.4 = (bf16[96,1280]{1,0:T(8,128)(2,1)S(1)}, bf16[96,1280]{1,0:T(8,128)(2,1)S(1)}, u32[]{:S(2)}, u32[]{:S(2)}) collective-permute-start(bf16[96,1280]{1,0:T(8,128)(2,1)S(1)} %get-tuple-element.24), channel_id=1, source_target_pairs={{0,4},{4,0},{8,12},{12,8},{1,5},{5,1},{9,13},{13,9},{2,6},{6,2},{1... | collective-permute-start | bytes 737288 | tf_op jit(solution)/shard_map/ppermute | solution.py:419
  24.0 1.3 %collective-permute-start.5 = (bf16[96,1280]{1,0:T(8,128)(2,1)S(1)}, bf16[96,1280]{1,0:T(8,128)(2,1)S(1)}, u32[]{:S(2)}, u32[]{:S(2)}) collective-permute-start(bf16[96,1280]{1,0:T(8,128)(2,1)S(1)} %get-tuple-element.25), channel_id=1, source_target_pairs={{0,8},{4,12},{8,0},{12,4},{1,9},{5,13},{9,1},{13,5},{2,10},{6,14},... | collective-permute-start | bytes 737288 | tf_op jit(solution)/shard_map/ppermute | solution.py:419
  25.4 0.5 %collective-permute-start.6 = (bf16[96,1280]{1,0:T(8,128)(2,1)S(1)}, bf16[96,1280]{1,0:T(8,128)(2,1)S(1)}, u32[]{:S(2)}, u32[]{:S(2)}) collective-permute-start(bf16[96,1280]{1,0:T(8,128)(2,1)S(1)} %get-tuple-element.26), channel_id=1, source_target_pairs={{0,12},{4,8},{8,4},{12,0},{1,13},{5,9},{9,5},{13,1},{2,14},{6,10},... | collective-permute-start | bytes 737288 | tf_op jit(solution)/shard_map/ppermute | solution.py:419
  25.9 0.8 %home_body.1 = (f32[48,128]{1,0:T(8,128)S(1)}, f32[48,128]{1,0:T(8,128)S(1)}, f32[16,256]{1,0:T(8,128)S(1)}, bf16[48,24]{1,0:T(8,128)(2,1)}, bf16[48,24]{1,0:T(8...) custom-call(f32[8,64]{1,0:T(8,128)S(1)} %get-tuple-element.17.facts_ref), custom_call_target="tpu_custom_call" | custom-call | flops 10000000 | bytes 100000 | tf_op jit(solution)/shard_map/home_body/pallas_call | solution.py:26
  26.7 6.8 %collective-permute-done.4.rest_1_ = bf16[96,1280]{1,0:T(8,128)(2,1)S(1)} collective-permute-done((bf16[96,1280]{1,0:T(8,128)(2,1)S(1)}, bf16[96,1280]{1,0:T(8,128)(2,1)S(1)}, u32[]{:S(2)}, u32[]{:S(2)}) %collective-permute-start.4) | collective-permute-done | bytes 245792 | tf_op jit(solution)/shard_map/ppermute | solution.py:419
  33.5 8.7 %collective-permute-done.5.rest_2_ = bf16[96,1280]{1,0:T(8,128)(2,1)S(1)} collective-permute-done((bf16[96,1280]{1,0:T(8,128)(2,1)S(1)}, bf16[96,1280]{1,0:T(8,128)(2,1)S(1)}, u32[]{:S(2)}, u32[]{:S(2)}) %collective-permute-start.5) | collective-permute-done | bytes 245792 | tf_op jit(solution)/shard_map/ppermute | solution.py:419
  42.2 5.9 %collective-permute-done.6.rest_3_ = bf16[96,1280]{1,0:T(8,128)(2,1)S(1)} collective-permute-done((bf16[96,1280]{1,0:T(8,128)(2,1)S(1)}, bf16[96,1280]{1,0:T(8,128)(2,1)S(1)}, u32[]{:S(2)}, u32[]{:S(2)}) %collective-permute-start.6) | collective-permute-done | bytes 245792 | tf_op jit(solution)/shard_map/ppermute | solution.py:419
  48.1 0.0 copy-done.2
  48.1 0.0 copy-done.1
  48.1 2.6 %attend_body.1 = bf16[48,2048]{1,0:T(8,128)(2,1)} custom-call(f32[48,128]{1,0:T(8,128)S(1)} %get-tuple-element.18.cos_ref, f32[48,128]{1,0:T(8,128)S(1)} %get-tuple-element.19.sin_ref, f32[16,256]{1,0:T(8,128)S(1)} %get-tuple-element.20.len_ref, bf16[16,2,256,128]{3,2,1,0:T(8,128)(2,1)S(1)} %copy-done.1, bf16[16,2,256,128]{3,2,1,0:T(8,128)(2,1)S(1)} %copy-done.2, ...), custom_call_target="tpu_custom_call" | custom-call | flops 100663296 | bytes 4194304 | tf_op jit(solution)/shard_map/attend_body/pallas_call | solution.py:26
  (6 shorter events, 0.0 us)
Async XLA Ops:
  2.2 12.8 %collective-permute-start = (bf16[96,2048]{1,0:T(8,128)(2,1)}, bf16[96,2048]{1,0:T(8,128)(2,1)S(1)}, u32[]{:S(2)}, u32[]{:S(2)}) collective-permute-start(bf16[96,2048]{1,0:T(8,128)(2,1)} %get-tuple-element.21), channel_id=1, source_target_pairs={{0,0},{1,12},{2,8},{3,4},{4,9},{5,5},{6,1},{7,13},{8,14},{9,6},{10... | collective-permute-start | bytes 1179656 | tf_op jit(solution)/shard_map/ppermute | solution.py:416
  5.2 1.1 %copy-start = (bf16[64,3,2048]{2,0,1:T(8,128)(2,1)S(1)}, bf16[64,3,2048]{2,0,1:T(8,128)(2,1)}, u32[]{:S(2)}) copy-start(bf16[64,3,2048]{2,0,1:T(8,128)(2,1)} %param.12) | copy-start | bytes 2359300
  6.3 1.2 %copy-start.3 = (bf16[2048,256]{1,0:T(8,128)(2,1)S(1)}, bf16[2048,256]{1,0:T(8,128)(2,1)}, u32[]{:S(2)}) copy-start(bf16[2048,256]{1,0:T(8,128)(2,1)} %k_ref.1) | copy-start | bytes 3145732
  7.5 1.2 %copy-start.4 = (bf16[2048,256]{1,0:T(8,128)(2,1)S(1)}, bf16[2048,256]{1,0:T(8,128)(2,1)}, u32[]{:S(2)}) copy-start(bf16[2048,256]{1,0:T(8,128)(2,1)} %v_ref.1) | copy-start | bytes 3145732
  8.7 0.7 %copy-start.8 = (f32[8,64]{1,0:T(8,128)S(1)}, f32[8,64]{1,0:T(8,128)}, u32[]{:S(2)}) copy-start(f32[8,64]{1,0:T(8,128)} %get-tuple-element.16.facts_ref) | copy-start | bytes 6148
  9.4 5.6 %copy-start.5 = (bf16[2,128,2048]{2,1,0:T(8,128)(2,1)S(1)}, bf16[2,128,2048]{2,1,0:T(8,128)(2,1)}, u32[]{:S(2)}) copy-start(bf16[2,128,2048]{2,1,0:T(8,128)(2,1)} %down_ref.1) | copy-start | bytes 3145732
  9.4 11.8 %copy-start.6 = (bf16[2,64,2048]{2,1,0:T(8,128)(2,1)S(1)}, bf16[2,64,2048]{2,1,0:T(8,128)(2,1)}, u32[]{:S(2)}) copy-start(bf16[2,64,2048]{2,1,0:T(8,128)(2,1)} %upq_ref.1) | copy-start | bytes 1572868
  9.4 11.8 %copy-start.7 = (bf16[2,64,256]{2,1,0:T(8,128)(2,1)S(1)}, bf16[2,64,256]{2,1,0:T(8,128)(2,1)}, u32[]{:S(2)}) copy-start(bf16[2,64,256]{2,1,0:T(8,128)(2,1)} %upv_ref.1) | copy-start | bytes 196612
  9.4 38.7 %copy-start.2 = (bf16[16,2,256,128]{3,2,1,0:T(8,128)(2,1)S(1)}, bf16[16,2,256,128]{3,2,1,0:T(8,128)(2,1)}, u32[]{:S(2)}) copy-start(bf16[16,2,256,128]{3,2,1,0:T(8,128)(2,1)} %vc_ref.1) | copy-start | bytes 6291460
  14.6 33.5 %copy-start.1 = (bf16[16,2,256,128]{3,2,1,0:T(8,128)(2,1)S(1)}, bf16[16,2,256,128]{3,2,1,0:T(8,128)(2,1)}, u32[]{:S(2)}) copy-start(bf16[16,2,256,128]{3,2,1,0:T(8,128)(2,1)} %kc_ref.1) | copy-start | bytes 6291460
  15.5 3.5 %collective-permute-start.3 = (bf16[96,128]{1,0:T(8,128)(2,1)S(1)}, bf16[96,128]{1,0:T(8,128)(2,1)S(1)}, u32[]{:S(2)}, u32[]{:S(2)}) collective-permute-start(bf16[96,128]{1,0:T(8,128)(2,1)S(1)} %shrink_body.1.rest_0_), channel_id=1, source_target_pairs={{0,3},{1,2},{2,1},{3,0},{4,7},{5,6},{6,5},{7,4},{8,11},{9,10},{10,... | collective-permute-start | bytes 73736 | tf_op jit(solution)/shard_map/ppermute | solution.py:470
  17.4 3.8 %collective-permute-start.2 = (bf16[96,128]{1,0:T(8,128)(2,1)S(1)}, bf16[96,128]{1,0:T(8,128)(2,1)S(1)}, u32[]{:S(2)}, u32[]{:S(2)}) collective-permute-start(bf16[96,128]{1,0:T(8,128)(2,1)S(1)} %shrink_body.1.rest_0_), channel_id=1, source_target_pairs={{0,2},{1,3},{2,0},{3,1},{4,6},{5,7},{6,4},{7,5},{8,10},{9,11},{10,... | collective-permute-start | bytes 73736 | tf_op jit(solution)/shard_map/ppermute | solution.py:470
  18.8 2.5 %collective-permute-start.1 = (bf16[96,128]{1,0:T(8,128)(2,1)S(1)}, bf16[96,128]{1,0:T(8,128)(2,1)S(1)}, u32[]{:S(2)}, u32[]{:S(2)}) collective-permute-start(bf16[96,128]{1,0:T(8,128)(2,1)S(1)} %shrink_body.1.rest_0_), channel_id=1, source_target_pairs={{0,1},{1,0},{2,3},{3,2},{4,5},{5,4},{6,7},{7,6},{8,9},{9,8},{10,11... | collective-permute-start | bytes 73736 | tf_op jit(solution)/shard_map/ppermute | solution.py:470
  22.4 11.2 %collective-permute-start.4 = (bf16[96,1280]{1,0:T(8,128)(2,1)S(1)}, bf16[96,1280]{1,0:T(8,128)(2,1)S(1)}, u32[]{:S(2)}, u32[]{:S(2)}) collective-permute-start(bf16[96,1280]{1,0:T(8,128)(2,1)S(1)} %get-tuple-element.24), channel_id=1, source_target_pairs={{0,4},{4,0},{8,12},{12,8},{1,5},{5,1},{9,13},{13,9},{2,6},{6,2},{1... | collective-permute-start | bytes 737288 | tf_op jit(solution)/shard_map/ppermute | solution.py:419
  24.0 18.2 %collective-permute-start.5 = (bf16[96,1280]{1,0:T(8,128)(2,1)S(1)}, bf16[96,1280]{1,0:T(8,128)(2,1)S(1)}, u32[]{:S(2)}, u32[]{:S(2)}) collective-permute-start(bf16[96,1280]{1,0:T(8,128)(2,1)S(1)} %get-tuple-element.25), channel_id=1, source_target_pairs={{0,8},{4,12},{8,0},{12,4},{1,9},{5,13},{9,1},{13,5},{2,10},{6,14},... | collective-permute-start | bytes 737288 | tf_op jit(solution)/shard_map/ppermute | solution.py:419
  25.4 22.7 %collective-permute-start.6 = (bf16[96,1280]{1,0:T(8,128)(2,1)S(1)}, bf16[96,1280]{1,0:T(8,128)(2,1)S(1)}, u32[]{:S(2)}, u32[]{:S(2)}) collective-permute-start(bf16[96,1280]{1,0:T(8,128)(2,1)S(1)} %get-tuple-element.26), channel_id=1, source_target_pairs={{0,12},{4,8},{8,4},{12,0},{1,13},{5,9},{9,5},{13,1},{2,14},{6,10},... | collective-permute-start | bytes 737288 | tf_op jit(solution)/shard_map/ppermute | solution.py:419

commit v4 on v3

--- a/solution.py
+++ b/solution.py
@@ -114,25 +114,7 @@
             out[s * places : (s + 1) * places] = nn(table, hid_ref[s]).astype(BF16)
 
 
-def project_early_body(home_rows, homes, heads, x_ref, q_ref, k_ref, v_ref, near_ref, far_ref, scr):
-    steps, rows = x_ref.shape[0] // (homes * home_rows), homes * home_rows
-    q_cols = q_ref.shape[1]
-    head_dim = k_ref.shape[1]
-    me = lax.axis_index("pool")
-    local_rows = steps * home_rows
-    base = pl.program_id(0) * 2 * local_rows
-    scr[:, :q_cols] = nn(x_ref[...], q_ref[...])
-    scr[:, q_cols : q_cols + head_dim] = nn(x_ref[...], k_ref[...])
-    scr[:, q_cols + head_dim :] = nn(x_ref[...], v_ref[...])
-    for out, ds in ((far_ref, (1, 3)), (near_ref, (0, 2))):
-        for n, d in enumerate(ds):
-            for s in range(steps):
-                begin = pl.multiple_of(s * rows + (me ^ d) * home_rows, home_rows)
-                there = pl.multiple_of(base + n * local_rows + s * home_rows, home_rows)
-                out[pl.ds(there, home_rows), :] = scr[pl.ds(begin, home_rows), :].astype(BF16)
-
-
-def project_late_body(x_ref, q_ref, k_ref, v_ref, facts_ref, out, facts_out):
+def project_body(x_ref, q_ref, k_ref, v_ref, facts_ref, out, facts_out):
     q_cols = q_ref.shape[1]
     head_dim = k_ref.shape[1]
     facts_out[...] = facts_ref[...]
@@ -145,13 +127,9 @@
     out_ref[...] = message_ref[...]
 
 
-def add_body(heads, near_ref, got_ref, out_ref):
-    rows = near_ref.shape[0] // (2 * heads)
-    for n in range(heads):
-        here = slice((2 * n + 1) * rows, (2 * n + 2) * rows)
-        out_ref[n * rows : (n + 1) * rows, :] = (
-            near_ref[here, :].astype(F32) + got_ref[here, :].astype(F32)
-        ).astype(BF16)
+def add_body(near_ref, got_ref, out_ref):
+    rows = near_ref.shape[1] // 2
+    out_ref[...] = (near_ref[:, rows:].astype(F32) + got_ref[:, rows:].astype(F32)).astype(BF16)
 
 
 def shrink_body(home_rows, cap, resident, parts, facts_ref, down_ref, *rest):
@@ -180,78 +158,56 @@
     out[...] = total.astype(BF16)
 
 
-def expand_body(home_rows, homes, cap, resident, early, late, facts_ref, upq_ref, upv_ref, *rest):
-    messages, rest, scr = rest[-1 - homes : -1], rest[: -1 - homes], rest[-1]
-    shares, partials = rest[:-1], rest[-1]
+def expand_body(home_rows, homes, heads, paired, features, facts_ref, upq_ref, upv_ref, *rest):
+    shares, partials, outs, scr = rest[:features], rest[features], rest[-1 - (2 if paired else homes) : -1], rest[-1]
     adapter_row, owner_row, slot_row = facts_ref[0:1], facts_ref[1:2], facts_ref[2:3]
     me = lax.axis_index("pool")
-    table = slot_table(owner_row, slot_row, me, home_rows, cap)
-    places, rows = table.shape
-    local = jnp.sum(jnp.where(table, adapter_row - (me * resident).astype(F32) + 1.0, 0.0), 1, keepdims=True) - 1.0
-    spread = table.astype(BF16)
+    resident, rank = upq_ref.shape[:2]
+    kv_heads, all_rows, width = partials.shape
+    rows = owner_row.shape[1]
+    steps = all_rows // rows
+    local_rows = steps * home_rows
     shrunk = shares[0][...].astype(F32)
     for share in shares[1:]:
         shrunk = shrunk + share[...].astype(F32)
-    steps = shrunk.shape[0] // places
-    local_rows = steps * home_rows
+    places = shrunk.shape[0] // steps
+    table = slot_table(owner_row, slot_row, me, home_rows, places // homes)
+    local = jnp.sum(jnp.where(table, adapter_row - (me * resident).astype(F32) + 1.0, 0.0), 1, keepdims=True) - 1.0
+    spread = table.astype(BF16)
     local = jnp.concatenate([local] * steps, 0)
-    rank = upq_ref.shape[1]
     low_q, low_v = shrunk[:, :rank], shrunk[:, rank:]
     masked_q = [jnp.where(local == float(a), low_q, 0.0).astype(BF16) for a in range(resident)]
     masked_v = [jnp.where(local == float(a), low_v, 0.0).astype(BF16) for a in range(resident)]
-    kv_heads = len(early) + len(late)
     width_q = upq_ref.shape[2] // kv_heads
     width_v = upv_ref.shape[2] // kv_heads
-
-    def up(h):
-        delta_q = delta_v = None
+    for at, h in enumerate(heads):
+        delta_q = delta_v = 0.0
         for a in range(resident):
-            term_q = nn(masked_q[a], upq_ref[a, :, h * width_q : (h + 1) * width_q])
-            term_v = nn(masked_v[a], upv_ref[a, :, h * width_v : (h + 1) * width_v])
-            delta_q = term_q if delta_q is None else delta_q + term_q
-            delta_v = term_v if delta_v is None else delta_v + term_v
-        return delta_q, delta_v
-
-    for n, h in enumerate(late):
-        delta_q, delta_v = up(h)
+            delta_q = delta_q + nn(masked_q[a], upq_ref[a, :, h * width_q : (h + 1) * width_q])
+            delta_v = delta_v + nn(masked_v[a], upv_ref[a, :, h * width_v : (h + 1) * width_v])
         for s in range(steps):
             here = slice(s * places, (s + 1) * places)
             there = slice(s * rows, (s + 1) * rows)
-            scr[there, :width_q] = partials[n, there, :width_q].astype(F32) + tn(spread, delta_q[here].astype(BF16))
-            scr[there, width_q : width_q + width_v] = partials[n, there, width_q : width_q + width_v].astype(F32)
-            scr[there, width_q + width_v :] = partials[n, there, width_q + width_v :].astype(F32) + tn(
-                spread, delta_v[here].astype(BF16)
-            )
+            middle, end = width_q, width_q + width_v
+            scr[there, :middle] = partials[h, there, :middle].astype(F32) + tn(spread, delta_q[here].astype(BF16))
+            scr[there, middle:end] = partials[h, there, middle:end].astype(F32)
+            scr[there, end:] = partials[h, there, end:].astype(F32) + tn(spread, delta_v[here].astype(BF16))
         for d in range(homes):
-            home = me ^ d
             for s in range(steps):
-                begin = pl.multiple_of(s * rows + home * home_rows, home_rows)
-                row = n * local_rows + s * home_rows
-                messages[d][row : row + home_rows, :] = scr[pl.ds(begin, home_rows), :].astype(BF16)
-    for n, h in enumerate(early):
-        delta_q, delta_v = up(h)
-        both = jnp.concatenate([delta_q, delta_v, jnp.zeros((steps * places, width_v), F32)], 1)
-        scr[: steps * places, :] = both
-        for d in range(homes):
-            home = me ^ d
-            pieces = []
-            for s in range(steps):
-                begin = pl.multiple_of(s * places + home * cap, cap)
-                pieces.append(scr[pl.ds(begin, cap), :])
-            row = len(late) * local_rows + n * steps * cap
-            messages[d][row : row + steps * cap, :] = jnp.concatenate(pieces, 0).astype(BF16)
-
-
-def home_body(home_rows, homes, cap, steps, facts_ref, cos_ref, sin_ref, len_ref, *places_out):
-    owner_row, slot_row, length_row = facts_ref[1:2], facts_ref[2:3], facts_ref[3:4]
+                begin = pl.multiple_of(s * rows + (me ^ d) * home_rows, home_rows)
+                row = s * home_rows + (d // 2 * local_rows if paired else 0)
+                out = outs[d % 2] if paired else outs[d]
+                out[at, row : row + home_rows, :] = scr[pl.ds(begin, home_rows), :].astype(BF16)
+
+
+def home_body(home_rows, facts_ref, cos_ref, sin_ref, len_ref):
+    length_row = facts_ref[3:4]
     me = lax.axis_index("pool")
     local_rows, head_dim = cos_ref.shape
     rows = facts_ref.shape[1]
     row, batch = iota((local_rows, rows), 0), iota((local_rows, rows), 1)
     mine = batch == me * home_rows + row % home_rows
     length = jnp.sum(jnp.where(mine, length_row, 0.0), 1, keepdims=True)
-    owner = jnp.sum(jnp.where(mine, owner_row, 0.0), 1, keepdims=True)
-    slot = jnp.sum(jnp.where(mine, slot_row, 0.0), 1, keepdims=True)
     len_ref[...] = jnp.broadcast_to(length[:home_rows], len_ref.shape)
     lane = iota((local_rows, head_dim), 1)
     step = iota((local_rows, head_dim), 0) // home_rows
@@ -260,47 +216,24 @@
     angle = (length + step.astype(F32)) * inverse_freq
     cos_ref[...] = jnp.cos(angle)
     sin_ref[...] = jnp.where(lane < half, -1.0, 1.0) * jnp.sin(angle)
-    place, local = iota((local_rows, steps * cap), 1), iota((local_rows, steps * cap), 0)
-    for d, out in enumerate(places_out):
-        out[...] = (
-            (owner == (me ^ d).astype(F32))
-            & (place // cap == local // home_rows)
-            & (slot == (place % cap).astype(F32))
-        ).astype(BF16)
-
-
-def attend_body(home_rows, homes, steps, early, late, cos_ref, sin_ref, len_ref, kc_ref, vc_ref, *rest):
-    spots, rest = rest[: homes if early else 0], rest[homes if early else 0 :]
-    early_sums, rest = rest[: 3 if early else 0], rest[3 if early else 0 :]
-    messages, (out, q_scr, new_scr, o_scr, total_scr) = rest[:homes], rest[homes:]
+
+
+def attend_body(home_rows, which, n_pieces, cos_ref, sin_ref, len_ref, kc_ref, vc_ref, *rest):
+    pieces, done, (out, q_scr, new_scr, o_scr, total_scr) = rest[:n_pieces], rest[n_pieces:-5], rest[-5:]
     local_rows, head_dim = cos_ref.shape
+    steps = local_rows // home_rows
     cached = kc_ref.shape[2]
-    heads = (messages[0].shape[1] - 2 * head_dim) // head_dim
+    kv_heads = len(which)
+    heads = q_scr.shape[0] // (kv_heads * local_rows)
     width_q = heads * head_dim
-    places = (messages[0].shape[0] - local_rows * len(late)) // max(1, len(early))
     scale = 1.0 / math.sqrt(head_dim)
     cos, sin = cos_ref[...], sin_ref[...]
-    kv_heads = len(early) + len(late)
 
     def rope(v):
         return v * cos + pltpu.roll(v, head_dim // 2, 1) * sin
 
-    def projected(h, begin, delta_begin):
-        columns = slice(begin, begin + head_dim)
-        if h in late:
-            row = late.index(h) * local_rows
-            pieces = [m[row : row + local_rows, columns] for m in messages]
-        else:
-            n = early.index(h)
-            near, got, far_sum = early_sums
-            here = slice(2 * n * local_rows, (2 * n + 1) * local_rows)
-            pieces = [near[here, columns], got[here, columns], far_sum[n * local_rows : (n + 1) * local_rows, columns]]
-        total = sum(piece.astype(F32) for piece in pieces)
-        if h in early and delta_begin is not None:
-            row = len(late) * local_rows + early.index(h) * places
-            columns = slice(delta_begin, delta_begin + head_dim)
-            total = total + sum(nn(spot[...], m[row : row + places, columns]) for spot, m in zip(spots, messages))
-        return total
+    def projected(h, begin):
+        return sum(piece[h, :local_rows, begin : begin + head_dim].astype(F32) for piece in pieces)
 
     row, col = iota((local_rows, local_rows), 0), iota((local_rows, local_rows), 1)
     live = (row % home_rows == col % home_rows) & (col // home_rows <= row // home_rows)
@@ -312,17 +245,17 @@
     }
     new_weights, values_new = {}, {}
     for h in range(kv_heads):
-        key_new = rope(projected(h, width_q, None)).astype(BF16)
-        values_new[h] = projected(h, width_q + head_dim, width_q).astype(BF16)
+        key_new = rope(projected(h, width_q)).astype(BF16)
+        values_new[h] = projected(h, width_q + head_dim).astype(BF16)
         for n in range(heads):
-            query = rope(projected(h, n * head_dim, n * head_dim)).astype(BF16)
+            query = rope(projected(h, n * head_dim)).astype(BF16)
             here = slice((h * heads + n) * local_rows, (h * heads + n + 1) * local_rows)
             q_scr[here, :] = query.astype(F32)
             weight = jnp.where(live, jnp.exp(nt(query, key_new) * scale), 0.0)
             new_weights[h, n] = weight
             new_scr[here, :] = jnp.broadcast_to(jnp.sum(weight, 1, keepdims=True), (local_rows, head_dim))
     for h in range(kv_heads):
-        scores = [nt(q_scr[mine[h, b], :].astype(BF16), kc_ref[b, h]) for b in range(home_rows)]
+        scores = [nt(q_scr[mine[h, b], :].astype(BF16), kc_ref[b, which[h]]) for b in range(home_rows)]
         probs = []
         for b in range(home_rows):
             weight = jnp.where(spot_ids < len_ref[b : b + 1, :], jnp.exp(scores[b] * scale), 0.0)
@@ -330,7 +263,7 @@
             total_scr[mine[h, b], :] = jnp.broadcast_to(total, (per_row, head_dim))
             probs.append((weight / total).astype(BF16))
         for b in range(home_rows):
-            o_scr[mine[h, b], :] = nn(probs[b], vc_ref[b, h])
+            o_scr[mine[h, b], :] = nn(probs[b], vc_ref[b, which[h]])
     for h in range(kv_heads):
         for n in range(heads):
             at = h * heads + n
@@ -339,6 +272,8 @@
             out[:, at * head_dim : (at + 1) * head_dim] = (
                 o_scr[here, :] + nn(prob, values_new[h])
             ).astype(BF16)
+    for piece in done:
+        out[:, kv_heads * width_q :] = piece[...]
 
 
 def on_device(
@@ -399,8 +334,7 @@
     rr, ra, ln = row_request.reshape(1, rows), request_adapter.reshape(1, rows), lengths.reshape(1, rows)
     by_step = hidden.transpose(1, 0, 2)
     x = by_step.reshape(steps * rows, slice_width)
-    early = ()
-    late = tuple(range(kv_here))
+    halved = kv_here // 2 if homes == 4 else 0
 
     *selected, facts = call(
         functools.partial(select_body, home_rows, cap, resident, owners),
@@ -428,25 +362,8 @@
             pl.BlockSpec((slice_width, head_dim), lambda i: (0, first + i)),
         ]
 
-    early_sums = ()
-    if early:
-        pair = shape((2 * local_rows * len(early), width), BF16)
-        near, far = call(
-            functools.partial(project_early_body, home_rows, homes, len(early)),
-            [pair] * 2,
-            weights,
-            limit=60,
-            in_specs=weight_specs(0),
-            out_specs=[pl.BlockSpec(pair.shape, lambda i: (0, 0))] * 2,
-            grid=(len(early),),
-            scratch=[pltpu.VMEM((steps * rows, width), F32)],
-            flops=2 * steps * rows * slice_width * width * len(early),
-            bytes_=2 * slice_width * width * len(early),
-        )
-        got = swap(far, 1)
-
     partials, facts = call(
-        project_late_body,
+        project_body,
         [shape((kv_here, steps * rows, width), BF16), shape(facts.shape, F32)],
         (*weights, facts),
         in_specs=weight_specs(0) + [pl.BlockSpec(facts.shape, lambda i: (0, 0))],
@@ -469,55 +386,62 @@
     shares = [share] + [
         lax.ppermute(share, FEATURE_AXES, [(i, i ^ d) for i in range(features)]) for d in range(1, features)
     ]
-    tables = call(
-        functools.partial(home_body, home_rows, homes, cap, steps),
-        [shape((local_rows, head_dim), F32)] * 2
-        + [shape((home_rows, cached), F32)]
-        + [shape((local_rows, steps * cap), BF16)] * homes,
+    cos, sin, length = call(
+        functools.partial(home_body, home_rows),
+        [shape((local_rows, head_dim), F32)] * 2 + [shape((home_rows, cached), F32)],
         (facts,),
         flops=10**7,
         bytes_=10**5,
     )
-    cos, sin, length, spots = tables[0], tables[1], tables[2], tables[3:]
-    if early:
-        far_sum = call(
-            functools.partial(add_body, len(early)),
-            shape((local_rows * len(early), width), BF16),
+    pair = shape((halved, 2 * local_rows, width), BF16)
+    message = shape((kv_here - halved, local_rows, width), BF16)
+
+    def expand(heads, paired, after):
+        kind = shape((len(heads), (2 if paired else 1) * local_rows, width), BF16)
+        return call(
+            functools.partial(expand_body, home_rows, homes, heads, paired, features),
+            [kind] * (2 if paired else homes),
+            (facts, adapter_up_query, adapter_up_value, *shares, partials, *after),
+            in_specs=[VMEM] * (4 + features) + [ANY] * len(after),
+            scratch=[pltpu.VMEM((steps * rows, width), F32)],
+            flops=2 * steps * places * rank * resident * q_cols * len(heads),
+            bytes_=2 * resident * rank * q_cols * len(heads),
+        )
+
+    direct = tuple(range(halved, kv_here))
+    messages = list(expand(direct, False, ()))
+    for d in range(2, homes):
+        messages[d] = swap(messages[d], d)
+    sums = ()
+    if halved:
+        near, far = expand(tuple(range(halved)), True, messages[:1])
+        got = swap(far, 1)
+        passed = call(
+            add_body,
+            shape((halved, local_rows, width), BF16),
             (near, got),
-            flops=local_rows * len(early) * width,
-            bytes_=6 * local_rows * len(early) * width,
+            flops=halved * local_rows * width,
+            bytes_=6 * halved * local_rows * width,
         )
-        early_sums = (near, got, swap(far_sum, 2))
-    message = shape((local_rows * len(late) + steps * cap * len(early), width), BF16)
-    messages = call(
-            functools.partial(expand_body, home_rows, homes, cap, resident, early, late),
-            [message] * homes,
-            (facts, adapter_up_query, adapter_up_value, *shares, partials),
-                        scratch=[pltpu.VMEM((max(rows, places) * steps, width), F32)],
-            flops=2 * steps * places * rank * resident * q_cols * kv_here,
-            bytes_=2 * resident * rank * q_cols * kv_here,
+        sums = (near, got, swap(passed, 2))
+        messages[1] = call(
+            pass_body, shape(messages[1].shape, BF16), (messages[1], messages[2]), in_specs=[VMEM, ANY]
         )
-    messages = list(messages)
-    if early:
-        messages[1] = call(pass_body, message, (messages[1], early_sums[2]), in_specs=[VMEM, ANY])
-    messages = [messages[0]] + [swap(messages[d], d) for d in range(1, homes)]
-    out = call(
-        functools.partial(attend_body, home_rows, homes, steps, early, late),
-        shape((local_rows, q_cols * kv_here), BF16),
-        (
-            cos,
-            sin,
-            length,
-            key_cache_rows,
-            value_cache_rows,
-            *(spots if early else ()),
-            *early_sums,
-            *messages,
-        ),
-        scratch=[pltpu.VMEM((kv_here * q_cols // head_dim * local_rows, head_dim), F32)] * 4,
-        flops=4 * local_rows * q_cols * kv_here * cached,
-        bytes_=4 * home_rows * cached * head_dim * kv_here,
-    )
+    messages[1] = swap(messages[1], 1)
+
+    def attend(heads, pieces, done):
+        return call(
+            functools.partial(attend_body, home_rows, heads, len(pieces)),
+            shape((local_rows, q_cols * (len(heads) + (len(direct) if done else 0))), BF16),
+            (cos, sin, length, key_cache_rows, value_cache_rows, *pieces, *done),
+            scratch=[pltpu.VMEM((len(heads) * q_cols // head_dim * local_rows, head_dim), F32)] * 4,
+            flops=4 * local_rows * q_cols * len(heads) * cached,
+            bytes_=4 * home_rows * cached * head_dim * len(heads),
+        )
+
+    out = attend(direct, messages, ())
+    if halved:
+        out = attend(tuple(range(halved)), sums, (out,))
     return out.reshape(steps, home_rows, q_cols * kv_here).transpose(1, 0, 2)
 
 

time: 51.1 us -> 49.1 us (0.961)
  the two profiles are of different devices: /device:TPU:8 before, /device:TPU:0 now
where the time goes in v4:
time: 49.1 us; the launch traced here: 48.8 us
  starting transfers between devices  18.7 us (38%)
  waiting for transfers between devices  13.4 us (27%)
  Pallas kernels  12.3 us (25%)
  local copies, waits for them, and re-layouts  4.29 us (9%)
    pallas_call x10, Pallas kernels, call(): pl.pallas_call(body, name=inner.__name__, out_shape=out_shape, in_specs=i...  12.3 us
    ppermute x5, waiting for transfers between devices, swap(): return lax.ppermute(value, 'pool', [(i, i ^ d) for i in range(homes)])  10.3 us
    ppermute x5, starting transfers between devices, swap(): return lax.ppermute(value, 'pool', [(i, i ^ d) for i in range(homes)])  10.2 us
    ppermute x3, starting transfers between devices, on_device(): lax.ppermute(share, FEATURE_AXES, [(i, i ^ d) for i in range(features)])  6.93 us
    unnamed x18, local copies, waits for them, and re-layouts  4.29 us
    ppermute x3, waiting for transfers between devices, on_device(): lax.ppermute(share, FEATURE_AXES, [(i, i ^ d) for i in range(features)])  3.02 us
    ppermute x1, starting transfers between devices, on_device(): lax.ppermute(s, ('pool', *FEATURE_AXES), perm)  1.65 us
  transfers between devices with their start and end apart: 9, of which 5 were waited for; matrix products, arithmetic and copies ran while one was open for 0% of the time, Pallas kernels for 13%

profile of v4, /device:TPU:0, one launch (start us, length us, event | category | flops | bytes accessed | tf_op | source)
XLA Modules:
  0.0 48.8 jit_solution(9589624586915288422)
XLA Ops:
  0.0 2.2 %select_body.1 = (bf16[96,2048]{1,0:T(8,128)(2,1)}, f32[8,64]{1,0:T(8,128)}) custom-call(s32[1,64]{1,0:T(1,128)} %bitcast.11, s32[1,64]{1,0:T(1,128)} %bitcast.12, s32[1,64]{1,0:T(1,128)} %bitcast.13, bf16[3,64,2048]{2,1,0:T(8,128)(2,1)} %bitcast.9), custom_call_target="tpu_custom_call" | custom-call | flops 25165824 | bytes 1179648 | tf_op jit(solution)/shard_map/select_body/pallas_call | solution.py:26
  2.2 1.7 %collective-permute-start = (bf16[96,2048]{1,0:T(8,128)(2,1)}, bf16[96,2048]{1,0:T(8,128)(2,1)S(1)}, u32[]{:S(2)}, u32[]{:S(2)}) collective-permute-start(bf16[96,2048]{1,0:T(8,128)(2,1)} %get-tuple-element.23), channel_id=1, source_target_pairs={{0,0},{1,12},{2,8},{3,4},{4,9},{5,5},{6,1},{7,13},{8,14},{9,6},{10... | collective-permute-start | bytes 1179656 | tf_op jit(solution)/shard_map/ppermute | solution.py:350
  3.9 1.1 %copy-done.2 = bf16[64,3,2048]{2,0,1:T(8,128)(2,1)S(1)} copy-done((bf16[64,3,2048]{2,0,1:T(8,128)(2,1)S(1)}, bf16[64,3,2048]{2,0,1:T(8,128)(2,1)}, u32[]{:S(2)}) %copy-start.2) | copy-done | bytes 786456
  5.0 1.2 %copy-done.4 = bf16[2048,256]{1,0:T(8,128)(2,1)S(1)} copy-done((bf16[2048,256]{1,0:T(8,128)(2,1)S(1)}, bf16[2048,256]{1,0:T(8,128)(2,1)}, u32[]{:S(2)}) %copy-start.4) | copy-done | bytes 1048600
  6.2 1.2 %copy-done.5 = bf16[2048,256]{1,0:T(8,128)(2,1)S(1)} copy-done((bf16[2048,256]{1,0:T(8,128)(2,1)S(1)}, bf16[2048,256]{1,0:T(8,128)(2,1)}, u32[]{:S(2)}) %copy-start.5) | copy-done | bytes 1048600
  7.5 0.7 %copy-done.8 = f32[8,64]{1,0:T(8,128)S(1)} copy-done((f32[8,64]{1,0:T(8,128)S(1)}, f32[8,64]{1,0:T(8,128)}, u32[]{:S(2)}) %copy-start.8) | copy-done | bytes 2072
  8.2 5.1 %project_body.1 = (bf16[2,192,1280]{2,1,0:T(8,128)(2,1)S(1)}, f32[8,64]{1,0:T(8,128)S(1)}) custom-call(bf16[192,2048]{1,0:T(8,128)(2,1)S(1)} %bitcast.10, bf16[2048,2048]{1,0:T(8,128)(2,1)} %q_ref.1, bf16[2048,256]{1,0:T(8,128)(2,1)S(1)} %copy-done.4, bf16[2048,256]{1,0:T(8,128)(2,1)S(1)} %copy-done.5, f32[8,64]{1,0:T(8,128)S(1)} %copy-done.8), custom_call_target="tpu_custom_call" | custom-call | flops 2013265920 | bytes 10485760 | tf_op jit(solution)/shard_map/project_body/pallas_call | solution.py:26
  13.3 0.0 collective-permute-done.rest_0_
  13.3 0.0 copy-done.6
  13.3 0.5 shrink_body.1.rest_0_
  13.8 5.5 %collective-permute-start.1 = (bf16[96,128]{1,0:T(8,128)(2,1)S(1)}, bf16[96,128]{1,0:T(8,128)(2,1)S(1)}, u32[]{:S(2)}, u32[]{:S(2)}) collective-permute-start(bf16[96,128]{1,0:T(8,128)(2,1)S(1)} %shrink_body.1.rest_0_), channel_id=1, source_target_pairs={{0,1},{1,0},{2,3},{3,2},{4,5},{5,4},{6,7},{7,6},{8,9},{9,8},{10,11... | collective-permute-start | bytes 73736 | tf_op jit(solution)/shard_map/ppermute | solution.py:387
  19.3 1.1 %collective-permute-start.2 = (bf16[96,128]{1,0:T(8,128)(2,1)S(1)}, bf16[96,128]{1,0:T(8,128)(2,1)S(1)}, u32[]{:S(2)}, u32[]{:S(2)}) collective-permute-start(bf16[96,128]{1,0:T(8,128)(2,1)S(1)} %shrink_body.1.rest_0_), channel_id=1, source_target_pairs={{0,2},{1,3},{2,0},{3,1},{4,6},{5,7},{6,4},{7,5},{8,10},{9,11},{10,... | collective-permute-start | bytes 73736 | tf_op jit(solution)/shard_map/ppermute | solution.py:387
  20.4 0.3 collective-permute-start.3
  20.7 0.0 collective-permute-done.1.rest_1_
  20.7 2.4 %collective-permute-done.2.rest_2_ = bf16[96,128]{1,0:T(8,128)(2,1)S(1)} collective-permute-done((bf16[96,128]{1,0:T(8,128)(2,1)S(1)}, bf16[96,128]{1,0:T(8,128)(2,1)S(1)}, u32[]{:S(2)}, u32[]{:S(2)}) %collective-permute-start.2) | collective-permute-done | bytes 24608 | tf_op jit(solution)/shard_map/ppermute | solution.py:387
  23.1 0.6 %collective-permute-done.3.rest_3_ = bf16[96,128]{1,0:T(8,128)(2,1)S(1)} collective-permute-done((bf16[96,128]{1,0:T(8,128)(2,1)S(1)}, bf16[96,128]{1,0:T(8,128)(2,1)S(1)}, u32[]{:S(2)}, u32[]{:S(2)}) %collective-permute-start.3) | collective-permute-done | bytes 24608 | tf_op jit(solution)/shard_map/ppermute | solution.py:387
  23.7 0.0 copy-done.7
  23.8 0.7 %expand_body.2 = (bf16[1,48,1280]{2,1,0:T(8,128)(2,1)S(1)}, bf16[1,48,1280]{2,1,0:T(8,128)(2,1)S(1)}, bf16[1,48,1280]{2,1,0:T(8,128)(2,1)S(1)}, bf16[1,48,1280]{2,1,0:T(8,128)(2,1)S(1)}) custom-call(f32[8,64]{1,0:T(8,128)S(1)} %get-tuple-element.19.facts_ref, bf16[2,64,2048]{2,1,0:T(8,128)(2,1)S(1)} %copy-done.3, bf16[2,64,256]{2,1,0:T(8,128)(2,1)S(1)} %copy-done.7, ...), custom_call_target="tpu_custom_call" | custom-call | flops 25165824 | bytes 262144 | tf_op jit(solution)/shard_map/expand_body/pallas_call | solution.py:26
  24.5 0.7 %expand_body.3 = (bf16[1,96,1280]{2,1,0:T(8,128)(2,1)S(1)}, bf16[1,96,1280]{2,1,0:T(8,128)(2,1)S(1)}) custom-call(f32[8,64]{1,0:T(8,128)S(1)} %get-tuple-element.19.facts_ref, bf16[2,64,2048]{2,1,0:T(8,128)(2,1)S(1)} %copy-done.3, bf16[2,64,256]{2,1,0:T(8,128)(2,1)S(1)} %copy-done.7, bf16[96,128]{1,0:T(8,128)(2,1)S(1)} %shrink_body.1.rest_0_, ...), custom_call_target="tpu_custom_call" | custom-call | flops 25165824 | bytes 262144 | tf_op jit(solution)/shard_map/expand_body/pallas_call | solution.py:26
  25.2 1.4 %collective-permute-start.4 = (bf16[1,96,1280]{2,1,0:T(8,128)(2,1)S(1)}, bf16[1,96,1280]{2,1,0:T(8,128)(2,1)S(1)}, u32[]{:S(2)}, u32[]{:S(2)}) collective-permute-start(bf16[1,96,1280]{2,1,0:T(8,128)(2,1)S(1)} %get-tuple-element.27), channel_id=1, source_target_pairs={{0,4},{4,0},{8,12},{12,8},{1,5},{5,1},{9,13},{13,9},{2,6},{6,2},{1... | collective-permute-start | bytes 737288 | tf_op jit(solution)/shard_map/ppermute | solution.py:353
  26.5 3.2 %collective-permute-start.6 = (bf16[1,48,1280]{2,1,0:T(8,128)(2,1)S(1)}, bf16[1,48,1280]{2,1,0:T(8,128)(2,1)S(1)}, u32[]{:S(2)}, u32[]{:S(2)}) collective-permute-start(bf16[1,48,1280]{2,1,0:T(8,128)(2,1)S(1)} %get-tuple-element.29), channel_id=1, source_target_pairs={{0,8},{4,12},{8,0},{12,4},{1,9},{5,13},{9,1},{13,5},{2,10},{6,14},... | collective-permute-start | bytes 368648 | tf_op jit(solution)/shard_map/ppermute | solution.py:353
  29.7 0.0 collective-permute-start.8
  29.7 5.8 %collective-permute-done.6._.rest_2_ = bf16[1,48,1280]{2,1,0:T(8,128)(2,1)S(1)} collective-permute-done((bf16[1,48,1280]{2,1,0:T(8,128)(2,1)S(1)}, bf16[1,48,1280]{2,1,0:T(8,128)(2,1)S(1)}, u32[]{:S(2)}, u32[]{:S(2)}) %collective-permute-start.6) | collective-permute-done | bytes 122912 | tf_op jit(solution)/shard_map/ppermute | solution.py:353
  35.5 3.7 %collective-permute-start.7 = (bf16[1,48,1280]{2,1,0:T(8,128)(2,1)S(1)}, bf16[1,48,1280]{2,1,0:T(8,128)(2,1)S(1)}, u32[]{:S(2)}, u32[]{:S(2)}) collective-permute-start(bf16[1,48,1280]{2,1,0:T(8,128)(2,1)S(1)} %pass_body.1), channel_id=1, source_target_pairs={{0,4},{4,0},{8,12},{12,8},{1,5},{5,1},{9,13},{13,9},{2,6},{6,2},{1... | collective-permute-start | bytes 368648 | tf_op jit(solution)/shard_map/ppermute | solution.py:353
  39.3 0.0 collective-permute-done.4.got_ref.rest_1_
  39.3 1.9 %collective-permute-start.5 = (bf16[1,48,1280]{2,1,0:T(8,128)(2,1)S(1)}, bf16[1,48,1280]{2,1,0:T(8,128)(2,1)S(1)}, u32[]{:S(2)}, u32[]{:S(2)}) collective-permute-start(bf16[1,48,1280]{2,1,0:T(8,128)(2,1)S(1)} %add_body.1), channel_id=1, source_target_pairs={{0,8},{4,12},{8,0},{12,4},{1,9},{5,13},{9,1},{13,5},{2,10},{6,14},... | collective-permute-start | bytes 368648 | tf_op jit(solution)/shard_map/ppermute | solution.py:353
  41.2 0.2 home_body.1
  41.4 0.0 collective-permute-done.8.rest_3_
  41.4 3.7 %collective-permute-done.7.rest_1_ = bf16[1,48,1280]{2,1,0:T(8,128)(2,1)S(1)} collective-permute-done((bf16[1,48,1280]{2,1,0:T(8,128)(2,1)S(1)}, bf16[1,48,1280]{2,1,0:T(8,128)(2,1)S(1)}, u32[]{:S(2)}, u32[]{:S(2)}) %collective-permute-start.7) | collective-permute-done | bytes 122912 | tf_op jit(solution)/shard_map/ppermute | solution.py:353
  45.1 1.1 %attend_body.2.rest_3_ = bf16[48,1024]{1,0:T(8,128)(2,1)S(1)} custom-call(f32[48,128]{1,0:T(8,128)S(1)} %get-tuple-element.20.cos_ref, f32[48,128]{1,0:T(8,128)S(1)} %get-tuple-element.21.sin_ref, f32[16,256]{1,0:T(8,128)S(1)} %get-tuple-element.22.len_ref, bf16[16,2,256,128]{3,2,1,0:T(8,128)(2,1)S(1)} %copy-done, bf16[16,2,256,128]{3,2,1,0:T(8,128)(2,1)S(1)} %copy-done.1, ...), custom_call_target="tpu_custom_call" | custom-call | flops 50331648 | bytes 2097152 | tf_op jit(solution)/shard_map/attend_body/pallas_call | solution.py:26
  46.2 0.8 %collective-permute-done.5.rest_2_ = bf16[1,48,1280]{2,1,0:T(8,128)(2,1)S(1)} collective-permute-done((bf16[1,48,1280]{2,1,0:T(8,128)(2,1)S(1)}, bf16[1,48,1280]{2,1,0:T(8,128)(2,1)S(1)}, u32[]{:S(2)}, u32[]{:S(2)}) %collective-permute-start.5) | collective-permute-done | bytes 122912 | tf_op jit(solution)/shard_map/ppermute | solution.py:353
  47.0 1.8 %attend_body.3 = bf16[48,2048]{1,0:T(8,128)(2,1)} custom-call(f32[48,128]{1,0:T(8,128)S(1)} %get-tuple-element.20.cos_ref, f32[48,128]{1,0:T(8,128)S(1)} %get-tuple-element.21.sin_ref, f32[16,256]{1,0:T(8,128)S(1)} %get-tuple-element.22.len_ref, bf16[16,2,256,128]{3,2,1,0:T(8,128)(2,1)S(1)} %copy-done, bf16[16,2,256,128]{3,2,1,0:T(8,128)(2,1)S(1)} %copy-done.1, ...), custom_call_target="tpu_custom_call" | custom-call | flops 50331648 | bytes 2097152 | tf_op jit(solution)/shard_map/attend_body/pallas_call | solution.py:26
  (14 shorter events, 0.1 us)
Async XLA Ops:
  2.2 11.1 %collective-permute-start = (bf16[96,2048]{1,0:T(8,128)(2,1)}, bf16[96,2048]{1,0:T(8,128)(2,1)S(1)}, u32[]{:S(2)}, u32[]{:S(2)}) collective-permute-start(bf16[96,2048]{1,0:T(8,128)(2,1)} %get-tuple-element.23), channel_id=1, source_target_pairs={{0,0},{1,12},{2,8},{3,4},{4,9},{5,5},{6,1},{7,13},{8,14},{9,6},{10... | collective-permute-start | bytes 1179656 | tf_op jit(solution)/shard_map/ppermute | solution.py:350
  3.9 1.1 %copy-start.2 = (bf16[64,3,2048]{2,0,1:T(8,128)(2,1)S(1)}, bf16[64,3,2048]{2,0,1:T(8,128)(2,1)}, u32[]{:S(2)}) copy-start(bf16[64,3,2048]{2,0,1:T(8,128)(2,1)} %param.12) | copy-start | bytes 2359300
  5.0 1.2 %copy-start.4 = (bf16[2048,256]{1,0:T(8,128)(2,1)S(1)}, bf16[2048,256]{1,0:T(8,128)(2,1)}, u32[]{:S(2)}) copy-start(bf16[2048,256]{1,0:T(8,128)(2,1)} %k_ref.1) | copy-start | bytes 3145732
  6.2 1.2 %copy-start.5 = (bf16[2048,256]{1,0:T(8,128)(2,1)S(1)}, bf16[2048,256]{1,0:T(8,128)(2,1)}, u32[]{:S(2)}) copy-start(bf16[2048,256]{1,0:T(8,128)(2,1)} %v_ref.1) | copy-start | bytes 3145732
  7.5 0.7 %copy-start.8 = (f32[8,64]{1,0:T(8,128)S(1)}, f32[8,64]{1,0:T(8,128)}, u32[]{:S(2)}) copy-start(f32[8,64]{1,0:T(8,128)} %get-tuple-element.18.facts_ref) | copy-start | bytes 6148
  8.2 5.2 %copy-start.6 = (bf16[2,128,2048]{2,1,0:T(8,128)(2,1)S(1)}, bf16[2,128,2048]{2,1,0:T(8,128)(2,1)}, u32[]{:S(2)}) copy-start(bf16[2,128,2048]{2,1,0:T(8,128)(2,1)} %down_ref.1) | copy-start | bytes 3145732
  8.2 15.6 %copy-start.3 = (bf16[2,64,2048]{2,1,0:T(8,128)(2,1)S(1)}, bf16[2,64,2048]{2,1,0:T(8,128)(2,1)}, u32[]{:S(2)}) copy-start(bf16[2,64,2048]{2,1,0:T(8,128)(2,1)} %upq_ref.3) | copy-start | bytes 1572868
  8.2 15.6 %copy-start.7 = (bf16[2,64,256]{2,1,0:T(8,128)(2,1)S(1)}, bf16[2,64,256]{2,1,0:T(8,128)(2,1)}, u32[]{:S(2)}) copy-start(bf16[2,64,256]{2,1,0:T(8,128)(2,1)} %upv_ref.3) | copy-start | bytes 196612
  13.8 6.9 %collective-permute-start.1 = (bf16[96,128]{1,0:T(8,128)(2,1)S(1)}, bf16[96,128]{1,0:T(8,128)(2,1)S(1)}, u32[]{:S(2)}, u32[]{:S(2)}) collective-permute-start(bf16[96,128]{1,0:T(8,128)(2,1)S(1)} %shrink_body.1.rest_0_), channel_id=1, source_target_pairs={{0,1},{1,0},{2,3},{3,2},{4,5},{5,4},{6,7},{7,6},{8,9},{9,8},{10,11... | collective-permute-start | bytes 73736 | tf_op jit(solution)/shard_map/ppermute | solution.py:387
  19.3 3.8 %collective-permute-start.2 = (bf16[96,128]{1,0:T(8,128)(2,1)S(1)}, bf16[96,128]{1,0:T(8,128)(2,1)S(1)}, u32[]{:S(2)}, u32[]{:S(2)}) collective-permute-start(bf16[96,128]{1,0:T(8,128)(2,1)S(1)} %shrink_body.1.rest_0_), channel_id=1, source_target_pairs={{0,2},{1,3},{2,0},{3,1},{4,6},{5,7},{6,4},{7,5},{8,10},{9,11},{10,... | collective-permute-start | bytes 73736 | tf_op jit(solution)/shard_map/ppermute | solution.py:387
  20.4 3.3 %collective-permute-start.3 = (bf16[96,128]{1,0:T(8,128)(2,1)S(1)}, bf16[96,128]{1,0:T(8,128)(2,1)S(1)}, u32[]{:S(2)}, u32[]{:S(2)}) collective-permute-start(bf16[96,128]{1,0:T(8,128)(2,1)S(1)} %shrink_body.1.rest_0_), channel_id=1, source_target_pairs={{0,3},{1,2},{2,1},{3,0},{4,7},{5,6},{6,5},{7,4},{8,11},{9,10},{10,... | collective-permute-start | bytes 73736 | tf_op jit(solution)/shard_map/ppermute | solution.py:387
  23.8 21.3 %copy-start = (bf16[16,2,256,128]{3,2,1,0:T(8,128)(2,1)S(1)}, bf16[16,2,256,128]{3,2,1,0:T(8,128)(2,1)}, u32[]{:S(2)}) copy-start(bf16[16,2,256,128]{3,2,1,0:T(8,128)(2,1)} %kc_ref.3) | copy-start | bytes 6291460
  23.8 21.3 %copy-start.1 = (bf16[16,2,256,128]{3,2,1,0:T(8,128)(2,1)S(1)}, bf16[16,2,256,128]{3,2,1,0:T(8,128)(2,1)}, u32[]{:S(2)}) copy-start(bf16[16,2,256,128]{3,2,1,0:T(8,128)(2,1)} %vc_ref.3) | copy-start | bytes 6291460
  25.2 14.1 %collective-permute-start.4 = (bf16[1,96,1280]{2,1,0:T(8,128)(2,1)S(1)}, bf16[1,96,1280]{2,1,0:T(8,128)(2,1)S(1)}, u32[]{:S(2)}, u32[]{:S(2)}) collective-permute-start(bf16[1,96,1280]{2,1,0:T(8,128)(2,1)S(1)} %get-tuple-element.27), channel_id=1, source_target_pairs={{0,4},{4,0},{8,12},{12,8},{1,5},{5,1},{9,13},{13,9},{2,6},{6,2},{1... | collective-permute-start | bytes 737288 | tf_op jit(solution)/shard_map/ppermute | solution.py:353
  26.5 9.0 %collective-permute-start.6 = (bf16[1,48,1280]{2,1,0:T(8,128)(2,1)S(1)}, bf16[1,48,1280]{2,1,0:T(8,128)(2,1)S(1)}, u32[]{:S(2)}, u32[]{:S(2)}) collective-permute-start(bf16[1,48,1280]{2,1,0:T(8,128)(2,1)S(1)} %get-tuple-element.29), channel_id=1, source_target_pairs={{0,8},{4,12},{8,0},{12,4},{1,9},{5,13},{9,1},{13,5},{2,10},{6,14},... | collective-permute-start | bytes 368648 | tf_op jit(solution)/shard_map/ppermute | solution.py:353
  29.7 11.7 %collective-permute-start.8 = (bf16[1,48,1280]{2,1,0:T(8,128)(2,1)S(1)}, bf16[1,48,1280]{2,1,0:T(8,128)(2,1)S(1)}, u32[]{:S(2)}, u32[]{:S(2)}) collective-permute-start(bf16[1,48,1280]{2,1,0:T(8,128)(2,1)S(1)} %get-tuple-element.30), channel_id=1, source_target_pairs={{0,12},{4,8},{8,4},{12,0},{1,13},{5,9},{9,5},{13,1},{2,14},{6,10},... | collective-permute-start | bytes 368648 | tf_op jit(solution)/shard_map/ppermute | solution.py:353
  35.5 9.6 %collective-permute-start.7 = (bf16[1,48,1280]{2,1,0:T(8,128)(2,1)S(1)}, bf16[1,48,1280]{2,1,0:T(8,128)(2,1)S(1)}, u32[]{:S(2)}, u32[]{:S(2)}) collective-permute-start(bf16[1,48,1280]{2,1,0:T(8,128)(2,1)S(1)} %pass_body.1), channel_id=1, source_target_pairs={{0,4},{4,0},{8,12},{12,8},{1,5},{5,1},{9,13},{13,9},{2,6},{6,2},{1... | collective-permute-start | bytes 368648 | tf_op jit(solution)/shard_map/ppermute | solution.py:353
  39.3 7.7 %collective-permute-start.5 = (bf16[1,48,1280]{2,1,0:T(8,128)(2,1)S(1)}, bf16[1,48,1280]{2,1,0:T(8,128)(2,1)S(1)}, u32[]{:S(2)}, u32[]{:S(2)}) collective-permute-start(bf16[1,48,1280]{2,1,0:T(8,128)(2,1)S(1)} %add_body.1), channel_id=1, source_target_pairs={{0,8},{4,12},{8,0},{12,4},{1,9},{5,13},{9,1},{13,5},{2,10},{6,14},... | collective-permute-start | bytes 368648 | tf_op jit(solution)/shard_map/ppermute | solution.py:353

commit v5 on v4

--- a/solution.py
+++ b/solution.py
@@ -12,7 +12,7 @@
 BF16 = jnp.bfloat16
 F32 = jnp.float32
 FEATURE_AXES = ("tp", "sub")
-CARRIER = ((0, 3, 2, 1), (2, 1, 0, 3), (3, 1, 2, 0), (1, 2, 0, 3))
+CARRIER = ((0, 3, 2, 1), (2, 1, 0, 3), (3, 1, 0, 2), (1, 2, 0, 3))
 
 
 def call(body, out_shape, args, in_specs=None, out_specs=None, grid=None, scratch=(), flops=0, bytes_=0, limit=40, **more):
@@ -158,8 +158,12 @@
     out[...] = total.astype(BF16)
 
 
-def expand_body(home_rows, homes, heads, paired, features, facts_ref, upq_ref, upv_ref, *rest):
-    shares, partials, outs, scr = rest[:features], rest[features], rest[-1 - (2 if paired else homes) : -1], rest[-1]
+def expand_body(home_rows, homes, halved, facts_ref, upq_ref, upv_ref, *rest):
+    scr, rest = rest[-1], rest[:-1]
+    messages, rest = rest[len(rest) - homes :], rest[: len(rest) - homes]
+    if halved:
+        (near_ref, far_ref), rest = rest[-2:], rest[:-2]
+    shares, partials = rest[:-1], rest[-1]
     adapter_row, owner_row, slot_row = facts_ref[0:1], facts_ref[1:2], facts_ref[2:3]
     me = lax.axis_index("pool")
     resident, rank = upq_ref.shape[:2]
@@ -180,7 +184,7 @@
     masked_v = [jnp.where(local == float(a), low_v, 0.0).astype(BF16) for a in range(resident)]
     width_q = upq_ref.shape[2] // kv_heads
     width_v = upv_ref.shape[2] // kv_heads
-    for at, h in enumerate(heads):
+    for h in range(kv_heads):
         delta_q = delta_v = 0.0
         for a in range(resident):
             delta_q = delta_q + nn(masked_q[a], upq_ref[a, :, h * width_q : (h + 1) * width_q])
@@ -195,8 +199,11 @@
         for d in range(homes):
             for s in range(steps):
                 begin = pl.multiple_of(s * rows + (me ^ d) * home_rows, home_rows)
-                row = s * home_rows + (d // 2 * local_rows if paired else 0)
-                out = outs[d % 2] if paired else outs[d]
+                row = s * home_rows
+                if h < halved:
+                    out, at, row = (far_ref if d % 2 else near_ref), h, row + d // 2 * local_rows
+                else:
+                    out, at = messages[d], h - halved
                 out[at, row : row + home_rows, :] = scr[pl.ds(begin, home_rows), :].astype(BF16)
 
 
@@ -396,25 +403,22 @@
     pair = shape((halved, 2 * local_rows, width), BF16)
     message = shape((kv_here - halved, local_rows, width), BF16)
 
-    def expand(heads, paired, after):
-        kind = shape((len(heads), (2 if paired else 1) * local_rows, width), BF16)
-        return call(
-            functools.partial(expand_body, home_rows, homes, heads, paired, features),
-            [kind] * (2 if paired else homes),
-            (facts, adapter_up_query, adapter_up_value, *shares, partials, *after),
-            in_specs=[VMEM] * (4 + features) + [ANY] * len(after),
-            scratch=[pltpu.VMEM((steps * rows, width), F32)],
-            flops=2 * steps * places * rank * resident * q_cols * len(heads),
-            bytes_=2 * resident * rank * q_cols * len(heads),
-        )
-
     direct = tuple(range(halved, kv_here))
-    messages = list(expand(direct, False, ()))
+    pair = shape((halved, 2 * local_rows, width), BF16)
+    grown = call(
+        functools.partial(expand_body, home_rows, homes, halved),
+        [pair] * (2 if halved else 0) + [shape((len(direct), local_rows, width), BF16)] * homes,
+        (facts, adapter_up_query, adapter_up_value, *shares, partials),
+        scratch=[pltpu.VMEM((steps * rows, width), F32)],
+        flops=2 * steps * places * rank * resident * q_cols * kv_here,
+        bytes_=2 * resident * rank * q_cols * kv_here,
+    )
+    messages = list(grown[-homes:])
     for d in range(2, homes):
         messages[d] = swap(messages[d], d)
     sums = ()
     if halved:
-        near, far = expand(tuple(range(halved)), True, messages[:1])
+        near, far = grown[:2]
         got = swap(far, 1)
         passed = call(
             add_body,

time: 49.1 us -> 47.5 us (0.967)
  starting transfers between devices: 18.7 us -> 17.1 us
    ppermute x5, starting transfers between devices: 10.2 us -> 8.28 us  [swap(): return lax.ppermute(value, 'pool', [(i, i ^ d) for i in range(homes)])]
    ppermute x5, waiting for transfers between devices: 10.3 us -> 10.9 us  [swap(): return lax.ppermute(value, 'pool', [(i, i ^ d) for i in range(homes)])]
    pallas_call x10 -> x9, Pallas kernels: 12.3 us -> 12 us  [call(): pl.pallas_call(body, name=inner.__name__, out_shape=out_shape, in_specs=i...]
  transfers between devices with their start and end apart: 9 -> 9, of which waited for: 5 -> 6; matrix products, arithmetic and copies ran while one was open for 0% -> 0% of each run, Pallas kernels for 13% -> 14%
where the time goes in v5:
time: 47.5 us; the launch traced here: 47.2 us
  starting transfers between devices  17.1 us (36%)
  waiting for transfers between devices  13.7 us (29%)
  Pallas kernels  12 us (25%)
  local copies, waits for them, and re-layouts  4.29 us (9%)
    pallas_call x9, Pallas kernels, call(): pl.pallas_call(body, name=inner.__name__, out_shape=out_shape, in_specs=i...  12 us
    ppermute x5, waiting for transfers between devices, swap(): return lax.ppermute(value, 'pool', [(i, i ^ d) for i in range(homes)])  10.9 us
    ppermute x5, starting transfers between devices, swap(): return lax.ppermute(value, 'pool', [(i, i ^ d) for i in range(homes)])  8.28 us
    ppermute x3, starting transfers between devices, on_device(): lax.ppermute(share, FEATURE_AXES, [(i, i ^ d) for i in range(features)])  7.13 us
    unnamed x18, local copies, waits for them, and re-layouts  4.29 us
    ppermute x3, waiting for transfers between devices, on_device(): lax.ppermute(share, FEATURE_AXES, [(i, i ^ d) for i in range(features)])  2.85 us
    ppermute x1, starting transfers between devices, on_device(): lax.ppermute(s, ('pool', *FEATURE_AXES), perm)  1.65 us
  transfers between devices with their start and end apart: 9, of which 6 were waited for; matrix products, arithmetic and copies ran while one was open for 0% of the time, Pallas kernels for 14%

profile of v5, /device:TPU:0, one launch (start us, length us, event | category | flops | bytes accessed | tf_op | source)
XLA Modules:
  0.0 47.2 jit_solution(14093090841439524808)
XLA Ops:
  0.0 2.2 %select_body.1 = (bf16[96,2048]{1,0:T(8,128)(2,1)}, f32[8,64]{1,0:T(8,128)}) custom-call(s32[1,64]{1,0:T(1,128)} %bitcast.11, s32[1,64]{1,0:T(1,128)} %bitcast.12, s32[1,64]{1,0:T(1,128)} %bitcast.13, bf16[3,64,2048]{2,1,0:T(8,128)(2,1)} %bitcast.9), custom_call_target="tpu_custom_call" | custom-call | flops 25165824 | bytes 1179648 | tf_op jit(solution)/shard_map/select_body/pallas_call | solution.py:26
  2.2 1.7 %collective-permute-start = (bf16[96,2048]{1,0:T(8,128)(2,1)}, bf16[96,2048]{1,0:T(8,128)(2,1)S(1)}, u32[]{:S(2)}, u32[]{:S(2)}) collective-permute-start(bf16[96,2048]{1,0:T(8,128)(2,1)} %get-tuple-element.23), channel_id=1, source_target_pairs={{0,0},{1,12},{2,8},{3,4},{4,9},{5,5},{6,1},{7,13},{8,10},{9,6},{10... | collective-permute-start | bytes 1179656 | tf_op jit(solution)/shard_map/ppermute | solution.py:357
  3.9 1.1 %copy-done.2 = bf16[64,3,2048]{2,0,1:T(8,128)(2,1)S(1)} copy-done((bf16[64,3,2048]{2,0,1:T(8,128)(2,1)S(1)}, bf16[64,3,2048]{2,0,1:T(8,128)(2,1)}, u32[]{:S(2)}) %copy-start.2) | copy-done | bytes 786456
  5.0 1.2 %copy-done.3 = bf16[2048,256]{1,0:T(8,128)(2,1)S(1)} copy-done((bf16[2048,256]{1,0:T(8,128)(2,1)S(1)}, bf16[2048,256]{1,0:T(8,128)(2,1)}, u32[]{:S(2)}) %copy-start.3) | copy-done | bytes 1048600
  6.2 1.2 %copy-done.4 = bf16[2048,256]{1,0:T(8,128)(2,1)S(1)} copy-done((bf16[2048,256]{1,0:T(8,128)(2,1)S(1)}, bf16[2048,256]{1,0:T(8,128)(2,1)}, u32[]{:S(2)}) %copy-start.4) | copy-done | bytes 1048600
  7.5 0.7 %copy-done.8 = f32[8,64]{1,0:T(8,128)S(1)} copy-done((f32[8,64]{1,0:T(8,128)S(1)}, f32[8,64]{1,0:T(8,128)}, u32[]{:S(2)}) %copy-start.8) | copy-done | bytes 2072
  8.2 5.2 %project_body.1 = (bf16[2,192,1280]{2,1,0:T(8,128)(2,1)S(1)}, f32[8,64]{1,0:T(8,128)S(1)}) custom-call(bf16[192,2048]{1,0:T(8,128)(2,1)S(1)} %bitcast.10, bf16[2048,2048]{1,0:T(8,128)(2,1)} %q_ref.1, bf16[2048,256]{1,0:T(8,128)(2,1)S(1)} %copy-done.3, bf16[2048,256]{1,0:T(8,128)(2,1)S(1)} %copy-done.4, f32[8,64]{1,0:T(8,128)S(1)} %copy-done.8), custom_call_target="tpu_custom_call" | custom-call | flops 2013265920 | bytes 10485760 | tf_op jit(solution)/shard_map/project_body/pallas_call | solution.py:26
  13.4 0.0 copy-start
  13.4 0.0 collective-permute-done.rest_0_
  13.4 0.0 copy-done.5
  13.4 0.5 shrink_body.1.rest_0_
  13.9 6.2 %collective-permute-start.3 = (bf16[96,128]{1,0:T(8,128)(2,1)S(1)}, bf16[96,128]{1,0:T(8,128)(2,1)S(1)}, u32[]{:S(2)}, u32[]{:S(2)}) collective-permute-start(bf16[96,128]{1,0:T(8,128)(2,1)S(1)} %shrink_body.1.rest_0_), channel_id=1, source_target_pairs={{0,3},{1,2},{2,1},{3,0},{4,7},{5,6},{6,5},{7,4},{8,11},{9,10},{10,... | collective-permute-start | bytes 73736 | tf_op jit(solution)/shard_map/ppermute | solution.py:394
  20.0 1.0 %collective-permute-start.2 = (bf16[96,128]{1,0:T(8,128)(2,1)S(1)}, bf16[96,128]{1,0:T(8,128)(2,1)S(1)}, u32[]{:S(2)}, u32[]{:S(2)}) collective-permute-start(bf16[96,128]{1,0:T(8,128)(2,1)S(1)} %shrink_body.1.rest_0_), channel_id=1, source_target_pairs={{0,2},{1,3},{2,0},{3,1},{4,6},{5,7},{6,4},{7,5},{8,10},{9,11},{10,... | collective-permute-start | bytes 73736 | tf_op jit(solution)/shard_map/ppermute | solution.py:394
  21.0 0.0 collective-permute-start.1
  21.0 0.5 %collective-permute-done.3.rest_3_ = bf16[96,128]{1,0:T(8,128)(2,1)S(1)} collective-permute-done((bf16[96,128]{1,0:T(8,128)(2,1)S(1)}, bf16[96,128]{1,0:T(8,128)(2,1)S(1)}, u32[]{:S(2)}, u32[]{:S(2)}) %collective-permute-start.3) | collective-permute-done | bytes 24608 | tf_op jit(solution)/shard_map/ppermute | solution.py:394
  21.5 2.3 %collective-permute-done.2.rest_2_ = bf16[96,128]{1,0:T(8,128)(2,1)S(1)} collective-permute-done((bf16[96,128]{1,0:T(8,128)(2,1)S(1)}, bf16[96,128]{1,0:T(8,128)(2,1)S(1)}, u32[]{:S(2)}, u32[]{:S(2)}) %collective-permute-start.2) | collective-permute-done | bytes 24608 | tf_op jit(solution)/shard_map/ppermute | solution.py:394
  23.8 0.0 collective-permute-done.1.rest_1_
  23.8 0.0 copy-done.6
  23.8 1.1 %expand_body.1 = (bf16[1,96,1280]{2,1,0:T(8,128)(2,1)S(1)}, bf16[1,96,1280]{2,1,0:T(8,128)(2,1)S(1)}, bf16[1,48,1280]{2,1,0:T(8,128)(2,1)S(1)}, bf16[1,48,1280]{...) custom-call(f32[8,64]{1,0:T(8,128)S(1)} %get-tuple-element.19.facts_ref, ...), custom_call_target="tpu_custom_call" | custom-call | flops 50331648 | bytes 524288 | tf_op jit(solution)/shard_map/expand_body/pallas_call | solution.py:26
  24.9 0.5 %collective-permute-start.4 = (bf16[1,96,1280]{2,1,0:T(8,128)(2,1)S(1)}, bf16[1,96,1280]{2,1,0:T(8,128)(2,1)S(1)}, u32[]{:S(2)}, u32[]{:S(2)}) collective-permute-start(bf16[1,96,1280]{2,1,0:T(8,128)(2,1)S(1)} %get-tuple-element.26), channel_id=1, source_target_pairs={{0,4},{4,0},{8,12},{12,8},{1,5},{5,1},{9,13},{13,9},{2,6},{6,2},{1... | collective-permute-start | bytes 737288 | tf_op jit(solution)/shard_map/ppermute | solution.py:360
  25.4 2.5 %collective-permute-start.6 = (bf16[1,48,1280]{2,1,0:T(8,128)(2,1)S(1)}, bf16[1,48,1280]{2,1,0:T(8,128)(2,1)S(1)}, u32[]{:S(2)}, u32[]{:S(2)}) collective-permute-start(bf16[1,48,1280]{2,1,0:T(8,128)(2,1)S(1)} %get-tuple-element.29), channel_id=1, source_target_pairs={{0,8},{4,12},{8,0},{12,4},{1,9},{5,13},{9,1},{13,5},{2,10},{6,14},... | collective-permute-start | bytes 368648 | tf_op jit(solution)/shard_map/ppermute | solution.py:360
  27.9 1.5 %collective-permute-start.8 = (bf16[1,48,1280]{2,1,0:T(8,128)(2,1)S(1)}, bf16[1,48,1280]{2,1,0:T(8,128)(2,1)S(1)}, u32[]{:S(2)}, u32[]{:S(2)}) collective-permute-start(bf16[1,48,1280]{2,1,0:T(8,128)(2,1)S(1)} %get-tuple-element.30), channel_id=1, source_target_pairs={{0,12},{4,8},{8,4},{12,0},{1,13},{5,9},{9,5},{13,1},{2,14},{6,10},... | collective-permute-start | bytes 368648 | tf_op jit(solution)/shard_map/ppermute | solution.py:360
  29.4 5.0 %collective-permute-done.6._.rest_2_ = bf16[1,48,1280]{2,1,0:T(8,128)(2,1)S(1)} collective-permute-done((bf16[1,48,1280]{2,1,0:T(8,128)(2,1)S(1)}, bf16[1,48,1280]{2,1,0:T(8,128)(2,1)S(1)}, u32[]{:S(2)}, u32[]{:S(2)}) %collective-permute-start.6) | collective-permute-done | bytes 122912 | tf_op jit(solution)/shard_map/ppermute | solution.py:360
  34.4 3.8 %collective-permute-start.7 = (bf16[1,48,1280]{2,1,0:T(8,128)(2,1)S(1)}, bf16[1,48,1280]{2,1,0:T(8,128)(2,1)S(1)}, u32[]{:S(2)}, u32[]{:S(2)}) collective-permute-start(bf16[1,48,1280]{2,1,0:T(8,128)(2,1)S(1)} %pass_body.1), channel_id=1, source_target_pairs={{0,4},{4,0},{8,12},{12,8},{1,5},{5,1},{9,13},{13,9},{2,6},{6,2},{1... | collective-permute-start | bytes 368648 | tf_op jit(solution)/shard_map/ppermute | solution.py:360
  38.2 0.0 collective-permute-done.4.got_ref.rest_1_
  38.2 0.1 collective-permute-start.5
  38.3 0.2 home_body.1
  38.5 1.4 %collective-permute-done.8.rest_3_ = bf16[1,48,1280]{2,1,0:T(8,128)(2,1)S(1)} collective-permute-done((bf16[1,48,1280]{2,1,0:T(8,128)(2,1)S(1)}, bf16[1,48,1280]{2,1,0:T(8,128)(2,1)S(1)}, u32[]{:S(2)}, u32[]{:S(2)}) %collective-permute-start.8) | collective-permute-done | bytes 122912 | tf_op jit(solution)/shard_map/ppermute | solution.py:360
  39.8 3.8 %collective-permute-done.7.rest_1_ = bf16[1,48,1280]{2,1,0:T(8,128)(2,1)S(1)} collective-permute-done((bf16[1,48,1280]{2,1,0:T(8,128)(2,1)S(1)}, bf16[1,48,1280]{2,1,0:T(8,128)(2,1)S(1)}, u32[]{:S(2)}, u32[]{:S(2)}) %collective-permute-start.7) | collective-permute-done | bytes 122912 | tf_op jit(solution)/shard_map/ppermute | solution.py:360
  43.7 1.1 %attend_body.2.rest_3_ = bf16[48,1024]{1,0:T(8,128)(2,1)S(1)} custom-call(f32[48,128]{1,0:T(8,128)S(1)} %get-tuple-element.20.cos_ref, f32[48,128]{1,0:T(8,128)S(1)} %get-tuple-element.21.sin_ref, f32[16,256]{1,0:T(8,128)S(1)} %get-tuple-element.22.len_ref, bf16[16,2,256,128]{3,2,1,0:T(8,128)(2,1)S(1)} %copy-done, bf16[16,2,256,128]{3,2,1,0:T(8,128)(2,1)S(1)} %copy-done.1, ...), custom_call_target="tpu_custom_call" | custom-call | flops 50331648 | bytes 2097152 | tf_op jit(solution)/shard_map/attend_body/pallas_call | solution.py:26
  44.7 0.7 %collective-permute-done.5.rest_2_ = bf16[1,48,1280]{2,1,0:T(8,128)(2,1)S(1)} collective-permute-done((bf16[1,48,1280]{2,1,0:T(8,128)(2,1)S(1)}, bf16[1,48,1280]{2,1,0:T(8,128)(2,1)S(1)}, u32[]{:S(2)}, u32[]{:S(2)}) %collective-permute-start.5) | collective-permute-done | bytes 122912 | tf_op jit(solution)/shard_map/ppermute | solution.py:360
  45.4 1.8 %attend_body.3 = bf16[48,2048]{1,0:T(8,128)(2,1)} custom-call(f32[48,128]{1,0:T(8,128)S(1)} %get-tuple-element.20.cos_ref, f32[48,128]{1,0:T(8,128)S(1)} %get-tuple-element.21.sin_ref, f32[16,256]{1,0:T(8,128)S(1)} %get-tuple-element.22.len_ref, bf16[16,2,256,128]{3,2,1,0:T(8,128)(2,1)S(1)} %copy-done, bf16[16,2,256,128]{3,2,1,0:T(8,128)(2,1)S(1)} %copy-done.1, ...), custom_call_target="tpu_custom_call" | custom-call | flops 50331648 | bytes 2097152 | tf_op jit(solution)/shard_map/attend_body/pallas_call | solution.py:26
  (13 shorter events, 0.1 us)
Async XLA Ops:
  2.2 11.1 %collective-permute-start = (bf16[96,2048]{1,0:T(8,128)(2,1)}, bf16[96,2048]{1,0:T(8,128)(2,1)S(1)}, u32[]{:S(2)}, u32[]{:S(2)}) collective-permute-start(bf16[96,2048]{1,0:T(8,128)(2,1)} %get-tuple-element.23), channel_id=1, source_target_pairs={{0,0},{1,12},{2,8},{3,4},{4,9},{5,5},{6,1},{7,13},{8,10},{9,6},{10... | collective-permute-start | bytes 1179656 | tf_op jit(solution)/shard_map/ppermute | solution.py:357
  3.9 1.1 %copy-start.2 = (bf16[64,3,2048]{2,0,1:T(8,128)(2,1)S(1)}, bf16[64,3,2048]{2,0,1:T(8,128)(2,1)}, u32[]{:S(2)}) copy-start(bf16[64,3,2048]{2,0,1:T(8,128)(2,1)} %param.12) | copy-start | bytes 2359300
  5.0 1.2 %copy-start.3 = (bf16[2048,256]{1,0:T(8,128)(2,1)S(1)}, bf16[2048,256]{1,0:T(8,128)(2,1)}, u32[]{:S(2)}) copy-start(bf16[2048,256]{1,0:T(8,128)(2,1)} %k_ref.1) | copy-start | bytes 3145732
  6.2 1.2 %copy-start.4 = (bf16[2048,256]{1,0:T(8,128)(2,1)S(1)}, bf16[2048,256]{1,0:T(8,128)(2,1)}, u32[]{:S(2)}) copy-start(bf16[2048,256]{1,0:T(8,128)(2,1)} %v_ref.1) | copy-start | bytes 3145732
  7.5 0.7 %copy-start.8 = (f32[8,64]{1,0:T(8,128)S(1)}, f32[8,64]{1,0:T(8,128)}, u32[]{:S(2)}) copy-start(f32[8,64]{1,0:T(8,128)} %get-tuple-element.18.facts_ref) | copy-start | bytes 6148
  8.2 5.2 %copy-start.5 = (bf16[2,128,2048]{2,1,0:T(8,128)(2,1)S(1)}, bf16[2,128,2048]{2,1,0:T(8,128)(2,1)}, u32[]{:S(2)}) copy-start(bf16[2,128,2048]{2,1,0:T(8,128)(2,1)} %down_ref.1) | copy-start | bytes 3145732
  8.2 15.7 %copy-start.6 = (bf16[2,64,2048]{2,1,0:T(8,128)(2,1)S(1)}, bf16[2,64,2048]{2,1,0:T(8,128)(2,1)}, u32[]{:S(2)}) copy-start(bf16[2,64,2048]{2,1,0:T(8,128)(2,1)} %upq_ref.1) | copy-start | bytes 1572868
  8.2 15.7 %copy-start.7 = (bf16[2,64,256]{2,1,0:T(8,128)(2,1)S(1)}, bf16[2,64,256]{2,1,0:T(8,128)(2,1)}, u32[]{:S(2)}) copy-start(bf16[2,64,256]{2,1,0:T(8,128)(2,1)} %upv_ref.1) | copy-start | bytes 196612
  8.2 35.5 %copy-start.1 = (bf16[16,2,256,128]{3,2,1,0:T(8,128)(2,1)S(1)}, bf16[16,2,256,128]{3,2,1,0:T(8,128)(2,1)}, u32[]{:S(2)}) copy-start(bf16[16,2,256,128]{3,2,1,0:T(8,128)(2,1)} %vc_ref.3) | copy-start | bytes 6291460
  13.4 30.3 %copy-start = (bf16[16,2,256,128]{3,2,1,0:T(8,128)(2,1)S(1)}, bf16[16,2,256,128]{3,2,1,0:T(8,128)(2,1)}, u32[]{:S(2)}) copy-start(bf16[16,2,256,128]{3,2,1,0:T(8,128)(2,1)} %kc_ref.3) | copy-start | bytes 6291460
  13.9 7.7 %collective-permute-start.3 = (bf16[96,128]{1,0:T(8,128)(2,1)S(1)}, bf16[96,128]{1,0:T(8,128)(2,1)S(1)}, u32[]{:S(2)}, u32[]{:S(2)}) collective-permute-start(bf16[96,128]{1,0:T(8,128)(2,1)S(1)} %shrink_body.1.rest_0_), channel_id=1, source_target_pairs={{0,3},{1,2},{2,1},{3,0},{4,7},{5,6},{6,5},{7,4},{8,11},{9,10},{10,... | collective-permute-start | bytes 73736 | tf_op jit(solution)/shard_map/ppermute | solution.py:394
  20.0 3.8 %collective-permute-start.2 = (bf16[96,128]{1,0:T(8,128)(2,1)S(1)}, bf16[96,128]{1,0:T(8,128)(2,1)S(1)}, u32[]{:S(2)}, u32[]{:S(2)}) collective-permute-start(bf16[96,128]{1,0:T(8,128)(2,1)S(1)} %shrink_body.1.rest_0_), channel_id=1, source_target_pairs={{0,2},{1,3},{2,0},{3,1},{4,6},{5,7},{6,4},{7,5},{8,10},{9,11},{10,... | collective-permute-start | bytes 73736 | tf_op jit(solution)/shard_map/ppermute | solution.py:394
  21.0 2.9 %collective-permute-start.1 = (bf16[96,128]{1,0:T(8,128)(2,1)S(1)}, bf16[96,128]{1,0:T(8,128)(2,1)S(1)}, u32[]{:S(2)}, u32[]{:S(2)}) collective-permute-start(bf16[96,128]{1,0:T(8,128)(2,1)S(1)} %shrink_body.1.rest_0_), channel_id=1, source_target_pairs={{0,1},{1,0},{2,3},{3,2},{4,5},{5,4},{6,7},{7,6},{8,9},{9,8},{10,11... | collective-permute-start | bytes 73736 | tf_op jit(solution)/shard_map/ppermute | solution.py:394
  24.9 13.2 %collective-permute-start.4 = (bf16[1,96,1280]{2,1,0:T(8,128)(2,1)S(1)}, bf16[1,96,1280]{2,1,0:T(8,128)(2,1)S(1)}, u32[]{:S(2)}, u32[]{:S(2)}) collective-permute-start(bf16[1,96,1280]{2,1,0:T(8,128)(2,1)S(1)} %get-tuple-element.26), channel_id=1, source_target_pairs={{0,4},{4,0},{8,12},{12,8},{1,5},{5,1},{9,13},{13,9},{2,6},{6,2},{1... | collective-permute-start | bytes 737288 | tf_op jit(solution)/shard_map/ppermute | solution.py:360
  25.4 9.0 %collective-permute-start.6 = (bf16[1,48,1280]{2,1,0:T(8,128)(2,1)S(1)}, bf16[1,48,1280]{2,1,0:T(8,128)(2,1)S(1)}, u32[]{:S(2)}, u32[]{:S(2)}) collective-permute-start(bf16[1,48,1280]{2,1,0:T(8,128)(2,1)S(1)} %get-tuple-element.29), channel_id=1, source_target_pairs={{0,8},{4,12},{8,0},{12,4},{1,9},{5,13},{9,1},{13,5},{2,10},{6,14},... | collective-permute-start | bytes 368648 | tf_op jit(solution)/shard_map/ppermute | solution.py:360
  27.9 11.9 %collective-permute-start.8 = (bf16[1,48,1280]{2,1,0:T(8,128)(2,1)S(1)}, bf16[1,48,1280]{2,1,0:T(8,128)(2,1)S(1)}, u32[]{:S(2)}, u32[]{:S(2)}) collective-permute-start(bf16[1,48,1280]{2,1,0:T(8,128)(2,1)S(1)} %get-tuple-element.30), channel_id=1, source_target_pairs={{0,12},{4,8},{8,4},{12,0},{1,13},{5,9},{9,5},{13,1},{2,14},{6,10},... | collective-permute-start | bytes 368648 | tf_op jit(solution)/shard_map/ppermute | solution.py:360
  34.4 9.3 %collective-permute-start.7 = (bf16[1,48,1280]{2,1,0:T(8,128)(2,1)S(1)}, bf16[1,48,1280]{2,1,0:T(8,128)(2,1)S(1)}, u32[]{:S(2)}, u32[]{:S(2)}) collective-permute-start(bf16[1,48,1280]{2,1,0:T(8,128)(2,1)S(1)} %pass_body.1), channel_id=1, source_target_pairs={{0,4},{4,0},{8,12},{12,8},{1,5},{5,1},{9,13},{13,9},{2,6},{6,2},{1... | collective-permute-start | bytes 368648 | tf_op jit(solution)/shard_map/ppermute | solution.py:360
  38.2 7.2 %collective-permute-start.5 = (bf16[1,48,1280]{2,1,0:T(8,128)(2,1)S(1)}, bf16[1,48,1280]{2,1,0:T(8,128)(2,1)S(1)}, u32[]{:S(2)}, u32[]{:S(2)}) collective-permute-start(bf16[1,48,1280]{2,1,0:T(8,128)(2,1)S(1)} %add_body.1), channel_id=1, source_target_pairs={{0,8},{4,12},{8,0},{12,4},{1,9},{5,13},{9,1},{13,5},{2,10},{6,14},... | collective-permute-start | bytes 368648 | tf_op jit(solution)/shard_map/ppermute | solution.py:360

commit v6 on v5

--- a/solution.py
+++ b/solution.py
@@ -12,7 +12,7 @@
 BF16 = jnp.bfloat16
 F32 = jnp.float32
 FEATURE_AXES = ("tp", "sub")
-CARRIER = ((0, 3, 2, 1), (2, 1, 0, 3), (3, 1, 0, 2), (1, 2, 0, 3))
+CARRIER = ((3, 1, 2, 0), (1, 2, 3, 0), (3, 1, 0, 2), (1, 3, 2, 0))
 
 
 def call(body, out_shape, args, in_specs=None, out_specs=None, grid=None, scratch=(), flops=0, bytes_=0, limit=40, **more):
@@ -429,7 +429,7 @@
         )
         sums = (near, got, swap(passed, 2))
         messages[1] = call(
-            pass_body, shape(messages[1].shape, BF16), (messages[1], messages[2]), in_specs=[VMEM, ANY]
+            pass_body, shape(messages[1].shape, BF16), (messages[1], passed), in_specs=[VMEM, ANY]
         )
     messages[1] = swap(messages[1], 1)
 

time: 47.5 us -> 44.9 us (0.945)
  starting transfers between devices: 17.1 us -> 13.5 us
  waiting for transfers between devices: 13.7 us -> 14.7 us
    ppermute x3, starting transfers between devices: 7.13 us -> 1.92 us  [on_device(): lax.ppermute(share, FEATURE_AXES, [(i, i ^ d) for i in range(features)])]
    ppermute x1, starting transfers between devices: 1.65 us -> 5.11 us  [on_device(): lax.ppermute(s, ('pool', *FEATURE_AXES), perm)]
    ppermute x5, starting transfers between devices: 8.28 us -> 6.52 us  [swap(): return lax.ppermute(value, 'pool', [(i, i ^ d) for i in range(homes)])]
    ppermute x5, waiting for transfers between devices: 10.9 us -> 12.4 us  [swap(): return lax.ppermute(value, 'pool', [(i, i ^ d) for i in range(homes)])]
    ppermute x3, waiting for transfers between devices: 2.85 us -> 2.29 us  [on_device(): lax.ppermute(share, FEATURE_AXES, [(i, i ^ d) for i in range(features)])]
  transfers between devices with their start and end apart: 9 -> 9, of which waited for: 6 -> 6; matrix products, arithmetic and copies ran while one was open for 0% -> 0% of each run, Pallas kernels for 14% -> 15%
where the time goes in v6:
time: 44.9 us; the launch traced here: 44.6 us
  waiting for transfers between devices  14.7 us (33%)
  starting transfers between devices  13.5 us (30%)
  Pallas kernels  12 us (27%)
  local copies, waits for them, and re-layouts  4.29 us (10%)
    ppermute x5, waiting for transfers between devices, swap(): return lax.ppermute(value, 'pool', [(i, i ^ d) for i in range(homes)])  12.4 us
    pallas_call x9, Pallas kernels, call(): pl.pallas_call(body, name=inner.__name__, out_shape=out_shape, in_specs=i...  12 us
    ppermute x5, starting transfers between devices, swap(): return lax.ppermute(value, 'pool', [(i, i ^ d) for i in range(homes)])  6.52 us
    ppermute x1, starting transfers between devices, on_device(): lax.ppermute(s, ('pool', *FEATURE_AXES), perm)  5.11 us
    unnamed x18, local copies, waits for them, and re-layouts  4.29 us
    ppermute x3, waiting for transfers between devices, on_device(): lax.ppermute(share, FEATURE_AXES, [(i, i ^ d) for i in range(features)])  2.29 us
    ppermute x3, starting transfers between devices, on_device(): lax.ppermute(share, FEATURE_AXES, [(i, i ^ d) for i in range(features)])  1.92 us
  transfers between devices with their start and end apart: 9, of which 6 were waited for; matrix products, arithmetic and copies ran while one was open for 0% of the time, Pallas kernels for 15%

profile of v6, /device:TPU:0, one launch (start us, length us, event | category | flops | bytes accessed | tf_op | source)
XLA Modules:
  0.0 44.6 jit_solution(12302823704366979754)
XLA Ops:
  0.0 2.2 %select_body.1 = (bf16[96,2048]{1,0:T(8,128)(2,1)}, f32[8,64]{1,0:T(8,128)}) custom-call(s32[1,64]{1,0:T(1,128)} %bitcast.11, s32[1,64]{1,0:T(1,128)} %bitcast.12, s32[1,64]{1,0:T(1,128)} %bitcast.13, bf16[3,64,2048]{2,1,0:T(8,128)(2,1)} %bitcast.9), custom_call_target="tpu_custom_call" | custom-call | flops 25165824 | bytes 1179648 | tf_op jit(solution)/shard_map/select_body/pallas_call | solution.py:26
  2.2 5.1 %collective-permute-start = (bf16[96,2048]{1,0:T(8,128)(2,1)}, bf16[96,2048]{1,0:T(8,128)(2,1)S(1)}, u32[]{:S(2)}, u32[]{:S(2)}) collective-permute-start(bf16[96,2048]{1,0:T(8,128)(2,1)} %get-tuple-element.23), channel_id=1, source_target_pairs={{0,12},{1,4},{2,8},{3,0},{4,13},{5,1},{6,5},{7,9},{8,10},{9,6},{10... | collective-permute-start | bytes 1179656 | tf_op jit(solution)/shard_map/ppermute | solution.py:357
  7.3 1.1 %copy-done.2 = bf16[64,3,2048]{2,0,1:T(8,128)(2,1)S(1)} copy-done((bf16[64,3,2048]{2,0,1:T(8,128)(2,1)S(1)}, bf16[64,3,2048]{2,0,1:T(8,128)(2,1)}, u32[]{:S(2)}) %copy-start.2) | copy-done | bytes 786456
  8.5 1.2 %copy-done.3 = bf16[2048,256]{1,0:T(8,128)(2,1)S(1)} copy-done((bf16[2048,256]{1,0:T(8,128)(2,1)S(1)}, bf16[2048,256]{1,0:T(8,128)(2,1)}, u32[]{:S(2)}) %copy-start.3) | copy-done | bytes 1048600
  9.7 1.2 %copy-done.4 = bf16[2048,256]{1,0:T(8,128)(2,1)S(1)} copy-done((bf16[2048,256]{1,0:T(8,128)(2,1)S(1)}, bf16[2048,256]{1,0:T(8,128)(2,1)}, u32[]{:S(2)}) %copy-start.4) | copy-done | bytes 1048600
  10.9 0.7 %copy-done.8 = f32[8,64]{1,0:T(8,128)S(1)} copy-done((f32[8,64]{1,0:T(8,128)S(1)}, f32[8,64]{1,0:T(8,128)}, u32[]{:S(2)}) %copy-start.8) | copy-done | bytes 2072
  11.6 5.2 %project_body.1 = (bf16[2,192,1280]{2,1,0:T(8,128)(2,1)S(1)}, f32[8,64]{1,0:T(8,128)S(1)}) custom-call(bf16[192,2048]{1,0:T(8,128)(2,1)S(1)} %bitcast.10, bf16[2048,2048]{1,0:T(8,128)(2,1)} %q_ref.1, bf16[2048,256]{1,0:T(8,128)(2,1)S(1)} %copy-done.3, bf16[2048,256]{1,0:T(8,128)(2,1)S(1)} %copy-done.4, f32[8,64]{1,0:T(8,128)S(1)} %copy-done.8), custom_call_target="tpu_custom_call" | custom-call | flops 2013265920 | bytes 10485760 | tf_op jit(solution)/shard_map/project_body/pallas_call | solution.py:26
  16.8 0.0 copy-start
  16.8 0.0 collective-permute-done.rest_0_
  16.8 0.0 copy-done.5
  16.8 0.5 %shrink_body.1.rest_0_ = bf16[96,128]{1,0:T(8,128)(2,1)S(1)} custom-call(f32[8,64]{1,0:T(8,128)S(1)} %get-tuple-element.19.facts_ref, bf16[2,128,2048]{2,1,0:T(8,128)(2,1)S(1)} %copy-done.5, bf16[96,2048]{1,0:T(8,128)(2,1)S(1)} %collective-permute-done.rest_0_), custom_call_target="tpu_custom_call" | custom-call | flops 100663296 | bytes 1048576 | tf_op jit(solution)/shard_map/shrink_body/pallas_call | solution.py:26
  17.3 0.1 collective-permute-start.3
  17.4 1.0 %collective-permute-start.2 = (bf16[96,128]{1,0:T(8,128)(2,1)S(1)}, bf16[96,128]{1,0:T(8,128)(2,1)S(1)}, u32[]{:S(2)}, u32[]{:S(2)}) collective-permute-start(bf16[96,128]{1,0:T(8,128)(2,1)S(1)} %shrink_body.1.rest_0_), channel_id=1, source_target_pairs={{0,2},{1,3},{2,0},{3,1},{4,6},{5,7},{6,4},{7,5},{8,10},{9,11},{10,... | collective-permute-start | bytes 73736 | tf_op jit(solution)/shard_map/ppermute | solution.py:394
  18.4 0.9 %collective-permute-start.1 = (bf16[96,128]{1,0:T(8,128)(2,1)S(1)}, bf16[96,128]{1,0:T(8,128)(2,1)S(1)}, u32[]{:S(2)}, u32[]{:S(2)}) collective-permute-start(bf16[96,128]{1,0:T(8,128)(2,1)S(1)} %shrink_body.1.rest_0_), channel_id=1, source_target_pairs={{0,1},{1,0},{2,3},{3,2},{4,5},{5,4},{6,7},{7,6},{8,9},{9,8},{10,11... | collective-permute-start | bytes 73736 | tf_op jit(solution)/shard_map/ppermute | solution.py:394
  19.2 1.4 %collective-permute-done.3.rest_3_ = bf16[96,128]{1,0:T(8,128)(2,1)S(1)} collective-permute-done((bf16[96,128]{1,0:T(8,128)(2,1)S(1)}, bf16[96,128]{1,0:T(8,128)(2,1)S(1)}, u32[]{:S(2)}, u32[]{:S(2)}) %collective-permute-start.3) | collective-permute-done | bytes 24608 | tf_op jit(solution)/shard_map/ppermute | solution.py:394
  20.6 0.9 %collective-permute-done.2.rest_2_ = bf16[96,128]{1,0:T(8,128)(2,1)S(1)} collective-permute-done((bf16[96,128]{1,0:T(8,128)(2,1)S(1)}, bf16[96,128]{1,0:T(8,128)(2,1)S(1)}, u32[]{:S(2)}, u32[]{:S(2)}) %collective-permute-start.2) | collective-permute-done | bytes 24608 | tf_op jit(solution)/shard_map/ppermute | solution.py:394
  21.5 0.0 collective-permute-done.1.rest_1_
  21.5 0.0 copy-done.7
  21.5 1.1 %expand_body.1 = (bf16[1,96,1280]{2,1,0:T(8,128)(2,1)S(1)}, bf16[1,96,1280]{2,1,0:T(8,128)(2,1)S(1)}, bf16[1,48,1280]{2,1,0:T(8,128)(2,1)S(1)}, bf16[1,48,1280]{...) custom-call(f32[8,64]{1,0:T(8,128)S(1)} %get-tuple-element.19.facts_ref, ...), custom_call_target="tpu_custom_call" | custom-call | flops 50331648 | bytes 524288 | tf_op jit(solution)/shard_map/expand_body/pallas_call | solution.py:26
  22.6 0.6 %collective-permute-start.4 = (bf16[1,96,1280]{2,1,0:T(8,128)(2,1)S(1)}, bf16[1,96,1280]{2,1,0:T(8,128)(2,1)S(1)}, u32[]{:S(2)}, u32[]{:S(2)}) collective-permute-start(bf16[1,96,1280]{2,1,0:T(8,128)(2,1)S(1)} %get-tuple-element.26), channel_id=1, source_target_pairs={{0,4},{4,0},{8,12},{12,8},{1,5},{5,1},{9,13},{13,9},{2,6},{6,2},{1... | collective-permute-start | bytes 737288 | tf_op jit(solution)/shard_map/ppermute | solution.py:360
  23.2 2.4 %collective-permute-start.7 = (bf16[1,48,1280]{2,1,0:T(8,128)(2,1)S(1)}, bf16[1,48,1280]{2,1,0:T(8,128)(2,1)S(1)}, u32[]{:S(2)}, u32[]{:S(2)}) collective-permute-start(bf16[1,48,1280]{2,1,0:T(8,128)(2,1)S(1)} %get-tuple-element.29), channel_id=1, source_target_pairs={{0,8},{4,12},{8,0},{12,4},{1,9},{5,13},{9,1},{13,5},{2,10},{6,14},... | collective-permute-start | bytes 368648 | tf_op jit(solution)/shard_map/ppermute | solution.py:360
  25.7 1.4 %collective-permute-start.8 = (bf16[1,48,1280]{2,1,0:T(8,128)(2,1)S(1)}, bf16[1,48,1280]{2,1,0:T(8,128)(2,1)S(1)}, u32[]{:S(2)}, u32[]{:S(2)}) collective-permute-start(bf16[1,48,1280]{2,1,0:T(8,128)(2,1)S(1)} %get-tuple-element.30), channel_id=1, source_target_pairs={{0,12},{4,8},{8,4},{12,0},{1,13},{5,9},{9,5},{13,1},{2,14},{6,10},... | collective-permute-start | bytes 368648 | tf_op jit(solution)/shard_map/ppermute | solution.py:360
  27.1 6.6 %collective-permute-done.4.got_ref.rest_1_ = bf16[1,96,1280]{2,1,0:T(8,128)(2,1)S(1)} collective-permute-done((bf16[1,96,1280]{2,1,0:T(8,128)(2,1)S(1)}, bf16[1,96,1280]{2,1,0:T(8,128)(2,1)S(1)}, u32[]{:S(2)}, u32[]{:S(2)}) %collective-permute-start.4) | collective-permute-done | bytes 245792 | tf_op jit(solution)/shard_map/ppermute | solution.py:360
  33.8 0.1 collective-permute-start.6
  33.9 2.0 %collective-permute-start.5 = (bf16[1,48,1280]{2,1,0:T(8,128)(2,1)S(1)}, bf16[1,48,1280]{2,1,0:T(8,128)(2,1)S(1)}, u32[]{:S(2)}, u32[]{:S(2)}) collective-permute-start(bf16[1,48,1280]{2,1,0:T(8,128)(2,1)S(1)} %add_body.1._), channel_id=1, source_target_pairs={{0,8},{4,12},{8,0},{12,4},{1,9},{5,13},{9,1},{13,5},{2,10},{6,14},... | collective-permute-start | bytes 368648 | tf_op jit(solution)/shard_map/ppermute | solution.py:360
  35.9 0.2 home_body.1
  36.0 0.0 collective-permute-done.7.rest_2_
  36.1 1.4 %collective-permute-done.8.rest_3_ = bf16[1,48,1280]{2,1,0:T(8,128)(2,1)S(1)} collective-permute-done((bf16[1,48,1280]{2,1,0:T(8,128)(2,1)S(1)}, bf16[1,48,1280]{2,1,0:T(8,128)(2,1)S(1)}, u32[]{:S(2)}, u32[]{:S(2)}) %collective-permute-start.8) | collective-permute-done | bytes 122912 | tf_op jit(solution)/shard_map/ppermute | solution.py:360
  37.4 3.2 %collective-permute-done.6.rest_1_ = bf16[1,48,1280]{2,1,0:T(8,128)(2,1)S(1)} collective-permute-done((bf16[1,48,1280]{2,1,0:T(8,128)(2,1)S(1)}, bf16[1,48,1280]{2,1,0:T(8,128)(2,1)S(1)}, u32[]{:S(2)}, u32[]{:S(2)}) %collective-permute-start.6) | collective-permute-done | bytes 122912 | tf_op jit(solution)/shard_map/ppermute | solution.py:360
  40.6 1.1 %attend_body.2.rest_3_ = bf16[48,1024]{1,0:T(8,128)(2,1)S(1)} custom-call(f32[48,128]{1,0:T(8,128)S(1)} %get-tuple-element.20.cos_ref, f32[48,128]{1,0:T(8,128)S(1)} %get-tuple-element.21.sin_ref, f32[16,256]{1,0:T(8,128)S(1)} %get-tuple-element.22.len_ref, bf16[16,2,256,128]{3,2,1,0:T(8,128)(2,1)S(1)} %copy-done, bf16[16,2,256,128]{3,2,1,0:T(8,128)(2,1)S(1)} %copy-done.1, ...), custom_call_target="tpu_custom_call" | custom-call | flops 50331648 | bytes 2097152 | tf_op jit(solution)/shard_map/attend_body/pallas_call | solution.py:26
  41.7 1.2 %collective-permute-done.5.rest_2_ = bf16[1,48,1280]{2,1,0:T(8,128)(2,1)S(1)} collective-permute-done((bf16[1,48,1280]{2,1,0:T(8,128)(2,1)S(1)}, bf16[1,48,1280]{2,1,0:T(8,128)(2,1)S(1)}, u32[]{:S(2)}, u32[]{:S(2)}) %collective-permute-start.5) | collective-permute-done | bytes 122912 | tf_op jit(solution)/shard_map/ppermute | solution.py:360
  42.9 1.8 %attend_body.3 = bf16[48,2048]{1,0:T(8,128)(2,1)} custom-call(f32[48,128]{1,0:T(8,128)S(1)} %get-tuple-element.20.cos_ref, f32[48,128]{1,0:T(8,128)S(1)} %get-tuple-element.21.sin_ref, f32[16,256]{1,0:T(8,128)S(1)} %get-tuple-element.22.len_ref, bf16[16,2,256,128]{3,2,1,0:T(8,128)(2,1)S(1)} %copy-done, bf16[16,2,256,128]{3,2,1,0:T(8,128)(2,1)S(1)} %copy-done.1, ...), custom_call_target="tpu_custom_call" | custom-call | flops 50331648 | bytes 2097152 | tf_op jit(solution)/shard_map/attend_body/pallas_call | solution.py:26
  (13 shorter events, 0.1 us)
Async XLA Ops:
  2.2 14.6 %collective-permute-start = (bf16[96,2048]{1,0:T(8,128)(2,1)}, bf16[96,2048]{1,0:T(8,128)(2,1)S(1)}, u32[]{:S(2)}, u32[]{:S(2)}) collective-permute-start(bf16[96,2048]{1,0:T(8,128)(2,1)} %get-tuple-element.23), channel_id=1, source_target_pairs={{0,12},{1,4},{2,8},{3,0},{4,13},{5,1},{6,5},{7,9},{8,10},{9,6},{10... | collective-permute-start | bytes 1179656 | tf_op jit(solution)/shard_map/ppermute | solution.py:357
  7.3 1.1 %copy-start.2 = (bf16[64,3,2048]{2,0,1:T(8,128)(2,1)S(1)}, bf16[64,3,2048]{2,0,1:T(8,128)(2,1)}, u32[]{:S(2)}) copy-start(bf16[64,3,2048]{2,0,1:T(8,128)(2,1)} %param.12) | copy-start | bytes 2359300
  8.5 1.2 %copy-start.3 = (bf16[2048,256]{1,0:T(8,128)(2,1)S(1)}, bf16[2048,256]{1,0:T(8,128)(2,1)}, u32[]{:S(2)}) copy-start(bf16[2048,256]{1,0:T(8,128)(2,1)} %k_ref.1) | copy-start | bytes 3145732
  9.7 1.2 %copy-start.4 = (bf16[2048,256]{1,0:T(8,128)(2,1)S(1)}, bf16[2048,256]{1,0:T(8,128)(2,1)}, u32[]{:S(2)}) copy-start(bf16[2048,256]{1,0:T(8,128)(2,1)} %v_ref.1) | copy-start | bytes 3145732
  10.9 0.7 %copy-start.8 = (f32[8,64]{1,0:T(8,128)S(1)}, f32[8,64]{1,0:T(8,128)}, u32[]{:S(2)}) copy-start(f32[8,64]{1,0:T(8,128)} %get-tuple-element.18.facts_ref) | copy-start | bytes 6148
  11.6 5.2 %copy-start.5 = (bf16[2,128,2048]{2,1,0:T(8,128)(2,1)S(1)}, bf16[2,128,2048]{2,1,0:T(8,128)(2,1)}, u32[]{:S(2)}) copy-start(bf16[2,128,2048]{2,1,0:T(8,128)(2,1)} %down_ref.1) | copy-start | bytes 3145732
  11.6 9.9 %copy-start.6 = (bf16[2,64,2048]{2,1,0:T(8,128)(2,1)S(1)}, bf16[2,64,2048]{2,1,0:T(8,128)(2,1)}, u32[]{:S(2)}) copy-start(bf16[2,64,2048]{2,1,0:T(8,128)(2,1)} %upq_ref.1) | copy-start | bytes 1572868
  11.6 9.9 %copy-start.7 = (bf16[2,64,256]{2,1,0:T(8,128)(2,1)S(1)}, bf16[2,64,256]{2,1,0:T(8,128)(2,1)}, u32[]{:S(2)}) copy-start(bf16[2,64,256]{2,1,0:T(8,128)(2,1)} %upv_ref.1) | copy-start | bytes 196612
  11.6 29.0 %copy-start.1 = (bf16[16,2,256,128]{3,2,1,0:T(8,128)(2,1)S(1)}, bf16[16,2,256,128]{3,2,1,0:T(8,128)(2,1)}, u32[]{:S(2)}) copy-start(bf16[16,2,256,128]{3,2,1,0:T(8,128)(2,1)} %vc_ref.3) | copy-start | bytes 6291460
  16.8 23.8 %copy-start = (bf16[16,2,256,128]{3,2,1,0:T(8,128)(2,1)S(1)}, bf16[16,2,256,128]{3,2,1,0:T(8,128)(2,1)}, u32[]{:S(2)}) copy-start(bf16[16,2,256,128]{3,2,1,0:T(8,128)(2,1)} %kc_ref.3) | copy-start | bytes 6291460
  17.3 3.3 %collective-permute-start.3 = (bf16[96,128]{1,0:T(8,128)(2,1)S(1)}, bf16[96,128]{1,0:T(8,128)(2,1)S(1)}, u32[]{:S(2)}, u32[]{:S(2)}) collective-permute-start(bf16[96,128]{1,0:T(8,128)(2,1)S(1)} %shrink_body.1.rest_0_), channel_id=1, source_target_pairs={{0,3},{1,2},{2,1},{3,0},{4,7},{5,6},{6,5},{7,4},{8,11},{9,10},{10,... | collective-permute-start | bytes 73736 | tf_op jit(solution)/shard_map/ppermute | solution.py:394
  17.4 4.1 %collective-permute-start.2 = (bf16[96,128]{1,0:T(8,128)(2,1)S(1)}, bf16[96,128]{1,0:T(8,128)(2,1)S(1)}, u32[]{:S(2)}, u32[]{:S(2)}) collective-permute-start(bf16[96,128]{1,0:T(8,128)(2,1)S(1)} %shrink_body.1.rest_0_), channel_id=1, source_target_pairs={{0,2},{1,3},{2,0},{3,1},{4,6},{5,7},{6,4},{7,5},{8,10},{9,11},{10,... | collective-permute-start | bytes 73736 | tf_op jit(solution)/shard_map/ppermute | solution.py:394
  18.4 3.2 %collective-permute-start.1 = (bf16[96,128]{1,0:T(8,128)(2,1)S(1)}, bf16[96,128]{1,0:T(8,128)(2,1)S(1)}, u32[]{:S(2)}, u32[]{:S(2)}) collective-permute-start(bf16[96,128]{1,0:T(8,128)(2,1)S(1)} %shrink_body.1.rest_0_), channel_id=1, source_target_pairs={{0,1},{1,0},{2,3},{3,2},{4,5},{5,4},{6,7},{7,6},{8,9},{9,8},{10,11... | collective-permute-start | bytes 73736 | tf_op jit(solution)/shard_map/ppermute | solution.py:394
  22.6 11.1 %collective-permute-start.4 = (bf16[1,96,1280]{2,1,0:T(8,128)(2,1)S(1)}, bf16[1,96,1280]{2,1,0:T(8,128)(2,1)S(1)}, u32[]{:S(2)}, u32[]{:S(2)}) collective-permute-start(bf16[1,96,1280]{2,1,0:T(8,128)(2,1)S(1)} %get-tuple-element.26), channel_id=1, source_target_pairs={{0,4},{4,0},{8,12},{12,8},{1,5},{5,1},{9,13},{13,9},{2,6},{6,2},{1... | collective-permute-start | bytes 737288 | tf_op jit(solution)/shard_map/ppermute | solution.py:360
  23.2 12.8 %collective-permute-start.7 = (bf16[1,48,1280]{2,1,0:T(8,128)(2,1)S(1)}, bf16[1,48,1280]{2,1,0:T(8,128)(2,1)S(1)}, u32[]{:S(2)}, u32[]{:S(2)}) collective-permute-start(bf16[1,48,1280]{2,1,0:T(8,128)(2,1)S(1)} %get-tuple-element.29), channel_id=1, source_target_pairs={{0,8},{4,12},{8,0},{12,4},{1,9},{5,13},{9,1},{13,5},{2,10},{6,14},... | collective-permute-start | bytes 368648 | tf_op jit(solution)/shard_map/ppermute | solution.py:360
  25.7 11.7 %collective-permute-start.8 = (bf16[1,48,1280]{2,1,0:T(8,128)(2,1)S(1)}, bf16[1,48,1280]{2,1,0:T(8,128)(2,1)S(1)}, u32[]{:S(2)}, u32[]{:S(2)}) collective-permute-start(bf16[1,48,1280]{2,1,0:T(8,128)(2,1)S(1)} %get-tuple-element.30), channel_id=1, source_target_pairs={{0,12},{4,8},{8,4},{12,0},{1,13},{5,9},{9,5},{13,1},{2,14},{6,10},... | collective-permute-start | bytes 368648 | tf_op jit(solution)/shard_map/ppermute | solution.py:360
  33.8 6.8 %collective-permute-start.6 = (bf16[1,48,1280]{2,1,0:T(8,128)(2,1)S(1)}, bf16[1,48,1280]{2,1,0:T(8,128)(2,1)S(1)}, u32[]{:S(2)}, u32[]{:S(2)}) collective-permute-start(bf16[1,48,1280]{2,1,0:T(8,128)(2,1)S(1)} %pass_body.1), channel_id=1, source_target_pairs={{0,4},{4,0},{8,12},{12,8},{1,5},{5,1},{9,13},{13,9},{2,6},{6,2},{1... | collective-permute-start | bytes 368648 | tf_op jit(solution)/shard_map/ppermute | solution.py:360
  33.9 9.0 %collective-permute-start.5 = (bf16[1,48,1280]{2,1,0:T(8,128)(2,1)S(1)}, bf16[1,48,1280]{2,1,0:T(8,128)(2,1)S(1)}, u32[]{:S(2)}, u32[]{:S(2)}) collective-permute-start(bf16[1,48,1280]{2,1,0:T(8,128)(2,1)S(1)} %add_body.1._), channel_id=1, source_target_pairs={{0,8},{4,12},{8,0},{12,4},{1,9},{5,13},{9,1},{13,5},{2,10},{6,14},... | collective-permute-start | bytes 368648 | tf_op jit(solution)/shard_map/ppermute | solution.py:360

commit v7 on v6

--- a/solution.py
+++ b/solution.py
@@ -123,13 +123,10 @@
     out[0, :, q_cols + head_dim :] = nn(x_ref[...], v_ref[...]).astype(BF16)
 
 
-def pass_body(message_ref, _, out_ref):
-    out_ref[...] = message_ref[...]
-
-
-def add_body(near_ref, got_ref, out_ref):
+def add_body(near_ref, got_ref, message_ref, out_ref, message_out):
     rows = near_ref.shape[1] // 2
     out_ref[...] = (near_ref[:, rows:].astype(F32) + got_ref[:, rows:].astype(F32)).astype(BF16)
+    message_out[...] = message_ref[...]
 
 
 def shrink_body(home_rows, cap, resident, parts, facts_ref, down_ref, *rest):
@@ -414,23 +411,20 @@
         bytes_=2 * resident * rank * q_cols * kv_here,
     )
     messages = list(grown[-homes:])
-    for d in range(2, homes):
+    for d in reversed(range(2, homes)):
         messages[d] = swap(messages[d], d)
     sums = ()
     if halved:
         near, far = grown[:2]
         got = swap(far, 1)
-        passed = call(
+        passed, messages[1] = call(
             add_body,
-            shape((halved, local_rows, width), BF16),
-            (near, got),
+            [shape((halved, local_rows, width), BF16), shape(messages[1].shape, BF16)],
+            (near, got, messages[1]),
             flops=halved * local_rows * width,
-            bytes_=6 * halved * local_rows * width,
+            bytes_=10 * halved * local_rows * width,
         )
         sums = (near, got, swap(passed, 2))
-        messages[1] = call(
-            pass_body, shape(messages[1].shape, BF16), (messages[1], passed), in_specs=[VMEM, ANY]
-        )
     messages[1] = swap(messages[1], 1)
 
     def attend(heads, pieces, done):

time: 44.9 us -> 44.9 us (level)
    pallas_call x9 -> x8, Pallas kernels: 12 us -> 12 us  [call(): pl.pallas_call(body, name=inner.__name__, out_shape=out_shape, in_specs=i...]
where the time goes in v7:
time: 44.9 us; the launch traced here: 44.6 us
  waiting for transfers between devices  14.7 us (33%)
  starting transfers between devices  13.6 us (30%)
  Pallas kernels  12 us (27%)
  local copies, waits for them, and re-layouts  4.29 us (10%)
    ppermute x5, waiting for transfers between devices, swap(): return lax.ppermute(value, 'pool', [(i, i ^ d) for i in range(homes)])  12.4 us
    pallas_call x8, Pallas kernels, call(): pl.pallas_call(body, name=inner.__name__, out_shape=out_shape, in_specs=i...  12 us
    ppermute x5, starting transfers between devices, swap(): return lax.ppermute(value, 'pool', [(i, i ^ d) for i in range(homes)])  6.55 us
    ppermute x1, starting transfers between devices, on_device(): lax.ppermute(s, ('pool', *FEATURE_AXES), perm)  5.11 us
    unnamed x18, local copies, waits for them, and re-layouts  4.29 us
    ppermute x3, waiting for transfers between devices, on_device(): lax.ppermute(share, FEATURE_AXES, [(i, i ^ d) for i in range(features)])  2.28 us
    ppermute x3, starting transfers between devices, on_device(): lax.ppermute(share, FEATURE_AXES, [(i, i ^ d) for i in range(features)])  1.92 us
  transfers between devices with their start and end apart: 9, of which 6 were waited for; matrix products, arithmetic and copies ran while one was open for 0% of the time, Pallas kernels for 15%

profile of v7, /device:TPU:0, one launch (start us, length us, event | category | flops | bytes accessed | tf_op | source)
XLA Modules:
  0.0 44.6 jit_solution(1399824746442444371)
XLA Ops:
  0.0 2.2 %select_body.1 = (bf16[96,2048]{1,0:T(8,128)(2,1)}, f32[8,64]{1,0:T(8,128)}) custom-call(s32[1,64]{1,0:T(1,128)} %bitcast.11, s32[1,64]{1,0:T(1,128)} %bitcast.12, s32[1,64]{1,0:T(1,128)} %bitcast.13, bf16[3,64,2048]{2,1,0:T(8,128)(2,1)} %bitcast.9), custom_call_target="tpu_custom_call" | custom-call | flops 25165824 | bytes 1179648 | tf_op jit(solution)/shard_map/select_body/pallas_call | solution.py:26
  2.2 5.1 %collective-permute-start = (bf16[96,2048]{1,0:T(8,128)(2,1)}, bf16[96,2048]{1,0:T(8,128)(2,1)S(1)}, u32[]{:S(2)}, u32[]{:S(2)}) collective-permute-start(bf16[96,2048]{1,0:T(8,128)(2,1)} %get-tuple-element.25), channel_id=1, source_target_pairs={{0,12},{1,4},{2,8},{3,0},{4,13},{5,1},{6,5},{7,9},{8,10},{9,6},{10... | collective-permute-start | bytes 1179656 | tf_op jit(solution)/shard_map/ppermute | solution.py:354
  7.3 1.1 %copy-done.2 = bf16[64,3,2048]{2,0,1:T(8,128)(2,1)S(1)} copy-done((bf16[64,3,2048]{2,0,1:T(8,128)(2,1)S(1)}, bf16[64,3,2048]{2,0,1:T(8,128)(2,1)}, u32[]{:S(2)}) %copy-start.2) | copy-done | bytes 786456
  8.5 1.2 %copy-done.3 = bf16[2048,256]{1,0:T(8,128)(2,1)S(1)} copy-done((bf16[2048,256]{1,0:T(8,128)(2,1)S(1)}, bf16[2048,256]{1,0:T(8,128)(2,1)}, u32[]{:S(2)}) %copy-start.3) | copy-done | bytes 1048600
  9.7 1.2 %copy-done.4 = bf16[2048,256]{1,0:T(8,128)(2,1)S(1)} copy-done((bf16[2048,256]{1,0:T(8,128)(2,1)S(1)}, bf16[2048,256]{1,0:T(8,128)(2,1)}, u32[]{:S(2)}) %copy-start.4) | copy-done | bytes 1048600
  10.9 0.7 %copy-done.8 = f32[8,64]{1,0:T(8,128)S(1)} copy-done((f32[8,64]{1,0:T(8,128)S(1)}, f32[8,64]{1,0:T(8,128)}, u32[]{:S(2)}) %copy-start.8) | copy-done | bytes 2072
  11.6 5.2 %project_body.1 = (bf16[2,192,1280]{2,1,0:T(8,128)(2,1)S(1)}, f32[8,64]{1,0:T(8,128)S(1)}) custom-call(bf16[192,2048]{1,0:T(8,128)(2,1)S(1)} %bitcast.10, bf16[2048,2048]{1,0:T(8,128)(2,1)} %q_ref.1, bf16[2048,256]{1,0:T(8,128)(2,1)S(1)} %copy-done.3, bf16[2048,256]{1,0:T(8,128)(2,1)S(1)} %copy-done.4, f32[8,64]{1,0:T(8,128)S(1)} %copy-done.8), custom_call_target="tpu_custom_call" | custom-call | flops 2013265920 | bytes 10485760 | tf_op jit(solution)/shard_map/project_body/pallas_call | solution.py:26
  16.8 0.0 copy-start
  16.8 0.0 collective-permute-done.rest_0_
  16.8 0.0 copy-done.5
  16.9 0.5 %shrink_body.1.rest_0_ = bf16[96,128]{1,0:T(8,128)(2,1)S(1)} custom-call(f32[8,64]{1,0:T(8,128)S(1)} %get-tuple-element.21.facts_ref, bf16[2,128,2048]{2,1,0:T(8,128)(2,1)S(1)} %copy-done.5, bf16[96,2048]{1,0:T(8,128)(2,1)S(1)} %collective-permute-done.rest_0_), custom_call_target="tpu_custom_call" | custom-call | flops 100663296 | bytes 1048576 | tf_op jit(solution)/shard_map/shrink_body/pallas_call | solution.py:26
  17.3 0.1 collective-permute-start.3
  17.4 1.0 %collective-permute-start.2 = (bf16[96,128]{1,0:T(8,128)(2,1)S(1)}, bf16[96,128]{1,0:T(8,128)(2,1)S(1)}, u32[]{:S(2)}, u32[]{:S(2)}) collective-permute-start(bf16[96,128]{1,0:T(8,128)(2,1)S(1)} %shrink_body.1.rest_0_), channel_id=1, source_target_pairs={{0,2},{1,3},{2,0},{3,1},{4,6},{5,7},{6,4},{7,5},{8,10},{9,11},{10,... | collective-permute-start | bytes 73736 | tf_op jit(solution)/shard_map/ppermute | solution.py:391
  18.4 0.9 %collective-permute-start.1 = (bf16[96,128]{1,0:T(8,128)(2,1)S(1)}, bf16[96,128]{1,0:T(8,128)(2,1)S(1)}, u32[]{:S(2)}, u32[]{:S(2)}) collective-permute-start(bf16[96,128]{1,0:T(8,128)(2,1)S(1)} %shrink_body.1.rest_0_), channel_id=1, source_target_pairs={{0,1},{1,0},{2,3},{3,2},{4,5},{5,4},{6,7},{7,6},{8,9},{9,8},{10,11... | collective-permute-start | bytes 73736 | tf_op jit(solution)/shard_map/ppermute | solution.py:391
  19.2 1.4 %collective-permute-done.3.rest_3_ = bf16[96,128]{1,0:T(8,128)(2,1)S(1)} collective-permute-done((bf16[96,128]{1,0:T(8,128)(2,1)S(1)}, bf16[96,128]{1,0:T(8,128)(2,1)S(1)}, u32[]{:S(2)}, u32[]{:S(2)}) %collective-permute-start.3) | collective-permute-done | bytes 24608 | tf_op jit(solution)/shard_map/ppermute | solution.py:391
  20.6 0.9 %collective-permute-done.2.rest_2_ = bf16[96,128]{1,0:T(8,128)(2,1)S(1)} collective-permute-done((bf16[96,128]{1,0:T(8,128)(2,1)S(1)}, bf16[96,128]{1,0:T(8,128)(2,1)S(1)}, u32[]{:S(2)}, u32[]{:S(2)}) %collective-permute-start.2) | collective-permute-done | bytes 24608 | tf_op jit(solution)/shard_map/ppermute | solution.py:391
  21.5 0.0 collective-permute-done.1.rest_1_
  21.5 1.1 %expand_body.1 = (bf16[1,96,1280]{2,1,0:T(8,128)(2,1)S(1)}, bf16[1,96,1280]{2,1,0:T(8,128)(2,1)S(1)}, bf16[1,48,1280]{2,1,0:T(8,128)(2,1)S(1)}, bf16[1,48,1280]{...) custom-call(f32[8,64]{1,0:T(8,128)S(1)} %get-tuple-element.21.facts_ref, ...), custom_call_target="tpu_custom_call" | custom-call | flops 50331648 | bytes 524288 | tf_op jit(solution)/shard_map/expand_body/pallas_call | solution.py:26
  22.6 0.6 %collective-permute-start.4 = (bf16[1,96,1280]{2,1,0:T(8,128)(2,1)S(1)}, bf16[1,96,1280]{2,1,0:T(8,128)(2,1)S(1)}, u32[]{:S(2)}, u32[]{:S(2)}) collective-permute-start(bf16[1,96,1280]{2,1,0:T(8,128)(2,1)S(1)} %get-tuple-element.28), channel_id=1, source_target_pairs={{0,4},{4,0},{8,12},{12,8},{1,5},{5,1},{9,13},{13,9},{2,6},{6,2},{1... | collective-permute-start | bytes 737288 | tf_op jit(solution)/shard_map/ppermute | solution.py:357
  23.2 2.4 %collective-permute-start.7 = (bf16[1,48,1280]{2,1,0:T(8,128)(2,1)S(1)}, bf16[1,48,1280]{2,1,0:T(8,128)(2,1)S(1)}, u32[]{:S(2)}, u32[]{:S(2)}) collective-permute-start(bf16[1,48,1280]{2,1,0:T(8,128)(2,1)S(1)} %get-tuple-element.33), channel_id=1, source_target_pairs={{0,8},{4,12},{8,0},{12,4},{1,9},{5,13},{9,1},{13,5},{2,10},{6,14},... | collective-permute-start | bytes 368648 | tf_op jit(solution)/shard_map/ppermute | solution.py:357
  25.7 1.4 %collective-permute-start.8 = (bf16[1,48,1280]{2,1,0:T(8,128)(2,1)S(1)}, bf16[1,48,1280]{2,1,0:T(8,128)(2,1)S(1)}, u32[]{:S(2)}, u32[]{:S(2)}) collective-permute-start(bf16[1,48,1280]{2,1,0:T(8,128)(2,1)S(1)} %get-tuple-element.34), channel_id=1, source_target_pairs={{0,12},{4,8},{8,4},{12,0},{1,13},{5,9},{9,5},{13,1},{2,14},{6,10},... | collective-permute-start | bytes 368648 | tf_op jit(solution)/shard_map/ppermute | solution.py:357
  27.1 6.6 %collective-permute-done.4.got_ref.rest_1_ = bf16[1,96,1280]{2,1,0:T(8,128)(2,1)S(1)} collective-permute-done((bf16[1,96,1280]{2,1,0:T(8,128)(2,1)S(1)}, bf16[1,96,1280]{2,1,0:T(8,128)(2,1)S(1)}, u32[]{:S(2)}, u32[]{:S(2)}) %collective-permute-start.4) | collective-permute-done | bytes 245792 | tf_op jit(solution)/shard_map/ppermute | solution.py:357
  33.7 0.1 collective-permute-start.6
  33.8 2.0 %collective-permute-start.5 = (bf16[1,48,1280]{2,1,0:T(8,128)(2,1)S(1)}, bf16[1,48,1280]{2,1,0:T(8,128)(2,1)S(1)}, u32[]{:S(2)}, u32[]{:S(2)}) collective-permute-start(bf16[1,48,1280]{2,1,0:T(8,128)(2,1)S(1)} %get-tuple-element.30), channel_id=1, source_target_pairs={{0,8},{4,12},{8,0},{12,4},{1,9},{5,13},{9,1},{13,5},{2,10},{6,14},... | collective-permute-start | bytes 368648 | tf_op jit(solution)/shard_map/ppermute | solution.py:357
  35.9 0.2 home_body.1
  36.0 0.0 collective-permute-done.7.rest_2_
  36.1 1.4 %collective-permute-done.8.rest_3_ = bf16[1,48,1280]{2,1,0:T(8,128)(2,1)S(1)} collective-permute-done((bf16[1,48,1280]{2,1,0:T(8,128)(2,1)S(1)}, bf16[1,48,1280]{2,1,0:T(8,128)(2,1)S(1)}, u32[]{:S(2)}, u32[]{:S(2)}) %collective-permute-start.8) | collective-permute-done | bytes 122912 | tf_op jit(solution)/shard_map/ppermute | solution.py:357
  37.4 3.2 %collective-permute-done.6.rest_1_ = bf16[1,48,1280]{2,1,0:T(8,128)(2,1)S(1)} collective-permute-done((bf16[1,48,1280]{2,1,0:T(8,128)(2,1)S(1)}, bf16[1,48,1280]{2,1,0:T(8,128)(2,1)S(1)}, u32[]{:S(2)}, u32[]{:S(2)}) %collective-permute-start.6) | collective-permute-done | bytes 122912 | tf_op jit(solution)/shard_map/ppermute | solution.py:357
  40.6 0.0 copy-done.1
  40.6 1.1 %attend_body.2.rest_3_ = bf16[48,1024]{1,0:T(8,128)(2,1)S(1)} custom-call(f32[48,128]{1,0:T(8,128)S(1)} %get-tuple-element.22.cos_ref, f32[48,128]{1,0:T(8,128)S(1)} %get-tuple-element.23.sin_ref, f32[16,256]{1,0:T(8,128)S(1)} %get-tuple-element.24.len_ref, bf16[16,2,256,128]{3,2,1,0:T(8,128)(2,1)S(1)} %copy-done, bf16[16,2,256,128]{3,2,1,0:T(8,128)(2,1)S(1)} %copy-done.1, ...), custom_call_target="tpu_custom_call" | custom-call | flops 50331648 | bytes 2097152 | tf_op jit(solution)/shard_map/attend_body/pallas_call | solution.py:26
  41.7 1.2 %collective-permute-done.5.rest_2_ = bf16[1,48,1280]{2,1,0:T(8,128)(2,1)S(1)} collective-permute-done((bf16[1,48,1280]{2,1,0:T(8,128)(2,1)S(1)}, bf16[1,48,1280]{2,1,0:T(8,128)(2,1)S(1)}, u32[]{:S(2)}, u32[]{:S(2)}) %collective-permute-start.5) | collective-permute-done | bytes 122912 | tf_op jit(solution)/shard_map/ppermute | solution.py:357
  42.9 1.8 %attend_body.3 = bf16[48,2048]{1,0:T(8,128)(2,1)} custom-call(f32[48,128]{1,0:T(8,128)S(1)} %get-tuple-element.22.cos_ref, f32[48,128]{1,0:T(8,128)S(1)} %get-tuple-element.23.sin_ref, f32[16,256]{1,0:T(8,128)S(1)} %get-tuple-element.24.len_ref, bf16[16,2,256,128]{3,2,1,0:T(8,128)(2,1)S(1)} %copy-done, bf16[16,2,256,128]{3,2,1,0:T(8,128)(2,1)S(1)} %copy-done.1, ...), custom_call_target="tpu_custom_call" | custom-call | flops 50331648 | bytes 2097152 | tf_op jit(solution)/shard_map/attend_body/pallas_call | solution.py:26
  (12 shorter events, 0.1 us)
Async XLA Ops:
  2.2 14.6 %collective-permute-start = (bf16[96,2048]{1,0:T(8,128)(2,1)}, bf16[96,2048]{1,0:T(8,128)(2,1)S(1)}, u32[]{:S(2)}, u32[]{:S(2)}) collective-permute-start(bf16[96,2048]{1,0:T(8,128)(2,1)} %get-tuple-element.25), channel_id=1, source_target_pairs={{0,12},{1,4},{2,8},{3,0},{4,13},{5,1},{6,5},{7,9},{8,10},{9,6},{10... | collective-permute-start | bytes 1179656 | tf_op jit(solution)/shard_map/ppermute | solution.py:354
  7.3 1.1 %copy-start.2 = (bf16[64,3,2048]{2,0,1:T(8,128)(2,1)S(1)}, bf16[64,3,2048]{2,0,1:T(8,128)(2,1)}, u32[]{:S(2)}) copy-start(bf16[64,3,2048]{2,0,1:T(8,128)(2,1)} %param.12) | copy-start | bytes 2359300
  8.5 1.2 %copy-start.3 = (bf16[2048,256]{1,0:T(8,128)(2,1)S(1)}, bf16[2048,256]{1,0:T(8,128)(2,1)}, u32[]{:S(2)}) copy-start(bf16[2048,256]{1,0:T(8,128)(2,1)} %k_ref.1) | copy-start | bytes 3145732
  9.7 1.2 %copy-start.4 = (bf16[2048,256]{1,0:T(8,128)(2,1)S(1)}, bf16[2048,256]{1,0:T(8,128)(2,1)}, u32[]{:S(2)}) copy-start(bf16[2048,256]{1,0:T(8,128)(2,1)} %v_ref.1) | copy-start | bytes 3145732
  10.9 0.7 %copy-start.8 = (f32[8,64]{1,0:T(8,128)S(1)}, f32[8,64]{1,0:T(8,128)}, u32[]{:S(2)}) copy-start(f32[8,64]{1,0:T(8,128)} %get-tuple-element.20.facts_ref) | copy-start | bytes 6148
  11.6 5.2 %copy-start.5 = (bf16[2,128,2048]{2,1,0:T(8,128)(2,1)S(1)}, bf16[2,128,2048]{2,1,0:T(8,128)(2,1)}, u32[]{:S(2)}) copy-start(bf16[2,128,2048]{2,1,0:T(8,128)(2,1)} %down_ref.1) | copy-start | bytes 3145732
  11.6 9.9 %copy-start.6 = (bf16[2,64,2048]{2,1,0:T(8,128)(2,1)S(1)}, bf16[2,64,2048]{2,1,0:T(8,128)(2,1)}, u32[]{:S(2)}) copy-start(bf16[2,64,2048]{2,1,0:T(8,128)(2,1)} %upq_ref.1) | copy-start | bytes 1572868
  11.6 9.9 %copy-start.7 = (bf16[2,64,256]{2,1,0:T(8,128)(2,1)S(1)}, bf16[2,64,256]{2,1,0:T(8,128)(2,1)}, u32[]{:S(2)}) copy-start(bf16[2,64,256]{2,1,0:T(8,128)(2,1)} %upv_ref.1) | copy-start | bytes 196612
  11.6 29.0 %copy-start.1 = (bf16[16,2,256,128]{3,2,1,0:T(8,128)(2,1)S(1)}, bf16[16,2,256,128]{3,2,1,0:T(8,128)(2,1)}, u32[]{:S(2)}) copy-start(bf16[16,2,256,128]{3,2,1,0:T(8,128)(2,1)} %vc_ref.3) | copy-start | bytes 6291460
  16.8 23.8 %copy-start = (bf16[16,2,256,128]{3,2,1,0:T(8,128)(2,1)S(1)}, bf16[16,2,256,128]{3,2,1,0:T(8,128)(2,1)}, u32[]{:S(2)}) copy-start(bf16[16,2,256,128]{3,2,1,0:T(8,128)(2,1)} %kc_ref.3) | copy-start | bytes 6291460
  17.3 3.3 %collective-permute-start.3 = (bf16[96,128]{1,0:T(8,128)(2,1)S(1)}, bf16[96,128]{1,0:T(8,128)(2,1)S(1)}, u32[]{:S(2)}, u32[]{:S(2)}) collective-permute-start(bf16[96,128]{1,0:T(8,128)(2,1)S(1)} %shrink_body.1.rest_0_), channel_id=1, source_target_pairs={{0,3},{1,2},{2,1},{3,0},{4,7},{5,6},{6,5},{7,4},{8,11},{9,10},{10,... | collective-permute-start | bytes 73736 | tf_op jit(solution)/shard_map/ppermute | solution.py:391
  17.4 4.1 %collective-permute-start.2 = (bf16[96,128]{1,0:T(8,128)(2,1)S(1)}, bf16[96,128]{1,0:T(8,128)(2,1)S(1)}, u32[]{:S(2)}, u32[]{:S(2)}) collective-permute-start(bf16[96,128]{1,0:T(8,128)(2,1)S(1)} %shrink_body.1.rest_0_), channel_id=1, source_target_pairs={{0,2},{1,3},{2,0},{3,1},{4,6},{5,7},{6,4},{7,5},{8,10},{9,11},{10,... | collective-permute-start | bytes 73736 | tf_op jit(solution)/shard_map/ppermute | solution.py:391
  18.4 3.2 %collective-permute-start.1 = (bf16[96,128]{1,0:T(8,128)(2,1)S(1)}, bf16[96,128]{1,0:T(8,128)(2,1)S(1)}, u32[]{:S(2)}, u32[]{:S(2)}) collective-permute-start(bf16[96,128]{1,0:T(8,128)(2,1)S(1)} %shrink_body.1.rest_0_), channel_id=1, source_target_pairs={{0,1},{1,0},{2,3},{3,2},{4,5},{5,4},{6,7},{7,6},{8,9},{9,8},{10,11... | collective-permute-start | bytes 73736 | tf_op jit(solution)/shard_map/ppermute | solution.py:391
  22.6 11.1 %collective-permute-start.4 = (bf16[1,96,1280]{2,1,0:T(8,128)(2,1)S(1)}, bf16[1,96,1280]{2,1,0:T(8,128)(2,1)S(1)}, u32[]{:S(2)}, u32[]{:S(2)}) collective-permute-start(bf16[1,96,1280]{2,1,0:T(8,128)(2,1)S(1)} %get-tuple-element.28), channel_id=1, source_target_pairs={{0,4},{4,0},{8,12},{12,8},{1,5},{5,1},{9,13},{13,9},{2,6},{6,2},{1... | collective-permute-start | bytes 737288 | tf_op jit(solution)/shard_map/ppermute | solution.py:357
  23.2 12.8 %collective-permute-start.7 = (bf16[1,48,1280]{2,1,0:T(8,128)(2,1)S(1)}, bf16[1,48,1280]{2,1,0:T(8,128)(2,1)S(1)}, u32[]{:S(2)}, u32[]{:S(2)}) collective-permute-start(bf16[1,48,1280]{2,1,0:T(8,128)(2,1)S(1)} %get-tuple-element.33), channel_id=1, source_target_pairs={{0,8},{4,12},{8,0},{12,4},{1,9},{5,13},{9,1},{13,5},{2,10},{6,14},... | collective-permute-start | bytes 368648 | tf_op jit(solution)/shard_map/ppermute | solution.py:357
  25.7 11.7 %collective-permute-start.8 = (bf16[1,48,1280]{2,1,0:T(8,128)(2,1)S(1)}, bf16[1,48,1280]{2,1,0:T(8,128)(2,1)S(1)}, u32[]{:S(2)}, u32[]{:S(2)}) collective-permute-start(bf16[1,48,1280]{2,1,0:T(8,128)(2,1)S(1)} %get-tuple-element.34), channel_id=1, source_target_pairs={{0,12},{4,8},{8,4},{12,0},{1,13},{5,9},{9,5},{13,1},{2,14},{6,10},... | collective-permute-start | bytes 368648 | tf_op jit(solution)/shard_map/ppermute | solution.py:357
  33.7 6.9 %collective-permute-start.6 = (bf16[1,48,1280]{2,1,0:T(8,128)(2,1)S(1)}, bf16[1,48,1280]{2,1,0:T(8,128)(2,1)S(1)}, u32[]{:S(2)}, u32[]{:S(2)}) collective-permute-start(bf16[1,48,1280]{2,1,0:T(8,128)(2,1)S(1)} %get-tuple-element.32), channel_id=1, source_target_pairs={{0,4},{4,0},{8,12},{12,8},{1,5},{5,1},{9,13},{13,9},{2,6},{6,2},{1... | collective-permute-start | bytes 368648 | tf_op jit(solution)/shard_map/ppermute | solution.py:357
  33.8 9.1 %collective-permute-start.5 = (bf16[1,48,1280]{2,1,0:T(8,128)(2,1)S(1)}, bf16[1,48,1280]{2,1,0:T(8,128)(2,1)S(1)}, u32[]{:S(2)}, u32[]{:S(2)}) collective-permute-start(bf16[1,48,1280]{2,1,0:T(8,128)(2,1)S(1)} %get-tuple-element.30), channel_id=1, source_target_pairs={{0,8},{4,12},{8,0},{12,4},{1,9},{5,13},{9,1},{13,5},{2,10},{6,14},... | collective-permute-start | bytes 368648 | tf_op jit(solution)/shard_map/ppermute | solution.py:357
